TPU v7x, 512 devices: a whole 4x4x16 slice. The times are simulated.
512 devices in a mesh: tm: 32 (over z, core), obs: 16 (over y, x).
Axes of the slice: x: 4, y: 4, z: 16, core: 2. Of those that a mesh axis runs over, the one named last changes fastest.
Arguments:
- footprints: bfloat16 [512, 4, 128, 128], P(('tm', 'obs')), may hold values from -0.5 to 0.5
- block_times: int32 [512, 4], P(('tm', 'obs')), may hold values from 0 to 7
- block_cells: int32 [512, 4], P(('tm', 'obs')), may hold values from 0 to 511
- live_counts: int32 [512], P(('tm', 'obs')), may hold values from 1 to 4
- cell_lat: int32 [65536], replicated, may hold values from 0 to 179
- cell_lon: int32 [65536], replicated, may hold values from 0 to 359
Outputs:
- cross_cov: float32 [65536, 4096], P(('tm', 'obs'))
- footprint_cov: float32 [512, 4, 128, 128], P(('tm', 'obs'))
All inputs are finite; a program needn't handle non-finite values.
Results may differ from a plain program's by a relative error of at most 0.004.
Values may be sent and summed in bfloat16 or wider, within the bound.
No kernel may reach another device: no remote copies, remote signals or barrier semaphores. Data moves between devices by JAX's collectives and lax.ppermute only.
A program may use at most 64 MiB of HBM per device.

v0:
```python
import math

import jax
import jax.numpy as jnp
from jax import lax
from jax.sharding import PartitionSpec as P

TSTEP = 8


corr_length = 0.6


def from_behind(array, axis, by):
    devices = lax.axis_size(axis)
    pairs = [(i, i + by) for i in range(devices) if 0 <= i + by < devices]
    return lax.ppermute(array, axis, pairs)


def unit_vectors(cell_lat, cell_lon):
    radians = math.pi / 180.0
    latitude = (cell_lat.astype(jnp.float32) - 89.5) * radians
    longitude = (cell_lon.astype(jnp.float32) + 0.5) * radians
    return jnp.stack(
        [
            jnp.cos(latitude) * jnp.cos(longitude),
            jnp.cos(latitude) * jnp.sin(longitude),
            jnp.sin(latitude),
        ]
    )


def kernel_weights(own_vec, own_time, far_vec, far_time, steps):
    squared = jnp.zeros((), jnp.float32)
    for component in range(3):
        offset = (
            own_vec[:, :, None, component, :, None] - far_vec[None, None, :, component, None, :]
        )
        squared = squared + offset * offset
    spatial = jnp.exp(-jnp.sqrt(squared) / corr_length)
    lagged = jnp.abs(own_time[:, :, None] - far_time[None, None, :])
    temporal = jnp.exp(-lagged / steps)
    weights = (temporal[:, :, :, None, None] * spatial).astype(jnp.bfloat16)
    own_count, own_slots, far_slots, edge, _ = weights.shape
    return weights.transpose(0, 1, 3, 2, 4).reshape(own_count, own_slots * edge, far_slots * edge)


def on_device(footprints, block_times, block_cells, live_counts, cell_lat, cell_lon):
    own_blocks, slots, edge, _ = footprints.shape
    group = lax.axis_size("obs")
    per_time = own_blocks * group
    steps = float(TSTEP)
    time_index = lax.axis_index("tm")
    slot_live = jnp.arange(slots)[None, :] < live_counts[:, None]
    prints = jnp.where(slot_live[:, :, None, None], footprints, jnp.zeros((), jnp.bfloat16))
    vectors = unit_vectors(cell_lat, cell_lon).reshape(3, -1, edge).transpose(1, 0, 2)
    own_vec = vectors[block_cells]
    own_time = (time_index * TSTEP + block_times).astype(jnp.float32)
    own_cat = prints.transpose(0, 2, 1, 3).reshape(own_blocks, edge, slots * edge)

    def far_tiles(far_prints, far_cells, far_times, time_base):

        def one_block(item_prints, item_cells, item_times):
            weights = kernel_weights(
                own_vec,
                own_time,
                vectors[item_cells],
                (time_base + item_times).astype(jnp.float32),
                steps,
            )
            gain = jnp.einsum("sac,scd->sad", own_cat, weights, preferred_element_type=jnp.float32)
            item_cat = item_prints.transpose(1, 0, 2).reshape(edge, slots * edge)
            return jnp.einsum(
                "sad,ed->sae",
                gain.astype(jnp.bfloat16),
                item_cat,
                preferred_element_type=jnp.float32,
            )

        count = far_prints.shape[0]
        bundle = 4
        turns = count // bundle

        def one_bundle(item):
            return jax.vmap(one_block)(item[0], item[1], item[2])

        grouped = (
            far_prints.reshape((turns, bundle) + far_prints.shape[1:]),
            far_cells.reshape(turns, bundle, slots),
            far_times.reshape(turns, bundle, slots),
        )
        result = lax.map(one_bundle, grouped)
        return result.reshape((count,) + result.shape[2:])

    def self_gain(cat_row, vec_row, time_row):
        weights = kernel_weights(vec_row[None], time_row[None], vec_row, time_row, steps)
        gain = jnp.einsum(
            "sac,scd->sad", cat_row[None], weights, preferred_element_type=jnp.float32
        )[0]
        return gain.reshape(edge, slots, edge).transpose(1, 0, 2)

    footprint_cov = jax.vmap(self_gain)(own_cat, own_vec, own_time)
    current = (
        lax.all_gather(prints, "obs", axis=0, tiled=True),
        lax.all_gather(block_cells, "obs", axis=0, tiled=True),
        lax.all_gather(block_times, "obs", axis=0, tiled=True),
    )
    prior = from_behind((current[0], current[1], current[2]), "tm", 1)
    earlier = far_tiles(prior[0], prior[1], prior[2], (time_index - 1) * TSTEP)
    later = far_tiles(current[0], current[1], current[2], time_index * TSTEP)
    tiles = jnp.concatenate([earlier, later], axis=0)
    cross_cov = tiles.transpose(1, 2, 0, 3).reshape(own_blocks * edge, 2 * per_time * edge)
    return (cross_cov, footprint_cov)


def solution(mesh):
    placed = (
        P(("tm", "obs"), None, None, None),
        P(("tm", "obs"), None),
        P(("tm", "obs"), None),
        P(("tm", "obs")),
        P(),
        P(),
    )
    return jax.shard_map(
        on_device,
        mesh=mesh,
        in_specs=placed,
        out_specs=(P(("tm", "obs"), None), P(("tm", "obs"), None, None, None)),
        check_vma=False,
    )
```

profile of v0, /device:TPU:1, one launch (start us, length us, event | category | flops | bytes accessed | tf_op | source)
XLA Modules:
  0.0 217.0 jit_solution(9960501482163797261)
XLA Ops:
  9.8 17.3 %all-gather = s32[16,1,4]{2,1,0:T(1,128)S(1)} all-gather(s32[1,1,4]{2,1,0:T(1,128)} %bitcast.253), channel_id=1, replica_groups=mesh['tm'=32,'obs'=16] {'obs'}, dimensions={0}, use_global_device_ids=true | all-gather | bytes 272 | tf_op jit(solution)/shard_map/all_gather | solution.py:106
  27.2 8.5 %collective-permute-start = (s32[16,4]{0,1:T(4,128)S(1)}, s32[16,4]{0,1:T(4,128)S(1)}, u32[]{:S(2)}, u32[]{:S(2)}) collective-permute-start(s32[16,4]{0,1:T(4,128)S(1)} %bitcast.247), channel_id=1, source_target_pairs={{0,16},{16,32},{32,48},{48,64},{64,80},{80,96},{96,112},{112,128},... | collective-permute-start | bytes 776 | tf_op jit(solution)/shard_map/ppermute | solution.py:17
  35.7 15.5 %all-gather.1 = s32[16,1,4]{2,1,0:T(1,128)S(1)} all-gather(s32[1,1,4]{2,1,0:T(1,128)} %bitcast.252), channel_id=1, replica_groups=mesh['tm'=32,'obs'=16] {'obs'}, dimensions={0}, use_global_device_ids=true | all-gather | bytes 272 | tf_op jit(solution)/shard_map/all_gather | solution.py:105
  51.3 5.7 %collective-permute-start.1 = (s32[16,4]{0,1:T(4,128)S(1)}, s32[16,4]{0,1:T(4,128)S(1)}, u32[]{:S(2)}, u32[]{:S(2)}) collective-permute-start(s32[16,4]{0,1:T(4,128)S(1)} %bitcast.248), channel_id=1, source_target_pairs={{0,16},{16,32},{32,48},{48,64},{64,80},{80,96},{96,112},{112,128},... | collective-permute-start | bytes 776 | tf_op jit(solution)/shard_map/ppermute | solution.py:17
  57.8 2.9 %cosine_multiply_fusion = (f32[65536]{0:T(1024)S(1)}, f32[65536]{0:T(1024)S(1)}, f32[65536]{0:T(1024)S(1)}) fusion(s32[65536]{0:T(1024)} %param.15, s32[65536]{0:T(1024)} %param.14), kind=kLoop, calls=%fused_computation.44 | loop fusion | flops 524288 | bytes 1310720 | tf_op jit(solution)/shard_map/mul | solution.py:26
  64.2 2.1 multiply_convert_fusion.2
  67.7 8.6 %all-gather.4.cloned.1.call-done = bf16[16,4,128,128]{3,2,1,0:T(8,128)(2,1)} async-done(((bf16[1,4,128,128]{3,2,1,0:T(8,128)(2,1)}), bf16[16,4,128,128]{3,2,1,0:T(8,128)(2,1)}) %all-gather.4.cloned.1.call-update) | async-done | bytes 2097168 | tf_op jit(solution)/shard_map/all_gather | solution.py:104
  76.3 4.7 %collective-permute-start.2 = (bf16[16,4,128,128]{3,2,1,0:T(8,128)(2,1)}, bf16[16,4,128,128]{3,2,1,0:T(8,128)(2,1)}, u32[]{:S(2)}, u32[]{:S(2)}) collective-permute-start(bf16[16,4,128,128]{3,2,1,0:T(8,128)(2,1)} %all-gather.4.cloned.1.call-done), channel_id=1, source_target_pairs={{0,16},{16,32},{32,48},{48,64},{64,80},{80,96},{96,112},{112,128},... | collective-permute-start | bytes 6291464 | tf_op jit(solution)/shard_map/ppermute | solution.py:17
  82.2 59.4 %while.21 = (s32[]{:T(128)}, f32[4,4,1,128,128]{4,3,1,2,0:T(8,128)}, f32[1,4]{1,0:T(1,128)S(1)}, s32[]{:T(128)}, s32[4,4,4]{2,1,0:T(4,128)S(1)}, /*index=5*/f32[...) while((s32[]{:T(128)}, ...), condition=%wide.region_3.4_spmd, body=%wide.region_2.3_spmd.sunk | while | flops 348390752 | bytes 12598989 | solution.py:92
  82.3 1.8 gather_fusion.1
  84.2 6.6 %fusion.49 = bf16[4,1,4,128,4,128]{5,4,3,2,0,1:T(4,128)(2,1)} fusion(f32[4,4,128]{2,1,0:T(4,128)S(1)} %bitcast.236, f32[4,128]{1,0:T(4,128)S(1)} %get-tuple-element.390, f32[4,4,128]{2,1,0:T(4,128)S(1)} %bitcast.235, f32[4,128]{1,0:T(4,128)S(1)} %get-tuple-element.392, f32[4,4,128]{2,1,0:T(4,128)S(1)} %bitcast.234, ...), kind=kLoop, calls=%fused_computation.21.clone.1 | loop fusion | flops 12582912 | bytes 2128128 | tf_op jit(solution)/shard_map/while/body/eval_jaxpr/vmap()/transpose | solution.py:45
  90.8 2.7 %reshape.553 = bf16[4,512,512]{2,1,0:T(8,128)(2,1)S(1)} reshape(bf16[4,1,4,128,4,128]{5,4,3,2,0,1:T(4,128)(2,1)} %fusion.49) | data formatting | bytes 4194304 | tf_op jit(solution)/shard_map/reshape.43
  97.1 1.8 gather_fusion.1
  99.0 6.6 %fusion.49 = bf16[4,1,4,128,4,128]{5,4,3,2,0,1:T(4,128)(2,1)} fusion(f32[4,4,128]{2,1,0:T(4,128)S(1)} %bitcast.236, f32[4,128]{1,0:T(4,128)S(1)} %get-tuple-element.390, f32[4,4,128]{2,1,0:T(4,128)S(1)} %bitcast.235, f32[4,128]{1,0:T(4,128)S(1)} %get-tuple-element.392, f32[4,4,128]{2,1,0:T(4,128)S(1)} %bitcast.234, ...), kind=kLoop, calls=%fused_computation.21.clone.1 | loop fusion | flops 12582912 | bytes 2128128 | tf_op jit(solution)/shard_map/while/body/eval_jaxpr/vmap()/transpose | solution.py:45
  105.6 2.7 %reshape.553 = bf16[4,512,512]{2,1,0:T(8,128)(2,1)S(1)} reshape(bf16[4,1,4,128,4,128]{5,4,3,2,0,1:T(4,128)(2,1)} %fusion.49) | data formatting | bytes 4194304 | tf_op jit(solution)/shard_map/reshape.43
  112.0 1.8 gather_fusion.1
  113.9 6.6 %fusion.49 = bf16[4,1,4,128,4,128]{5,4,3,2,0,1:T(4,128)(2,1)} fusion(f32[4,4,128]{2,1,0:T(4,128)S(1)} %bitcast.236, f32[4,128]{1,0:T(4,128)S(1)} %get-tuple-element.390, f32[4,4,128]{2,1,0:T(4,128)S(1)} %bitcast.235, f32[4,128]{1,0:T(4,128)S(1)} %get-tuple-element.392, f32[4,4,128]{2,1,0:T(4,128)S(1)} %bitcast.234, ...), kind=kLoop, calls=%fused_computation.21.clone.1 | loop fusion | flops 12582912 | bytes 2128128 | tf_op jit(solution)/shard_map/while/body/eval_jaxpr/vmap()/transpose | solution.py:45
  120.5 2.7 %reshape.553 = bf16[4,512,512]{2,1,0:T(8,128)(2,1)S(1)} reshape(bf16[4,1,4,128,4,128]{5,4,3,2,0,1:T(4,128)(2,1)} %fusion.49) | data formatting | bytes 4194304 | tf_op jit(solution)/shard_map/reshape.43
  128.8 6.6 %fusion.49 = bf16[4,1,4,128,4,128]{5,4,3,2,0,1:T(4,128)(2,1)} fusion(f32[4,4,128]{2,1,0:T(4,128)S(1)} %bitcast.236, f32[4,128]{1,0:T(4,128)S(1)} %get-tuple-element.390, f32[4,4,128]{2,1,0:T(4,128)S(1)} %bitcast.235, f32[4,128]{1,0:T(4,128)S(1)} %get-tuple-element.392, f32[4,4,128]{2,1,0:T(4,128)S(1)} %bitcast.234, ...), kind=kLoop, calls=%fused_computation.21.clone.1 | loop fusion | flops 12582912 | bytes 2128128 | tf_op jit(solution)/shard_map/while/body/eval_jaxpr/vmap()/transpose | solution.py:45
  135.4 2.7 %reshape.553 = bf16[4,512,512]{2,1,0:T(8,128)(2,1)S(1)} reshape(bf16[4,1,4,128,4,128]{5,4,3,2,0,1:T(4,128)(2,1)} %fusion.49) | data formatting | bytes 4194304 | tf_op jit(solution)/shard_map/reshape.43
  141.6 2.8 %copy.78 = f32[16,1,128,128]{3,0,2,1:T(8,128)} copy(f32[16,1,128,128]{3,2,0,1:T(8,128)} %bitcast.220) | data formatting | bytes 2097152 | tf_op jit(solution)/shard_map/reshape | solution.py:93
  145.5 59.4 %while.20 = (s32[]{:T(128)}, f32[4,4,1,128,128]{4,3,1,2,0:T(8,128)}, f32[1,4]{1,0:T(1,128)S(1)}, s32[]{:T(128)}, s32[4,4,4]{2,1,0:T(4,128)S(1)}, /*index=5*/f32[...) while((s32[]{:T(128)}, ...), condition=%wide.region_1.2_spmd, body=%wide.region_0.1_spmd.sunk | while | flops 348390752 | bytes 12598989 | solution.py:92
  147.5 6.6 %fusion.43 = bf16[4,1,4,128,4,128]{5,4,3,2,0,1:T(4,128)(2,1)} fusion(f32[4,4,128]{2,1,0:T(4,128)S(1)} %bitcast.239, f32[4,128]{1,0:T(4,128)S(1)} %get-tuple-element.374, f32[4,4,128]{2,1,0:T(4,128)S(1)} %bitcast.238, f32[4,128]{1,0:T(4,128)S(1)} %get-tuple-element.376, f32[4,4,128]{2,1,0:T(4,128)S(1)} %bitcast.237, ...), kind=kLoop, calls=%fused_computation.4.clone.1 | loop fusion | flops 12582912 | bytes 2128128 | tf_op jit(solution)/shard_map/while/body/eval_jaxpr/vmap()/transpose | solution.py:45
  154.1 2.7 %reshape.548 = bf16[4,512,512]{2,1,0:T(8,128)(2,1)S(1)} reshape(bf16[4,1,4,128,4,128]{5,4,3,2,0,1:T(4,128)(2,1)} %fusion.43) | data formatting | bytes 4194304 | tf_op jit(solution)/shard_map/reshape.12
  162.4 6.6 %fusion.43 = bf16[4,1,4,128,4,128]{5,4,3,2,0,1:T(4,128)(2,1)} fusion(f32[4,4,128]{2,1,0:T(4,128)S(1)} %bitcast.239, f32[4,128]{1,0:T(4,128)S(1)} %get-tuple-element.374, f32[4,4,128]{2,1,0:T(4,128)S(1)} %bitcast.238, f32[4,128]{1,0:T(4,128)S(1)} %get-tuple-element.376, f32[4,4,128]{2,1,0:T(4,128)S(1)} %bitcast.237, ...), kind=kLoop, calls=%fused_computation.4.clone.1 | loop fusion | flops 12582912 | bytes 2128128 | tf_op jit(solution)/shard_map/while/body/eval_jaxpr/vmap()/transpose | solution.py:45
  169.0 2.7 %reshape.548 = bf16[4,512,512]{2,1,0:T(8,128)(2,1)S(1)} reshape(bf16[4,1,4,128,4,128]{5,4,3,2,0,1:T(4,128)(2,1)} %fusion.43) | data formatting | bytes 4194304 | tf_op jit(solution)/shard_map/reshape.12
  177.3 6.6 %fusion.43 = bf16[4,1,4,128,4,128]{5,4,3,2,0,1:T(4,128)(2,1)} fusion(f32[4,4,128]{2,1,0:T(4,128)S(1)} %bitcast.239, f32[4,128]{1,0:T(4,128)S(1)} %get-tuple-element.374, f32[4,4,128]{2,1,0:T(4,128)S(1)} %bitcast.238, f32[4,128]{1,0:T(4,128)S(1)} %get-tuple-element.376, f32[4,4,128]{2,1,0:T(4,128)S(1)} %bitcast.237, ...), kind=kLoop, calls=%fused_computation.4.clone.1 | loop fusion | flops 12582912 | bytes 2128128 | tf_op jit(solution)/shard_map/while/body/eval_jaxpr/vmap()/transpose | solution.py:45
  183.8 2.7 %reshape.548 = bf16[4,512,512]{2,1,0:T(8,128)(2,1)S(1)} reshape(bf16[4,1,4,128,4,128]{5,4,3,2,0,1:T(4,128)(2,1)} %fusion.43) | data formatting | bytes 4194304 | tf_op jit(solution)/shard_map/reshape.12
  192.1 6.6 %fusion.43 = bf16[4,1,4,128,4,128]{5,4,3,2,0,1:T(4,128)(2,1)} fusion(f32[4,4,128]{2,1,0:T(4,128)S(1)} %bitcast.239, f32[4,128]{1,0:T(4,128)S(1)} %get-tuple-element.374, f32[4,4,128]{2,1,0:T(4,128)S(1)} %bitcast.238, f32[4,128]{1,0:T(4,128)S(1)} %get-tuple-element.376, f32[4,4,128]{2,1,0:T(4,128)S(1)} %bitcast.237, ...), kind=kLoop, calls=%fused_computation.4.clone.1 | loop fusion | flops 12582912 | bytes 2128128 | tf_op jit(solution)/shard_map/while/body/eval_jaxpr/vmap()/transpose | solution.py:45
  198.7 2.7 %reshape.548 = bf16[4,512,512]{2,1,0:T(8,128)(2,1)S(1)} reshape(bf16[4,1,4,128,4,128]{5,4,3,2,0,1:T(4,128)(2,1)} %fusion.43) | data formatting | bytes 4194304 | tf_op jit(solution)/shard_map/reshape.12
  204.9 1.9 copy.77
  207.2 3.0 %copy.101 = f32[16,8,32,128]{3,1,2,0:T(8,128)} copy(f32[16,8,32,128]{3,2,1,0:T(8,128)S(1)} %bitcast.218) | data formatting | bytes 4194304
  (126 shorter events, 48.6 us)
Async XLA Ops:
  7.2 57.0 %copy-start.1 = (s32[1,4]{1,0:T(1,128)S(1)}, s32[1,4]{1,0:T(1,128)}, u32[]{:S(2)}) copy-start(s32[1,4]{1,0:T(1,128)} %param.11) | copy-start | bytes 52
  7.2 69.2 %all-gather.4.cloned.1.call-start = ((), (), s32[]{:S(2)}) async-start(), calls=%async_computation | async-start | bytes 2228224 | tf_op jit(solution)/shard_map/all_gather | solution.py:104
  27.2 40.4 %collective-permute-start = (s32[16,4]{0,1:T(4,128)S(1)}, s32[16,4]{0,1:T(4,128)S(1)}, u32[]{:S(2)}, u32[]{:S(2)}) collective-permute-start(s32[16,4]{0,1:T(4,128)S(1)} %bitcast.247), channel_id=1, source_target_pairs={{0,16},{16,32},{32,48},{48,64},{64,80},{80,96},{96,112},{112,128},... | collective-permute-start | bytes 776 | tf_op jit(solution)/shard_map/ppermute | solution.py:17
  51.3 16.3 %collective-permute-start.1 = (s32[16,4]{0,1:T(4,128)S(1)}, s32[16,4]{0,1:T(4,128)S(1)}, u32[]{:S(2)}, u32[]{:S(2)}) collective-permute-start(s32[16,4]{0,1:T(4,128)S(1)} %bitcast.248), channel_id=1, source_target_pairs={{0,16},{16,32},{32,48},{48,64},{64,80},{80,96},{96,112},{112,128},... | collective-permute-start | bytes 776 | tf_op jit(solution)/shard_map/ppermute | solution.py:17
  76.3 68.1 %collective-permute-start.2 = (bf16[16,4,128,128]{3,2,1,0:T(8,128)(2,1)}, bf16[16,4,128,128]{3,2,1,0:T(8,128)(2,1)}, u32[]{:S(2)}, u32[]{:S(2)}) collective-permute-start(bf16[16,4,128,128]{3,2,1,0:T(8,128)(2,1)} %all-gather.4.cloned.1.call-done), channel_id=1, source_target_pairs={{0,16},{16,32},{32,48},{48,64},{64,80},{80,96},{96,112},{112,128},... | collective-permute-start | bytes 6291464 | tf_op jit(solution)/shard_map/ppermute | solution.py:17
  204.9 1.9 copy-start
Sparse Core Ops, SparseCore 0:
  11.6 64.6 all-gather.3
where the time goes:
time: 218 us; the launch traced here: 217 us
  local copies, waits for them, and re-layouts  64.9 us (30%)
  other arithmetic  61.3 us (28%)
  blocking collectives  32.8 us (15%)
  starting transfers between devices  19 us (9%)
  matrix products  15.1 us (7%)
  between operations  14.8 us (7%)
  waiting for transfers between devices  8.63 us (4%)
    transpose x8, other arithmetic, kernel_weights(): weights.transpose(0, 1, 3, 2, 4)  52.7 us
    another operation x10, local copies, waits for them, and re-layouts  24.1 us
    ppermute x3, starting transfers between devices, from_behind(): return lax.ppermute(array, axis, pairs)  19 us
    all_gather x1, blocking collectives, on_device(): lax.all_gather(block_times, 'obs', axis=0, tiled=True)  17.3 us
    all_gather x1, blocking collectives, on_device(): lax.all_gather(block_cells, 'obs', axis=0, tiled=True)  15.5 us
    gather x8, local copies, waits for them, and re-layouts, one_block(): vectors[item_cells]  14.5 us
    dot_general x8, matrix products, one_block(): jnp.einsum('sad,ed->sae', gain.astype(jnp.bfloat16), item_cat, preferred_...  14.1 us
    dynamic_slice x16, local copies, waits for them, and re-layouts, far_tiles(): result = lax.map(one_bundle, grouped)  11.9 us
  transfers between devices with their start and end apart: 4, of which 1 were waited for; matrix products, arithmetic and copies ran while one was open for 34% of the time, Pallas kernels for 0%

commit v1 on v0

v1 whole, which is shorter than its diff:
```python
import functools
import math

import jax
import jax.numpy as jnp
from jax import lax
from jax.experimental import pallas as pl
from jax.experimental.pallas import tpu as pltpu
from jax.sharding import PartitionSpec as P

BLOCK = 128
SLOTS = 4
WIDE = SLOTS * BLOCK
TSTEP = 8
CORR = 0.6
DEPTH = 32
LOG2E = math.log2(math.e)
SCALE = (LOG2E / CORR) ** 2
DECAY = LOG2E / TSTEP
TINY = 1e-12
RADIANS = math.pi / 180.0


def split3(x):
    high = x.astype(jnp.bfloat16).astype(jnp.float32)
    rest = x - high
    mid = rest.astype(jnp.bfloat16).astype(jnp.float32)
    low = (rest - mid).astype(jnp.bfloat16).astype(jnp.float32)
    return high, mid, low


def unit_rows(lat, lon):
    latitude = (lat - 89.5) * RADIANS
    longitude = (lon + 0.5) * RADIANS
    across = jnp.cos(latitude)
    return across * jnp.cos(longitude), across * jnp.sin(longitude), jnp.sin(latitude)


def far_terms(units):
    terms = []
    for unit in units:
        h, m, l = split3(unit)
        terms += [h, m, h, m, l, h]
    one = jnp.ones_like(units[0])
    return terms + [one, one, one]


def near_terms(units):
    terms = []
    for unit in units:
        h, m, l = split3(unit * (-2.0 * SCALE))
        terms += [h, h, m, m, h, l]
    return terms + list(split3(jnp.full_like(units[0], 2.0 * SCALE)))


def load_rows(meta, rows, lat_ref, lon_ref, lat_rows, lon_rows, base):
    for row in range(rows):
        for slot in range(SLOTS):
            cell = meta[row, slot]
            span = pl.ds(slot * BLOCK, BLOCK)
            lat_rows[pl.ds(base + row, 1), span] = lat_ref[pl.ds(cell, 1), :].astype(jnp.float32)
            lon_rows[pl.ds(base + row, 1), span] = lon_ref[pl.ds(cell, 1), :].astype(jnp.float32)


def prepare(far, near, n_far, n_near, lat_ref, lon_ref, lat_rows, lon_rows, far_vec, near_rows, near_vec):
    lat_rows[...] = jnp.zeros_like(lat_rows)
    lon_rows[...] = jnp.zeros_like(lon_rows)
    load_rows(far, n_far, lat_ref, lon_ref, lat_rows, lon_rows, 0)
    load_rows(near, n_near, lat_ref, lon_ref, lat_rows, lon_rows, n_far)
    units = unit_rows(lat_rows[...], lon_rows[...])
    far_vec[...] = jnp.zeros_like(far_vec)
    for q, term in enumerate(far_terms(units)):
        for row in range(n_far):
            far_vec[row, pl.ds(q, 1), :] = term[row : row + 1]
    near_rows[...] = jnp.zeros_like(near_rows)
    for q, term in enumerate(near_terms(units)):
        for row in range(n_near):
            near_rows[row, pl.ds(q, 1), :] = term[n_far + row : n_far + row + 1]
    for row in range(n_near):
        near_vec[row] = near_rows[row].T.astype(jnp.bfloat16)


def one_gain(far, near, r, s, cat, far_block, near_vec, weights):
    times = jnp.concatenate(
        [jnp.full((1, BLOCK), far[r, SLOTS + j], jnp.int32) for j in range(SLOTS)], axis=1
    ).astype(jnp.float32)
    for k in range(SLOTS):
        rows = pl.ds(k * BLOCK, BLOCK)
        own_time = near[s, SLOTS + k].astype(jnp.float32)
        lag = jnp.abs(own_time - times) * (-DECAY)
        square = jnp.maximum(
            jnp.dot(near_vec[s, rows, :], far_block, preferred_element_type=jnp.float32), TINY
        )
        weights[rows, :] = jnp.exp2(lag - square * lax.rsqrt(square)).astype(jnp.bfloat16)
    return jnp.dot(cat, weights[...], preferred_element_type=jnp.float32)


def gains_kernel(n_far, far, near, lat_ref, lon_ref, cats, out, lat_rows, lon_rows, far_vec, near_rows, near_vec, weights):
    r = pl.program_id(0)

    @pl.when(r == 0)
    def _():
        prepare(far, near, n_far, 2, lat_ref, lon_ref, lat_rows, lon_rows, far_vec, near_rows, near_vec)

    far_block = far_vec[r].astype(jnp.bfloat16)
    for s in range(2):
        gain = one_gain(far, near, r, s, cats[s], far_block, near_vec, weights)
        out[s, 0] = gain.astype(jnp.bfloat16)


def self_kernel(near, lat_ref, lon_ref, cat, out, lat_rows, lon_rows, far_vec, near_rows, near_vec, weights):
    prepare(near, near, 1, 1, lat_ref, lon_ref, lat_rows, lon_rows, far_vec, near_rows, near_vec)
    gain = one_gain(near, near, 0, 0, cat[0], far_vec[0].astype(jnp.bfloat16), near_vec, weights)
    for j in range(SLOTS):
        out[0, j] = gain[:, j * BLOCK : (j + 1) * BLOCK]


def scratch_of(n_far, n_near):
    rows = -(-(n_far + n_near) // 8) * 8
    return [
        pltpu.VMEM((rows, WIDE), jnp.float32),
        pltpu.VMEM((rows, WIDE), jnp.float32),
        pltpu.VMEM((n_far, DEPTH, WIDE), jnp.float32),
        pltpu.VMEM((n_near, DEPTH, WIDE), jnp.float32),
        pltpu.VMEM((n_near, WIDE, DEPTH), jnp.bfloat16),
        pltpu.VMEM((WIDE, WIDE), jnp.bfloat16),
    ]


def whole(*shape):
    return pl.BlockSpec(shape, lambda *_: (0,) * len(shape))


def self_gain(near, lat, lon, cat):
    return pl.pallas_call(
        self_kernel,
        out_shape=jax.ShapeDtypeStruct((1, SLOTS, BLOCK, BLOCK), jnp.float32),
        in_specs=[pl.BlockSpec(memory_space=pltpu.SMEM)] + [pl.BlockSpec(memory_space=pltpu.VMEM)] * 3,
        out_specs=pl.BlockSpec(memory_space=pltpu.VMEM),
        scratch_shapes=scratch_of(1, 1),
        compiler_params=pltpu.CompilerParams(vmem_limit_bytes=24 * 2**20),
        cost_estimate=pl.CostEstimate(flops=10**8, bytes_accessed=10**6, transcendentals=2**19),
        name="self_gain",
    )(near, lat, lon, cat)


def gains(far, near, lat, lon, cats):
    n_far = far.shape[0]
    return pl.pallas_call(
        functools.partial(gains_kernel, n_far),
        grid=(n_far,),
        out_shape=jax.ShapeDtypeStruct((2, n_far, BLOCK, WIDE), jnp.bfloat16),
        in_specs=[pl.BlockSpec(memory_space=pltpu.SMEM)] * 2
        + [whole(*lat.shape), whole(*lon.shape), whole(*cats.shape)],
        out_specs=pl.BlockSpec((2, 1, BLOCK, WIDE), lambda r: (0, r, 0, 0)),
        scratch_shapes=scratch_of(n_far, 2),
        compiler_params=pltpu.CompilerParams(vmem_limit_bytes=32 * 2**20),
        cost_estimate=pl.CostEstimate(flops=3 * 10**9, bytes_accessed=8 * 10**6, transcendentals=2**24),
        name="gains",
    )(far, near, lat, lon, cats)


def tiles_kernel(group, gain, cat, out):
    for i in range(group):
        tile = lax.dot_general(
            gain[0, i], cat[i], (((1,), (1,)), ((), ())), preferred_element_type=jnp.float32
        )
        out[:, i * BLOCK : (i + 1) * BLOCK] = tile.astype(out.dtype)


def tiles(gain, cats, which, dtype, blocks, shift):
    n_far = cats.shape[0]
    group = 4
    return pl.pallas_call(
        functools.partial(tiles_kernel, group),
        grid=(n_far // group,),
        out_shape=jax.ShapeDtypeStruct((BLOCK, blocks * BLOCK), dtype),
        in_specs=[
            pl.BlockSpec((1, group, BLOCK, WIDE), lambda i: (which, i, 0, 0)),
            pl.BlockSpec((group, BLOCK, WIDE), lambda i: (i, 0, 0)),
        ],
        out_specs=pl.BlockSpec((BLOCK, group * BLOCK), lambda i: (0, i + shift // group)),
        compiler_params=pltpu.CompilerParams(vmem_limit_bytes=24 * 2**20),
        cost_estimate=pl.CostEstimate(flops=3 * 10**8, bytes_accessed=5 * 10**6, transcendentals=0),
        name="tiles",
    )(gain, cats)


def widen_kernel(tile, whole_ref, out):
    del whole_ref
    out[...] = tile[...].astype(jnp.float32)


def put_earlier(tile, cross):
    steps = 2
    width = tile.shape[1] // steps
    return pl.pallas_call(
        widen_kernel,
        grid=(steps,),
        out_shape=jax.ShapeDtypeStruct(cross.shape, cross.dtype),
        in_specs=[
            pl.BlockSpec((BLOCK, width), lambda i: (0, i)),
            pl.BlockSpec(memory_space=pl.ANY),
        ],
        out_specs=pl.BlockSpec((BLOCK, width), lambda i: (0, i)),
        input_output_aliases={1: 0},
        compiler_params=pltpu.CompilerParams(vmem_limit_bytes=24 * 2**20),
        name="put_earlier",
    )(tile, cross)


def on_device(footprints, block_times, block_cells, live_counts, cell_lat, cell_lon):
    group = lax.axis_size("obs")
    spans = lax.axis_size("tm")
    forward = [(i, i + 1) for i in range(spans - 1)]
    backward = [(i + 1, i) for i in range(spans - 1)]
    time_index = lax.axis_index("tm")
    lat = cell_lat.reshape(-1, BLOCK)
    lon = cell_lon.reshape(-1, BLOCK)
    slot_live = jnp.arange(SLOTS)[None, :] < live_counts[:, None]
    prints = jnp.where(slot_live[:, :, None, None], footprints, jnp.zeros((), jnp.bfloat16))
    cat = prints.transpose(0, 2, 1, 3).reshape(1, BLOCK, WIDE)
    pattern = jnp.concatenate([block_cells, time_index * TSTEP + block_times], axis=1)

    far = lax.all_to_all(jnp.broadcast_to(pattern, (group, 2 * SLOTS)), "obs", 0, 0, tiled=True)
    far_cats = lax.all_to_all(jnp.broadcast_to(cat, (group, BLOCK, WIDE)), "obs", 0, 0, tiled=True)
    next_cat = lax.ppermute(cat, "tm", backward)
    next_pattern = lax.ppermute(pattern, "tm", backward)

    footprint_cov = self_gain(pattern, lat, lon, cat)
    near = jnp.concatenate([pattern, next_pattern], axis=0)
    gain = gains(far, near, lat, lon, jnp.concatenate([cat, next_cat], axis=0))
    onward = tiles(gain, far_cats, 1, jnp.bfloat16, group, 0)
    earlier = lax.ppermute(onward, "tm", forward)
    cross = tiles(gain, far_cats, 0, jnp.float32, 2 * group, group)
    cross_cov = put_earlier(earlier, cross)
    return (cross_cov, footprint_cov)


def solution(mesh):
    placed = (
        P(("tm", "obs"), None, None, None),
        P(("tm", "obs"), None),
        P(("tm", "obs"), None),
        P(("tm", "obs")),
        P(),
        P(),
    )
    return jax.shard_map(
        on_device,
        mesh=mesh,
        in_specs=placed,
        out_specs=(P(("tm", "obs"), None), P(("tm", "obs"), None, None, None)),
        check_vma=False,
    )
```

time: 218 us -> 68.4 us (0.31)
  other arithmetic: 61.3 us -> 1.65 us
  local copies, waits for them, and re-layouts: 64.9 us -> 7.53 us
  blocking collectives: 32.8 us -> 0 us
  Pallas kernels: 0 us -> 25.6 us
  matrix products: 15.1 us -> 0 us
  between operations: 14.8 us -> 1.42 us
  starting transfers between devices: 19 us -> 21.9 us
    transpose x9 -> x0, other arithmetic: 54.4 us -> none  [the longest x8 52.7 us: kernel_weights(): weights.transpose(0, 1, 3, 2, 4)]
    all_gather x2 -> x0, blocking collectives: 32.8 us -> none  [the longest x1 17.3 us: on_device(): lax.all_gather(block_times, 'obs', axis=0, tiled=True)]
    pallas_call x0 -> x5, Pallas kernels: none -> 25.6 us  [the longest x1 18.9 us: gains(): pl.pallas_call(functools.partial(gains_kernel, n_far), grid=(n_far,), out...]
    another operation x10 -> x0, local copies, waits for them, and re-layouts: 24.1 us -> none
    gather x10 -> x0, local copies, waits for them, and re-layouts: 16.3 us -> none  [the longest x8 14.5 us: one_block(): vectors[item_cells]]
    dot_general x9 -> x0, matrix products: 15.1 us -> none  [the longest x8 14.1 us: one_block(): jnp.einsum('sad,ed->sae', gain.astype(jnp.bfloat16), item_cat, preferred_...]
    dynamic_slice x16 -> x0, local copies, waits for them, and re-layouts: 11.9 us -> none  [far_tiles(): result = lax.map(one_bundle, grouped)]
    all_to_all x0 -> x2, starting transfers between devices: none -> 11.4 us  [the longest x1 7.58 us: on_device(): lax.all_to_all(jnp.broadcast_to(pattern, (group, 2 * SLOTS)), 'obs', 0, 0...]
  transfers between devices with their start and end apart: 4 -> 5, of which waited for: 1 -> 3; matrix products, arithmetic and copies ran while one was open for 34% -> 2% of each run, Pallas kernels for 0% -> 35%
where the time goes in v1:
time: 68.4 us; the launch traced here: 67.5 us
  Pallas kernels  25.6 us (37%)
  starting transfers between devices  21.9 us (32%)
  waiting for transfers between devices  9.35 us (14%)
  local copies, waits for them, and re-layouts  7.53 us (11%)
  other arithmetic  1.65 us (2%)
  between operations  1.42 us (2%)
    pallas_call x1, Pallas kernels, gains(): pl.pallas_call(functools.partial(gains_kernel, n_far), grid=(n_far,), out...  18.9 us
    all_to_all x1, starting transfers between devices, on_device(): lax.all_to_all(jnp.broadcast_to(pattern, (group, 2 * SLOTS)), 'obs', 0, 0...  7.58 us
    ppermute x1, starting transfers between devices, on_device(): next_cat = lax.ppermute(cat, 'tm', backward)  5.76 us
    unnamed x13, local copies, waits for them, and re-layouts  5.17 us
    all_to_all x1, waiting for transfers between devices, on_device(): lax.all_to_all(jnp.broadcast_to(pattern, (group, 2 * SLOTS)), 'obs', 0, 0...  4.42 us
    all_to_all x1, starting transfers between devices, on_device(): lax.all_to_all(jnp.broadcast_to(cat, (group, BLOCK, WIDE)), 'obs', 0, 0,...  3.85 us
    pallas_call x2, Pallas kernels, tiles(): pl.pallas_call(functools.partial(tiles_kernel, group), grid=(n_far // gro...  3.57 us
    ppermute x1, waiting for transfers between devices, on_device(): next_pattern = lax.ppermute(pattern, 'tm', backward)  3.23 us
  transfers between devices with their start and end apart: 5, of which 3 were waited for; matrix products, arithmetic and copies ran while one was open for 2% of the time, Pallas kernels for 35%

profile of v1, /device:TPU:1, one launch (start us, length us, event | category | flops | bytes accessed | tf_op | source)
XLA Modules:
  0.0 67.5 jit_solution(12009166490249731518)
XLA Ops:
  0.6 0.7 broadcast_add_fusion
  1.3 0.7 %fusion = s32[8]{0:T(128)S(1)} fusion(s32[1,4]{1,0:T(1,128)S(1)} %broadcast_add_fusion, s32[1,4]{1,0:T(1,128)} %param.8), kind=kLoop, calls=%fused_computation.6 | loop fusion | flops 8 | bytes 64 | tf_op jit(solution)/shard_map/concatenate | solution.py:223
  2.0 0.6 broadcast_in_dim.27
  2.6 7.6 %all-to-all-start = ((s32[16,1,8]{2,1,0:T(1,128)}), s32[16,1,8]{2,1,0:T(1,128)S(1)}, u32[]{:S(2)}, u32[]{:S(2)}) async-start(s32[16,1,8]{2,1,0:T(1,128)} %broadcast_in_dim.27), calls=%async_computation | async-start | bytes 16384 | tf_op jit(solution)/shard_map/all_to_all | solution.py:225
  10.2 1.0 %copy.16 = bf16[1,4,128,128]{2,3,1,0:T(8,128)(2,1)S(1)} copy(bf16[1,4,128,128]{3,2,1,0:T(8,128)(2,1)} %param.6) | data formatting | bytes 262144 | tf_op args[0]
  11.9 0.1 broadcast_select_fusion
  12.0 0.1 copy.19
  12.1 4.4 %all-to-all-done = s32[16,1,8]{2,1,0:T(1,128)S(1)} async-done(((s32[16,1,8]{2,1,0:T(1,128)}), s32[16,1,8]{2,1,0:T(1,128)S(1)}, u32[]{:S(2)}, u32[]{:S(2)}) %all-to-all-start) | async-done | bytes 544 | tf_op jit(solution)/shard_map/all_to_all | solution.py:225
  16.6 1.5 %broadcast_in_dim.31 = bf16[16,128,512]{2,1,0:T(8,128)(2,1)} broadcast(bf16[128,512]{1,0:T(8,128)(2,1)S(1)} %copy.19), dimensions={1,2} | broadcast | bytes 2228224 | tf_op jit(solution)/shard_map/broadcast_in_dim | solution.py:226
  18.1 3.9 %all-to-all-start.1 = ((bf16[16,128,512]{2,1,0:T(8,128)(2,1)}), bf16[16,128,512]{2,1,0:T(8,128)(2,1)S(1)}, u32[]{:S(2)}, u32[]{:S(2)}) async-start(bf16[16,128,512]{2,1,0:T(8,128)(2,1)} %broadcast_in_dim.31), calls=%async_computation.1 | async-start | bytes 4194304 | tf_op jit(solution)/shard_map/all_to_all | solution.py:226
  21.9 0.1 copy.21.cat
  22.1 5.8 %collective-permute-start.1 = (bf16[1,128,512]{2,1,0:T(8,128)(2,1)S(1)}, bf16[1,128,512]{2,1,0:T(8,128)(2,1)S(1)}, u32[]{:S(2)}, u32[]{:S(2)}) collective-permute-start(bf16[1,128,512]{2,1,0:T(8,128)(2,1)S(1)} %copy.21.cat), channel_id=1, source_target_pairs={{16,0},{32,16},{48,32},{64,48},{80,64},{96,80},{112,96},{128,112},... | collective-permute-start | bytes 393224 | tf_op jit(solution)/shard_map/ppermute | solution.py:227
  27.8 0.0 copy-done.5
  27.8 0.1 pad_add_fusion.1.near
  27.9 1.9 %collective-permute-start = (s32[1,8]{1,0:T(1,128)S(1)}, s32[1,8]{1,0:T(1,128)S(1)}, u32[]{:S(2)}, u32[]{:S(2)}) collective-permute-start(s32[1,8]{1,0:T(1,128)S(1)} %pad_add_fusion.1.near), channel_id=1, source_target_pairs={{16,0},{32,16},{48,32},{64,48},{80,64},{96,80},{112,96},{128,112},... | collective-permute-start | bytes 104 | tf_op jit(solution)/shard_map/ppermute | solution.py:228
  29.8 3.2 %collective-permute-done = s32[1,8]{1,0:T(1,128)S(1)} collective-permute-done((s32[1,8]{1,0:T(1,128)S(1)}, s32[1,8]{1,0:T(1,128)S(1)}, u32[]{:S(2)}, u32[]{:S(2)}) %collective-permute-start) | collective-permute-done | bytes 64 | tf_op jit(solution)/shard_map/ppermute | solution.py:228
  33.1 0.1 pad_add_fusion.near
  33.1 0.0 collective-permute-done.1
  33.2 0.0 copy-done.3
  33.2 0.0 copy-done.4
  33.2 18.9 %gains.1.gain = bf16[2,16,128,512]{3,2,1,0:T(8,128)(2,1)S(1)} custom-call(s32[16,8]{1,0:T(8,128)S(1)} %bitcast.12, s32[2,8]{1,0:T(2,128)S(1)} %pad_add_fusion.near, s32[512,128]{1,0:T(8,128)S(1)} %bitcast.13, s32[512,128]{1,0:T(8,128)S(1)} %bitcast.15, bf16[2,128,512]{2,1,0:T(8,128)(2,1)S(1)} %pad_maximum_fusion.cats), custom_call_target="tpu_custom_call" | custom-call | flops 3000000000 | bytes 8000000 | tf_op jit(solution)/shard_map/gains/pallas_call | solution.py:149
  52.1 0.0 copy-start
  52.1 1.9 %copy-done = bf16[2,16,128,512]{3,2,1,0:T(8,128)(2,1)} copy-done((bf16[2,16,128,512]{3,2,1,0:T(8,128)(2,1)}, bf16[2,16,128,512]{3,2,1,0:T(8,128)(2,1)S(1)}, u32[]{:S(2)}) %copy-start) | copy-done | bytes 4194328
  54.1 0.0 all-to-all-done.1.cat
  54.1 2.2 %copy-done.1 = bf16[2,16,128,512]{3,2,1,0:T(8,128)(2,1)S(1)} copy-done((bf16[2,16,128,512]{3,2,1,0:T(8,128)(2,1)S(1)}, bf16[2,16,128,512]{3,2,1,0:T(8,128)(2,1)}, u32[]{:S(2)}) %copy-start.1) | copy-done | bytes 4194328
  56.3 1.3 %tiles.2 = bf16[128,2048]{1,0:T(8,128)(2,1)S(1)} custom-call(bf16[2,16,128,512]{3,2,1,0:T(8,128)(2,1)S(1)} %copy-done.1, bf16[16,128,512]{2,1,0:T(8,128)(2,1)S(1)} %all-to-all-done.1.cat), custom_call_target="tpu_custom_call" | custom-call | flops 300000000 | bytes 5000000 | tf_op jit(solution)/shard_map/tiles/pallas_call | solution.py:174
  57.5 2.7 %collective-permute-start.2 = (bf16[128,2048]{1,0:T(8,128)(2,1)S(1)}, bf16[128,2048]{1,0:T(8,128)(2,1)S(1)}, u32[]{:S(2)}, u32[]{:S(2)}) collective-permute-start(bf16[128,2048]{1,0:T(8,128)(2,1)S(1)} %tiles.2), channel_id=1, source_target_pairs={{0,16},{16,32},{32,48},{48,64},{64,80},{80,96},{96,112},{112,128},... | collective-permute-start | bytes 1572872 | tf_op jit(solution)/shard_map/ppermute | solution.py:234
  60.3 2.1 %self_gain.1 = f32[1,4,128,128]{3,2,1,0:T(8,128)} custom-call(s32[1,8]{1,0:T(1,128)S(1)} %pad_add_fusion.1.near, s32[512,128]{1,0:T(8,128)S(1)} %bitcast.14, s32[512,128]{1,0:T(8,128)S(1)} %bitcast.16, bf16[1,128,512]{2,1,0:T(8,128)(2,1)S(1)} %copy.21.cat), custom_call_target="tpu_custom_call" | custom-call | flops 100000000 | bytes 1000000 | tf_op jit(solution)/shard_map/self_gain/pallas_call | solution.py:135
  62.4 0.0 copy-done.2
  62.4 2.3 %tiles.3.whole_ref = f32[128,4096]{1,0:T(8,128)} custom-call(bf16[2,16,128,512]{3,2,1,0:T(8,128)(2,1)S(1)} %copy-done.2, bf16[16,128,512]{2,1,0:T(8,128)(2,1)S(1)} %all-to-all-done.1.cat), custom_call_target="tpu_custom_call" | custom-call | flops 300000000 | bytes 5000000 | tf_op jit(solution)/shard_map/tiles/pallas_call | solution.py:174
  64.7 1.7 %collective-permute-done.2.tile = bf16[128,2048]{1,0:T(8,128)(2,1)S(1)} collective-permute-done((bf16[128,2048]{1,0:T(8,128)(2,1)S(1)}, bf16[128,2048]{1,0:T(8,128)(2,1)S(1)}, u32[]{:S(2)}, u32[]{:S(2)}) %collective-permute-start.2) | collective-permute-done | bytes 524320 | tf_op jit(solution)/shard_map/ppermute | solution.py:234
  66.4 1.1 %put_earlier.1 = f32[128,4096]{1,0:T(8,128)} custom-call(bf16[128,2048]{1,0:T(8,128)(2,1)S(1)} %collective-permute-done.2.tile, f32[128,4096]{1,0:T(8,128)} %tiles.3.whole_ref), custom_call_target="tpu_custom_call", output_to_operand_aliasing={{}: (1, {})} | custom-call | tf_op jit(solution)/shard_map/put_earlier/pallas_call | solution.py:197
  (7 shorter events, 0.0 us)
Async XLA Ops:
  2.6 13.9 %all-to-all-start = ((s32[16,1,8]{2,1,0:T(1,128)}), s32[16,1,8]{2,1,0:T(1,128)S(1)}, u32[]{:S(2)}, u32[]{:S(2)}) async-start(s32[16,1,8]{2,1,0:T(1,128)} %broadcast_in_dim.27), calls=%async_computation | async-start | bytes 16384 | tf_op jit(solution)/shard_map/all_to_all | solution.py:225
  18.1 9.8 %copy-start.5 = (s32[1,4]{1,0:T(1,128)S(1)}, s32[1,4]{1,0:T(1,128)}, u32[]{:S(2)}) copy-start(s32[1,4]{1,0:T(1,128)} %param.8) | copy-start | bytes 52
  18.1 15.1 %copy-start.3 = (s32[65536]{0:T(1024)S(1)}, s32[65536]{0:T(1024)}, u32[]{:S(2)}) copy-start(s32[65536]{0:T(1024)} %param.10) | copy-start | bytes 786436
  18.1 15.1 %copy-start.4 = (s32[65536]{0:T(1024)S(1)}, s32[65536]{0:T(1024)}, u32[]{:S(2)}) copy-start(s32[65536]{0:T(1024)} %param.11) | copy-start | bytes 786436
  18.1 36.0 %all-to-all-start.1 = ((bf16[16,128,512]{2,1,0:T(8,128)(2,1)}), bf16[16,128,512]{2,1,0:T(8,128)(2,1)S(1)}, u32[]{:S(2)}, u32[]{:S(2)}) async-start(bf16[16,128,512]{2,1,0:T(8,128)(2,1)} %broadcast_in_dim.31), calls=%async_computation.1 | async-start | bytes 4194304 | tf_op jit(solution)/shard_map/all_to_all | solution.py:226
  22.1 11.1 %collective-permute-start.1 = (bf16[1,128,512]{2,1,0:T(8,128)(2,1)S(1)}, bf16[1,128,512]{2,1,0:T(8,128)(2,1)S(1)}, u32[]{:S(2)}, u32[]{:S(2)}) collective-permute-start(bf16[1,128,512]{2,1,0:T(8,128)(2,1)S(1)} %copy.21.cat), channel_id=1, source_target_pairs={{16,0},{32,16},{48,32},{64,48},{80,64},{96,80},{112,96},{128,112},... | collective-permute-start | bytes 393224 | tf_op jit(solution)/shard_map/ppermute | solution.py:227
  27.9 5.1 %collective-permute-start = (s32[1,8]{1,0:T(1,128)S(1)}, s32[1,8]{1,0:T(1,128)S(1)}, u32[]{:S(2)}, u32[]{:S(2)}) collective-permute-start(s32[1,8]{1,0:T(1,128)S(1)} %pad_add_fusion.1.near), channel_id=1, source_target_pairs={{16,0},{32,16},{48,32},{64,48},{80,64},{96,80},{112,96},{128,112},... | collective-permute-start | bytes 104 | tf_op jit(solution)/shard_map/ppermute | solution.py:228
  52.1 2.0 %copy-start = (bf16[2,16,128,512]{3,2,1,0:T(8,128)(2,1)}, bf16[2,16,128,512]{3,2,1,0:T(8,128)(2,1)S(1)}, u32[]{:S(2)}) copy-start(bf16[2,16,128,512]{3,2,1,0:T(8,128)(2,1)S(1)} %gains.1.gain) | copy-start | bytes 12582916
  54.1 2.2 %copy-start.1 = (bf16[2,16,128,512]{3,2,1,0:T(8,128)(2,1)S(1)}, bf16[2,16,128,512]{3,2,1,0:T(8,128)(2,1)}, u32[]{:S(2)}) copy-start(bf16[2,16,128,512]{3,2,1,0:T(8,128)(2,1)} %copy-done) | copy-start | bytes 12582916
  56.3 6.1 %copy-start.2 = (bf16[2,16,128,512]{3,2,1,0:T(8,128)(2,1)S(1)}, bf16[2,16,128,512]{3,2,1,0:T(8,128)(2,1)}, u32[]{:S(2)}) copy-start(bf16[2,16,128,512]{3,2,1,0:T(8,128)(2,1)} %copy-done) | copy-start | bytes 12582916
  57.5 8.9 %collective-permute-start.2 = (bf16[128,2048]{1,0:T(8,128)(2,1)S(1)}, bf16[128,2048]{1,0:T(8,128)(2,1)S(1)}, u32[]{:S(2)}, u32[]{:S(2)}) collective-permute-start(bf16[128,2048]{1,0:T(8,128)(2,1)S(1)} %tiles.2), channel_id=1, source_target_pairs={{0,16},{16,32},{32,48},{48,64},{64,80},{80,96},{96,112},{112,128},... | collective-permute-start | bytes 1572872 | tf_op jit(solution)/shard_map/ppermute | solution.py:234

commit v2 on v0

v2 whole, which is shorter than its diff:
```python
import functools
import math

import jax
import jax.numpy as jnp
from jax import lax
from jax.experimental import pallas as pl
from jax.experimental.pallas import tpu as pltpu
from jax.sharding import PartitionSpec as P

BLOCK = 128
SLOTS = 4
WIDE = SLOTS * BLOCK
PATTERN = 16
ROWS = BLOCK + PATTERN
PARTS = 3
DEPTH = PARTS * PATTERN
ONE_ROW = 9
TIME_ROW = 10
TSTEP = 8
CORR = 0.6
SCALE = (math.log2(math.e) / CORR) ** 2
DECAY = math.log2(math.e) / TSTEP
TINY = 1e-12
RADIANS = math.pi / 180.0
SIDE = 4
PAIR = 2


def rounded(x):
    return x.astype(jnp.bfloat16).astype(jnp.float32)


def split3(x):
    high = rounded(x)
    mid = rounded(x - high)
    return high, mid, rounded(x - high - mid)


def block_kernel(count, prints, times, cells, live, lat_ref, lon_ref, block, payload, lat_row, lon_row, pattern, sems):
    copies = []
    for j in range(SLOTS):
        for source, target, sem in ((lat_ref, lat_row, 0), (lon_ref, lon_row, 1)):
            copy = pltpu.make_async_copy(source.at[cells[0, j]], target.at[j], sems.at[sem, j])
            copy.start()
            copies.append(copy)
    for j in range(SLOTS):
        kept = jnp.where(j < live[0], prints[0, j], jnp.zeros((BLOCK, BLOCK), jnp.bfloat16))
        block[0, 0:BLOCK, j * BLOCK : (j + 1) * BLOCK] = kept
    base = lax.axis_index("tm") * TSTEP
    for copy in copies:
        copy.wait()
    lat = jnp.concatenate([lat_row[j] for j in range(SLOTS)], axis=1).astype(jnp.float32)
    lon = jnp.concatenate([lon_row[j] for j in range(SLOTS)], axis=1).astype(jnp.float32)
    latitude = (lat - 89.5) * RADIANS
    longitude = (lon + 0.5) * RADIANS
    across = jnp.cos(latitude)
    units = (across * jnp.cos(longitude), across * jnp.sin(longitude), jnp.sin(latitude))
    pattern[...] = jnp.zeros_like(pattern)
    for c, unit in enumerate(units):
        for part, value in enumerate(split3(unit)):
            pattern[pl.ds(PARTS * c + part, 1), :] = value
    pattern[pl.ds(ONE_ROW, 1), :] = jnp.ones((1, WIDE), jnp.float32)
    for j in range(SLOTS):
        when = (base + times[0, j]).astype(jnp.float32)
        pattern[pl.ds(TIME_ROW, 1), j * BLOCK : (j + 1) * BLOCK] = jnp.full((1, BLOCK), when)
    block[0, BLOCK:ROWS, :] = pattern[...].astype(jnp.bfloat16)
    for i in range(count):
        payload[i] = block[0]


def make_block(footprints, times, cells, live, lat, lon, count):
    smem = pl.BlockSpec(memory_space=pltpu.SMEM)
    vmem = pl.BlockSpec(memory_space=pltpu.VMEM)
    hbm = pl.BlockSpec(memory_space=pl.ANY)
    return pl.pallas_call(
        functools.partial(block_kernel, count),
        out_shape=(
            jax.ShapeDtypeStruct((1, ROWS, WIDE), jnp.bfloat16),
            jax.ShapeDtypeStruct((count, ROWS, WIDE), jnp.bfloat16),
        ),
        in_specs=[vmem, smem, smem, smem, hbm, hbm],
        out_specs=(vmem, vmem),
        scratch_shapes=[
            pltpu.VMEM((SLOTS, 1, BLOCK), jnp.int32),
            pltpu.VMEM((SLOTS, 1, BLOCK), jnp.int32),
            pltpu.VMEM((PATTERN, WIDE), jnp.float32),
            pltpu.SemaphoreType.DMA((2, SLOTS)),
        ],
        compiler_params=pltpu.CompilerParams(vmem_limit_bytes=12 * 2**20),
        name="make_block",
    )(footprints, times, cells, live, lat, lon)


def prepare_near(block, near_rows):
    pattern = block[0, BLOCK:ROWS, :].astype(jnp.float32)
    near_rows[...] = jnp.zeros_like(near_rows)
    for c in range(3):
        high, mid, low = (pattern[PARTS * c + part : PARTS * c + part + 1] for part in range(PARTS))
        scaled = split3((high + mid + low) * (-2.0 * SCALE))
        for segment, value in enumerate(scaled):
            for part in range(PARTS - segment):
                near_rows[pl.ds(segment * PATTERN + PARTS * c + part, 1), :] = value
    ends = split3(jnp.full((1, WIDE), 2.0 * SCALE, jnp.float32))
    for segment, value in enumerate(ends):
        near_rows[pl.ds(segment * PATTERN + ONE_ROW, 1), :] = value
    near_rows[pl.ds(TIME_ROW, 1), :] = jnp.zeros((1, WIDE), jnp.float32)
    return near_rows[...].T.astype(jnp.bfloat16), pattern[TIME_ROW : TIME_ROW + 1]


def weigh(near_vec, near_time, far_pattern, weights):
    far_vec = jnp.concatenate([far_pattern] * PARTS, axis=0)
    far_time = far_pattern.astype(jnp.float32)[TIME_ROW : TIME_ROW + 1]
    for k in range(SLOTS):
        rows = pl.ds(k * BLOCK, BLOCK)
        own = jnp.concatenate([near_time[:, k * BLOCK : (k + 1) * BLOCK]] * SLOTS, axis=1)
        lag = jnp.abs(own - far_time) * (-DECAY)
        square = jnp.maximum(jnp.dot(near_vec[rows, :], far_vec, preferred_element_type=jnp.float32), TINY)
        weights[rows, :] = jnp.exp2(lag - square * lax.rsqrt(square)).astype(jnp.bfloat16)


def self_kernel(block, out, near_rows, near_vec, weights):
    near_vec[...], when = prepare_near(block, near_rows)
    weigh(near_vec, when, block[0, BLOCK:ROWS, :], weights)
    gain = jnp.dot(block[0, 0:BLOCK, :], weights[...], preferred_element_type=jnp.float32)
    for j in range(SLOTS):
        out[0, j] = gain[:, j * BLOCK : (j + 1) * BLOCK]


def self_gain(block):
    return pl.pallas_call(
        self_kernel,
        out_shape=jax.ShapeDtypeStruct((1, SLOTS, BLOCK, BLOCK), jnp.float32),
        in_specs=[pl.BlockSpec(memory_space=pltpu.VMEM)],
        out_specs=pl.BlockSpec(memory_space=pltpu.VMEM),
        scratch_shapes=[
            pltpu.VMEM((DEPTH, WIDE), jnp.float32),
            pltpu.VMEM((WIDE, DEPTH), jnp.bfloat16),
            pltpu.VMEM((WIDE, WIDE), jnp.bfloat16),
        ],
        compiler_params=pltpu.CompilerParams(vmem_limit_bytes=12 * 2**20),
        cost_estimate=pl.CostEstimate(flops=2 * 10**9, bytes_accessed=10**6, transcendentals=2**19),
        name="self_gain",
    )(block)


def tiles_kernel(count, *refs):
    blocks, far, outs = refs[:count], refs[count], refs[count + 1 : 2 * count + 1]
    near_rows, near_vec, near_time, cats, tiles, weights = refs[2 * count + 1 :]
    n_far = far.shape[0]
    units = count * n_far
    for s in range(count):
        vec, when = prepare_near(blocks[s], near_rows)
        near_vec[s] = vec
        near_time[s] = jnp.broadcast_to(when, near_time.shape[1:])
        cats[s] = blocks[s][0, 0:BLOCK, :]

    def weigh_unit(u, slot):
        s, r = u // n_far, lax.rem(u, n_far)
        weigh(near_vec.at[s], near_time[s, 0:1, :], far[r, BLOCK:ROWS, :], weights.at[slot])

    def tile_unit(u, slot):
        s, r = u // n_far, lax.rem(u, n_far)
        gain = jnp.dot(cats[s], weights[slot], preferred_element_type=jnp.float32)
        tiles[u] = lax.dot_general(
            gain.astype(jnp.bfloat16),
            far[r, 0:BLOCK, :],
            (((1,), (1,)), ((), ())),
            preferred_element_type=jnp.float32,
        ).astype(tiles.dtype)

    def turn(i, carry):
        u = 2 * i
        weigh_unit(u, 0)
        tile_unit(jnp.maximum(u - 1, 0), 1)
        weigh_unit(u + 1, 1)
        tile_unit(u, 0)
        return carry

    lax.fori_loop(0, units // 2, turn, 0)
    tile_unit(units - 1, 1)
    for u in range(units):
        s, r = u // n_far, u % n_far
        outs[s][:, r * BLOCK : (r + 1) * BLOCK] = tiles[u]


def make_tiles(blocks, far, dtype):
    count, n_far = len(blocks), far.shape[0]
    vmem = pl.BlockSpec(memory_space=pltpu.VMEM)
    shape = jax.ShapeDtypeStruct((BLOCK, n_far * BLOCK), dtype)
    return pl.pallas_call(
        functools.partial(tiles_kernel, count),
        out_shape=(shape,) * count,
        in_specs=[vmem] * (count + 1),
        out_specs=(vmem,) * count,
        scratch_shapes=[
            pltpu.VMEM((DEPTH, WIDE), jnp.float32),
            pltpu.VMEM((count, WIDE, DEPTH), jnp.bfloat16),
            pltpu.VMEM((count, 8, WIDE), jnp.float32),
            pltpu.VMEM((count, BLOCK, WIDE), jnp.bfloat16),
            pltpu.VMEM((count * n_far, BLOCK, BLOCK), dtype),
            pltpu.VMEM((2, WIDE, WIDE), jnp.bfloat16),
        ],
        compiler_params=pltpu.CompilerParams(vmem_limit_bytes=16 * 2**20),
        cost_estimate=pl.CostEstimate(
            flops=count * 10**9, bytes_accessed=count * 2 * 10**6, transcendentals=count * 2**22
        ),
        name="make_tiles",
    )(*blocks, far)


def place_kernel(own, partner, before, before_partner, out):
    step = pl.program_id(0)
    lower = lax.rem(lax.axis_index("obs"), SIDE) < PAIR
    half = PAIR * BLOCK
    mine = jnp.where(step < SIDE, before[...].astype(jnp.float32), own[...])
    other = jnp.where(step < SIDE, before_partner[...], partner[...]).astype(jnp.float32)
    out[:, 0:half] = jnp.where(lower, mine, other)
    out[:, half:] = jnp.where(lower, other, mine)


def place(own, partner, before, before_partner):
    half = PAIR * BLOCK
    late = pl.BlockSpec((BLOCK, half), lambda i: (0, jnp.maximum(i - SIDE, 0)))
    early = pl.BlockSpec((BLOCK, half), lambda i: (0, jnp.minimum(i, SIDE - 1)))
    return pl.pallas_call(
        place_kernel,
        grid=(2 * SIDE,),
        out_shape=jax.ShapeDtypeStruct((BLOCK, 4 * own.shape[1]), jnp.float32),
        in_specs=[late, late, early, early],
        out_specs=pl.BlockSpec((BLOCK, 2 * half), lambda i: (0, i)),
        compiler_params=pltpu.CompilerParams(vmem_limit_bytes=12 * 2**20),
        name="place",
    )(own, partner, before, before_partner)


def on_device(footprints, block_times, block_cells, live_counts, cell_lat, cell_lon):
    group = lax.axis_size("obs")
    spans = lax.axis_size("tm")
    axes = ("tm", "obs")
    near_by = [[o for o in range(group) if o % SIDE // PAIR == b] for b in range(SIDE // PAIR)]
    across = [o // SIDE * SIDE + SIDE - 1 - o % SIDE for o in range(group)]
    to_partner = [(t * group + o, t * group + across[o]) for t in range(spans) for o in range(group)]

    def steps(by, crossing):
        return [
            (t * group + o, (t + by) * group + (across[o] if crossing else o))
            for t in range(spans)
            if 0 <= t + by < spans
            for o in range(group)
        ]

    lat = cell_lat.reshape(-1, 1, BLOCK)
    lon = cell_lon.reshape(-1, 1, BLOCK)
    block, payload = make_block(
        footprints, block_times, block_cells, live_counts, lat, lon, group // (SIDE // PAIR)
    )
    far = lax.all_to_all(payload, "obs", 0, 0, tiled=True, axis_index_groups=near_by)
    partner_block = lax.ppermute(block, axes, to_partner)
    next_block = lax.ppermute(block, axes, steps(-1, False))
    next_partner_block = lax.ppermute(block, axes, steps(-1, True))
    footprint_cov = self_gain(block)
    next_partner_tiles, next_tiles = make_tiles((next_partner_block, next_block), far, jnp.bfloat16)
    before_partner = lax.ppermute(next_partner_tiles, axes, steps(1, True))
    before = lax.ppermute(next_tiles, axes, steps(1, False))
    (partner_tiles,) = make_tiles((partner_block,), far, jnp.bfloat16)
    partner = lax.ppermute(partner_tiles, axes, to_partner)
    (own,) = make_tiles((block,), far, jnp.float32)
    cross_cov = place(own, partner, before, before_partner)
    return (cross_cov, footprint_cov)


def solution(mesh):
    placed = (
        P(("tm", "obs"), None, None, None),
        P(("tm", "obs"), None),
        P(("tm", "obs"), None),
        P(("tm", "obs")),
        P(),
        P(),
    )
    return jax.shard_map(
        on_device,
        mesh=mesh,
        in_specs=placed,
        out_specs=(P(("tm", "obs"), None), P(("tm", "obs"), None, None, None)),
        check_vma=False,
    )
```

time: 218 us -> 65 us (0.30)
  the two profiles are of different devices: /device:TPU:1 before, /device:TPU:96 now
where the time goes in v2:
time: 65 us; the launch traced here: 64.6 us
  starting transfers between devices  26.2 us (40%)
  Pallas kernels  22.1 us (34%)
  waiting for transfers between devices  10.7 us (16%)
  local copies, waits for them, and re-layouts  4.11 us (6%)
  between operations  1.39 us (2%)
    pallas_call x3, Pallas kernels, make_tiles(): pl.pallas_call(functools.partial(tiles_kernel, count), out_shape=(shape,)...  15.6 us
    all_to_all x1, waiting for transfers between devices, on_device(): lax.all_to_all(payload, 'obs', 0, 0, tiled=True, axis_index_groups=near_by)  7.56 us
    ppermute x1, starting transfers between devices, on_device(): before_partner = lax.ppermute(next_partner_tiles, axes, steps(1, True))  6.83 us
    all_to_all x1, starting transfers between devices, on_device(): lax.all_to_all(payload, 'obs', 0, 0, tiled=True, axis_index_groups=near_by)  5.41 us
    unnamed x10, local copies, waits for them, and re-layouts  4.11 us
    ppermute x1, starting transfers between devices, on_device(): next_partner_block = lax.ppermute(block, axes, steps(-1, True))  3.61 us
    ppermute x1, starting transfers between devices, on_device(): next_block = lax.ppermute(block, axes, steps(-1, False))  3.31 us
    pallas_call x1, Pallas kernels, place(): pl.pallas_call(place_kernel, grid=(2 * SIDE,), out_shape=jax.ShapeDtypeSt...  3.18 us
  transfers between devices with their start and end apart: 7, of which 3 were waited for; matrix products, arithmetic and copies ran while one was open for 0% of the time, Pallas kernels for 26%

profile of v2, /device:TPU:96, one launch (start us, length us, event | category | flops | bytes accessed | tf_op | source)
XLA Modules:
  0.0 64.6 jit_solution(2074649395668636652)
XLA Ops:
  1.3 0.0 copy-start
  1.3 0.9 %copy-done = s32[65536]{0:T(1024)S(1)} copy-done((s32[65536]{0:T(1024)S(1)}, s32[65536]{0:T(1024)}, u32[]{:S(2)}) %copy-start) | copy-done | bytes 262168
  2.2 0.0 copy-start.1
  2.2 0.9 %copy-done.1 = s32[65536]{0:T(1024)S(1)} copy-done((s32[65536]{0:T(1024)S(1)}, s32[65536]{0:T(1024)}, u32[]{:S(2)}) %copy-start.1) | copy-done | bytes 262168
  3.2 0.0 copy-start.2
  3.2 0.9 %copy-done.2 = bf16[1,4,128,128]{3,2,1,0:T(8,128)(2,1)S(1)} copy-done((bf16[1,4,128,128]{3,2,1,0:T(8,128)(2,1)S(1)}, bf16[1,4,128,128]{3,2,1,0:T(8,128)(2,1)}, u32[]{:S(2)}) %copy-start.2) | copy-done | bytes 131096
  4.1 0.0 copy-start.3
  4.1 0.7 %copy-done.3 = s32[1,4]{1,0:T(1,128)S(1)} copy-done((s32[1,4]{1,0:T(1,128)S(1)}, s32[1,4]{1,0:T(1,128)}, u32[]{:S(2)}) %copy-start.3) | copy-done | bytes 40
  4.7 0.0 copy-start.4
  4.7 0.7 %copy-done.4 = s32[1,4]{1,0:T(1,128)S(1)} copy-done((s32[1,4]{1,0:T(1,128)S(1)}, s32[1,4]{1,0:T(1,128)}, u32[]{:S(2)}) %copy-start.4) | copy-done | bytes 40
  5.4 1.9 %make_block.1 = (bf16[1,144,512]{2,1,0:T(8,128)(2,1)S(1)}, bf16[8,144,512]{2,1,0:T(8,128)(2,1)}) custom-call(bf16[1,4,128,128]{3,2,1,0:T(8,128)(2,1)S(1)} %copy-done.2, s32[1,4]{1,0:T(1,128)S(1)} %copy-done.3, s32[1,4]{1,0:T(1,128)S(1)} %copy-done.4, s32[1]{0:T(128)S(6)} %copy.8.live, s32[512,1,128]{2,1,0:T(1,128)S(1)} %bitcast.2, s32[512,1,128]{2,1,0:T(1,128)S(1)} %bitcast.3), custom_call_target="tpu_custom_call" | custom-call | tf_op jit(solution)/shard_map/make_block/pallas_call | solution.py:76
  7.3 5.4 %all-to-all-start = ((bf16[8,144,512]{2,1,0:T(8,128)(2,1)}), bf16[8,144,512]{2,1,0:T(8,128)(2,1)S(1)}, u32[]{:S(2)}, u32[]{:S(2)}) async-start(bf16[8,144,512]{2,1,0:T(8,128)(2,1)} %get-tuple-element.7), calls=%async_computation | async-start | bytes 2359296 | tf_op jit(solution)/shard_map/all_to_all | solution.py:258
  12.7 3.6 %collective-permute-start.2 = (bf16[1,144,512]{2,1,0:T(8,128)(2,1)S(1)}, bf16[1,144,512]{2,1,0:T(8,128)(2,1)S(1)}, u32[]{:S(2)}, u32[]{:S(2)}) collective-permute-start(bf16[1,144,512]{2,1,0:T(8,128)(2,1)S(1)} %get-tuple-element.6.refs_0_.block), channel_id=1, source_target_pairs={{16,3},{17,2},{18,1},{19,0},{20,7},{21,6},{22,5},{23,4},{24,11},{2... | collective-permute-start | bytes 442376 | tf_op jit(solution)/shard_map/ppermute | solution.py:261
  16.4 3.3 %collective-permute-start.3 = (bf16[1,144,512]{2,1,0:T(8,128)(2,1)S(1)}, bf16[1,144,512]{2,1,0:T(8,128)(2,1)S(1)}, u32[]{:S(2)}, u32[]{:S(2)}) collective-permute-start(bf16[1,144,512]{2,1,0:T(8,128)(2,1)S(1)} %get-tuple-element.6.refs_0_.block), channel_id=1, source_target_pairs={{16,0},{17,1},{18,2},{19,3},{20,4},{21,5},{22,6},{23,7},{24,8},{25... | collective-permute-start | bytes 442376 | tf_op jit(solution)/shard_map/ppermute | solution.py:260
  19.7 2.1 %collective-permute-start = (bf16[1,144,512]{2,1,0:T(8,128)(2,1)S(1)}, bf16[1,144,512]{2,1,0:T(8,128)(2,1)S(1)}, u32[]{:S(2)}, u32[]{:S(2)}) collective-permute-start(bf16[1,144,512]{2,1,0:T(8,128)(2,1)S(1)} %get-tuple-element.6.refs_0_.block), channel_id=1, source_target_pairs={{0,3},{1,2},{2,1},{3,0},{4,7},{5,6},{6,5},{7,4},{8,11},{9,10},{10,... | collective-permute-start | bytes 442376 | tf_op jit(solution)/shard_map/ppermute | solution.py:259
  21.8 0.0 collective-permute-done.2.refs_0_
  21.8 0.5 collective-permute-done.3.refs_1_
  22.3 7.6 %all-to-all-done.refs_1_.refs_2_ = bf16[8,144,512]{2,1,0:T(8,128)(2,1)S(1)} async-done(((bf16[8,144,512]{2,1,0:T(8,128)(2,1)}), bf16[8,144,512]{2,1,0:T(8,128)(2,1)S(1)}, u32[]{:S(2)}, u32[]{:S(2)}) %all-to-all-start) | async-done | bytes 1179680 | tf_op jit(solution)/shard_map/all_to_all | solution.py:258
  29.9 7.6 %make_tiles.5 = (bf16[128,1024]{1,0:T(8,128)(2,1)S(1)}, bf16[128,1024]{1,0:T(8,128)(2,1)S(1)}) custom-call(bf16[1,144,512]{2,1,0:T(8,128)(2,1)S(1)} %collective-permute-done.2.refs_0_, bf16[1,144,512]{2,1,0:T(8,128)(2,1)S(1)} %collective-permute-done.3.refs_1_, bf16[8,144,512]{2,1,0:T(8,128)(2,1)S(1)} %all-to-all-done.refs_1_.refs_2_), custom_call_target="tpu_custom_call" | custom-call | flops 2000000000 | bytes 4000000 | tf_op jit(solution)/shard_map/make_tiles/pallas_call | solution.py:191
  37.5 1.9 %collective-permute-start.4 = (bf16[128,1024]{1,0:T(8,128)(2,1)S(1)}, bf16[128,1024]{1,0:T(8,128)(2,1)S(1)}, u32[]{:S(2)}, u32[]{:S(2)}) collective-permute-start(bf16[128,1024]{1,0:T(8,128)(2,1)S(1)} %get-tuple-element.8), channel_id=1, source_target_pairs={{0,16},{1,17},{2,18},{3,19},{4,20},{5,21},{6,22},{7,23},{8,24},{9,... | collective-permute-start | bytes 786440 | tf_op jit(solution)/shard_map/ppermute | solution.py:265
  39.4 6.8 %collective-permute-start.5 = (bf16[128,1024]{1,0:T(8,128)(2,1)S(1)}, bf16[128,1024]{1,0:T(8,128)(2,1)S(1)}, u32[]{:S(2)}, u32[]{:S(2)}) collective-permute-start(bf16[128,1024]{1,0:T(8,128)(2,1)S(1)} %get-tuple-element.9), channel_id=1, source_target_pairs={{0,19},{1,18},{2,17},{3,16},{4,23},{5,22},{6,21},{7,20},{8,27},{9,... | collective-permute-start | bytes 786440 | tf_op jit(solution)/shard_map/ppermute | solution.py:264
  46.2 0.0 collective-permute-done.refs_0_
  46.3 4.0 %make_tiles.4 = bf16[128,1024]{1,0:T(8,128)(2,1)S(1)} custom-call(bf16[1,144,512]{2,1,0:T(8,128)(2,1)S(1)} %collective-permute-done.refs_0_, bf16[8,144,512]{2,1,0:T(8,128)(2,1)S(1)} %all-to-all-done.refs_1_.refs_2_), custom_call_target="tpu_custom_call" | custom-call | flops 1000000000 | bytes 2000000 | tf_op jit(solution)/shard_map/make_tiles/pallas_call | solution.py:191
  50.3 3.1 %collective-permute-start.1 = (bf16[128,1024]{1,0:T(8,128)(2,1)S(1)}, bf16[128,1024]{1,0:T(8,128)(2,1)S(1)}, u32[]{:S(2)}, u32[]{:S(2)}) collective-permute-start(bf16[128,1024]{1,0:T(8,128)(2,1)S(1)} %make_tiles.4), channel_id=1, source_target_pairs={{0,3},{1,2},{2,1},{3,0},{4,7},{5,6},{6,5},{7,4},{8,11},{9,10},{10,... | collective-permute-start | bytes 786440 | tf_op jit(solution)/shard_map/ppermute | solution.py:267
  53.4 1.4 %self_gain.1 = f32[1,4,128,128]{3,2,1,0:T(8,128)} custom-call(bf16[1,144,512]{2,1,0:T(8,128)(2,1)S(1)} %get-tuple-element.6.refs_0_.block), custom_call_target="tpu_custom_call" | custom-call | flops 2000000000 | bytes 1000000 | tf_op jit(solution)/shard_map/self_gain/pallas_call | solution.py:131
  54.8 4.0 %make_tiles.3.own = f32[128,1024]{1,0:T(8,128)S(1)} custom-call(bf16[1,144,512]{2,1,0:T(8,128)(2,1)S(1)} %get-tuple-element.6.refs_0_.block, bf16[8,144,512]{2,1,0:T(8,128)(2,1)S(1)} %all-to-all-done.refs_1_.refs_2_), custom_call_target="tpu_custom_call" | custom-call | flops 1000000000 | bytes 2000000 | tf_op jit(solution)/shard_map/make_tiles/pallas_call | solution.py:191
  58.8 0.0 collective-permute-done.4.before
  58.8 0.0 collective-permute-done.5.before_partner
  58.8 2.6 %collective-permute-done.1.partner = bf16[128,1024]{1,0:T(8,128)(2,1)S(1)} collective-permute-done((bf16[128,1024]{1,0:T(8,128)(2,1)S(1)}, bf16[128,1024]{1,0:T(8,128)(2,1)S(1)}, u32[]{:S(2)}, u32[]{:S(2)}) %collective-permute-start.1) | collective-permute-done | bytes 262176 | tf_op jit(solution)/shard_map/ppermute | solution.py:267
  61.4 3.2 %place.1 = f32[128,4096]{1,0:T(8,128)} custom-call(f32[128,1024]{1,0:T(8,128)S(1)} %make_tiles.3.own, bf16[128,1024]{1,0:T(8,128)(2,1)S(1)} %collective-permute-done.1.partner, bf16[128,1024]{1,0:T(8,128)(2,1)S(1)} %collective-permute-done.4.before, bf16[128,1024]{1,0:T(8,128)(2,1)S(1)} %collective-permute-done.5.before_partner), custom_call_target="tpu_custom_call" | custom-call | tf_op jit(solution)/shard_map/place/pallas_call | solution.py:226
Async XLA Ops:
  1.3 1.0 %copy-start = (s32[65536]{0:T(1024)S(1)}, s32[65536]{0:T(1024)}, u32[]{:S(2)}) copy-start(s32[65536]{0:T(1024)} %param.10) | copy-start | bytes 786436
  2.2 0.9 %copy-start.1 = (s32[65536]{0:T(1024)S(1)}, s32[65536]{0:T(1024)}, u32[]{:S(2)}) copy-start(s32[65536]{0:T(1024)} %param.11) | copy-start | bytes 786436
  3.2 0.9 %copy-start.2 = (bf16[1,4,128,128]{3,2,1,0:T(8,128)(2,1)S(1)}, bf16[1,4,128,128]{3,2,1,0:T(8,128)(2,1)}, u32[]{:S(2)}) copy-start(bf16[1,4,128,128]{3,2,1,0:T(8,128)(2,1)} %prints.1) | copy-start | bytes 393220
  4.1 0.7 %copy-start.3 = (s32[1,4]{1,0:T(1,128)S(1)}, s32[1,4]{1,0:T(1,128)}, u32[]{:S(2)}) copy-start(s32[1,4]{1,0:T(1,128)} %times.1) | copy-start | bytes 52
  4.7 0.7 %copy-start.4 = (s32[1,4]{1,0:T(1,128)S(1)}, s32[1,4]{1,0:T(1,128)}, u32[]{:S(2)}) copy-start(s32[1,4]{1,0:T(1,128)} %cells.1) | copy-start | bytes 52
  7.3 22.6 %all-to-all-start = ((bf16[8,144,512]{2,1,0:T(8,128)(2,1)}), bf16[8,144,512]{2,1,0:T(8,128)(2,1)S(1)}, u32[]{:S(2)}, u32[]{:S(2)}) async-start(bf16[8,144,512]{2,1,0:T(8,128)(2,1)} %get-tuple-element.7), calls=%async_computation | async-start | bytes 2359296 | tf_op jit(solution)/shard_map/all_to_all | solution.py:258
  12.7 9.1 %collective-permute-start.2 = (bf16[1,144,512]{2,1,0:T(8,128)(2,1)S(1)}, bf16[1,144,512]{2,1,0:T(8,128)(2,1)S(1)}, u32[]{:S(2)}, u32[]{:S(2)}) collective-permute-start(bf16[1,144,512]{2,1,0:T(8,128)(2,1)S(1)} %get-tuple-element.6.refs_0_.block), channel_id=1, source_target_pairs={{16,3},{17,2},{18,1},{19,0},{20,7},{21,6},{22,5},{23,4},{24,11},{2... | collective-permute-start | bytes 442376 | tf_op jit(solution)/shard_map/ppermute | solution.py:261
  16.4 6.0 %collective-permute-start.3 = (bf16[1,144,512]{2,1,0:T(8,128)(2,1)S(1)}, bf16[1,144,512]{2,1,0:T(8,128)(2,1)S(1)}, u32[]{:S(2)}, u32[]{:S(2)}) collective-permute-start(bf16[1,144,512]{2,1,0:T(8,128)(2,1)S(1)} %get-tuple-element.6.refs_0_.block), channel_id=1, source_target_pairs={{16,0},{17,1},{18,2},{19,3},{20,4},{21,5},{22,6},{23,7},{24,8},{25... | collective-permute-start | bytes 442376 | tf_op jit(solution)/shard_map/ppermute | solution.py:260
  19.7 26.6 %collective-permute-start = (bf16[1,144,512]{2,1,0:T(8,128)(2,1)S(1)}, bf16[1,144,512]{2,1,0:T(8,128)(2,1)S(1)}, u32[]{:S(2)}, u32[]{:S(2)}) collective-permute-start(bf16[1,144,512]{2,1,0:T(8,128)(2,1)S(1)} %get-tuple-element.6.refs_0_.block), channel_id=1, source_target_pairs={{0,3},{1,2},{2,1},{3,0},{4,7},{5,6},{6,5},{7,4},{8,11},{9,10},{10,... | collective-permute-start | bytes 442376 | tf_op jit(solution)/shard_map/ppermute | solution.py:259
  37.5 21.3 %collective-permute-start.4 = (bf16[128,1024]{1,0:T(8,128)(2,1)S(1)}, bf16[128,1024]{1,0:T(8,128)(2,1)S(1)}, u32[]{:S(2)}, u32[]{:S(2)}) collective-permute-start(bf16[128,1024]{1,0:T(8,128)(2,1)S(1)} %get-tuple-element.8), channel_id=1, source_target_pairs={{0,16},{1,17},{2,18},{3,19},{4,20},{5,21},{6,22},{7,23},{8,24},{9,... | collective-permute-start | bytes 786440 | tf_op jit(solution)/shard_map/ppermute | solution.py:265
  39.4 19.4 %collective-permute-start.5 = (bf16[128,1024]{1,0:T(8,128)(2,1)S(1)}, bf16[128,1024]{1,0:T(8,128)(2,1)S(1)}, u32[]{:S(2)}, u32[]{:S(2)}) collective-permute-start(bf16[128,1024]{1,0:T(8,128)(2,1)S(1)} %get-tuple-element.9), channel_id=1, source_target_pairs={{0,19},{1,18},{2,17},{3,16},{4,23},{5,22},{6,21},{7,20},{8,27},{9,... | collective-permute-start | bytes 786440 | tf_op jit(solution)/shard_map/ppermute | solution.py:264
  50.3 11.2 %collective-permute-start.1 = (bf16[128,1024]{1,0:T(8,128)(2,1)S(1)}, bf16[128,1024]{1,0:T(8,128)(2,1)S(1)}, u32[]{:S(2)}, u32[]{:S(2)}) collective-permute-start(bf16[128,1024]{1,0:T(8,128)(2,1)S(1)} %make_tiles.4), channel_id=1, source_target_pairs={{0,3},{1,2},{2,1},{3,0},{4,7},{5,6},{6,5},{7,4},{8,11},{9,10},{10,... | collective-permute-start | bytes 786440 | tf_op jit(solution)/shard_map/ppermute | solution.py:267

commit v3 on v2

v3 whole, which is shorter than its diff:
```python
import functools
import math

import jax
import jax.numpy as jnp
from jax import lax
from jax.experimental import pallas as pl
from jax.experimental.pallas import tpu as pltpu
from jax.sharding import PartitionSpec as P

BLOCK = 128
SLOTS = 4
WIDE = SLOTS * BLOCK
PATTERN = 16
ROWS = BLOCK + PATTERN
PARTS = 3
DEPTH = PARTS * PATTERN
ONE_ROW = 9
TIME_ROW = 10
LIVE_ROW = 11
CHUNK = 2 * BLOCK
TSTEP = 8
CORR = 0.6
SCALE = (math.log2(math.e) / CORR) ** 2
DECAY = math.log2(math.e) / TSTEP
TINY = 1e-12
RADIANS = math.pi / 180.0
SIDE = 4
PAIR = 2


def rounded(x):
    return x.astype(jnp.bfloat16).astype(jnp.float32)


def split3(x):
    high = rounded(x)
    mid = rounded(x - high)
    return high, mid, rounded(x - high - mid)


def block_kernel(count, prints, times, cells, live, lat_ref, lon_ref, block, payload, own, when, where, alive, lat_row, lon_row, pattern, sems, row_sems):
    loads = [
        pltpu.make_async_copy(source, target, sems.at[i])
        for i, (source, target) in enumerate(((cells, where), (times, when), (live, alive), (prints, own)))
    ]
    for load in loads:
        load.start()
    loads[0].wait()
    copies = []
    for j in range(SLOTS):
        for source, target, sem in ((lat_ref, lat_row, 0), (lon_ref, lon_row, 1)):
            copy = pltpu.make_async_copy(source.at[where[0, j]], target.at[j], row_sems.at[sem, j])
            copy.start()
            copies.append(copy)
    for load in loads[1:]:
        load.wait()
    for j in range(SLOTS):
        kept = jnp.where(j < alive[0], own[0, j], jnp.zeros((BLOCK, BLOCK), jnp.bfloat16))
        block[0, 0:BLOCK, j * BLOCK : (j + 1) * BLOCK] = kept
    base = lax.axis_index("tm") * TSTEP
    pattern[...] = jnp.zeros_like(pattern)
    pattern[pl.ds(ONE_ROW, 1), :] = jnp.ones((1, WIDE), jnp.float32)
    pattern[pl.ds(LIVE_ROW, 1), :] = jnp.full((1, WIDE), alive[0].astype(jnp.float32))
    for j in range(SLOTS):
        moment = (base + when[0, j]).astype(jnp.float32)
        pattern[pl.ds(TIME_ROW, 1), j * BLOCK : (j + 1) * BLOCK] = jnp.full((1, BLOCK), moment)
    for copy in copies:
        copy.wait()
    lat = jnp.concatenate([lat_row[j] for j in range(SLOTS)], axis=1).astype(jnp.float32)
    lon = jnp.concatenate([lon_row[j] for j in range(SLOTS)], axis=1).astype(jnp.float32)
    latitude = (lat - 89.5) * RADIANS
    longitude = (lon + 0.5) * RADIANS
    across = jnp.cos(latitude)
    units = (across * jnp.cos(longitude), across * jnp.sin(longitude), jnp.sin(latitude))
    for c, unit in enumerate(units):
        for part, value in enumerate(split3(unit)):
            pattern[pl.ds(PARTS * c + part, 1), :] = value
    block[0, BLOCK:ROWS, :] = pattern[...].astype(jnp.bfloat16)
    for i in range(count):
        payload[i] = block[0]


def make_block(footprints, times, cells, live, lat, lon, count):
    vmem = pl.BlockSpec(memory_space=pltpu.VMEM)
    hbm = pl.BlockSpec(memory_space=pltpu.HBM)
    return pl.pallas_call(
        functools.partial(block_kernel, count),
        out_shape=(
            jax.ShapeDtypeStruct((1, ROWS, WIDE), jnp.bfloat16),
            jax.ShapeDtypeStruct((count, ROWS, WIDE), jnp.bfloat16),
        ),
        in_specs=[hbm] * 6,
        out_specs=(vmem, vmem),
        scratch_shapes=[
            pltpu.VMEM((1, SLOTS, BLOCK, BLOCK), jnp.bfloat16),
            pltpu.SMEM((1, SLOTS), jnp.int32),
            pltpu.SMEM((1, SLOTS), jnp.int32),
            pltpu.SMEM((1,), jnp.int32),
            pltpu.VMEM((SLOTS, 1, BLOCK), jnp.int32),
            pltpu.VMEM((SLOTS, 1, BLOCK), jnp.int32),
            pltpu.VMEM((PATTERN, WIDE), jnp.float32),
            pltpu.SemaphoreType.DMA((4,)),
            pltpu.SemaphoreType.DMA((2, SLOTS)),
        ],
        compiler_params=pltpu.CompilerParams(vmem_limit_bytes=60 * 2**20),
        name="make_block",
    )(footprints, times, cells, live, lat, lon)


def prepare_near(block, near_rows):
    pattern = block[0, BLOCK:ROWS, :].astype(jnp.float32)
    near_rows[...] = jnp.zeros_like(near_rows)
    for c in range(3):
        high, mid, low = (pattern[PARTS * c + part : PARTS * c + part + 1] for part in range(PARTS))
        scaled = split3((high + mid + low) * (-2.0 * SCALE))
        for segment, value in enumerate(scaled):
            for part in range(PARTS - segment):
                near_rows[pl.ds(segment * PATTERN + PARTS * c + part, 1), :] = value
    ends = split3(jnp.full((1, WIDE), 2.0 * SCALE, jnp.float32))
    for segment, value in enumerate(ends):
        near_rows[pl.ds(segment * PATTERN + ONE_ROW, 1), :] = value
    near_rows[pl.ds(TIME_ROW, 1), :] = jnp.zeros((1, WIDE), jnp.float32)
    return near_rows[...].T.astype(jnp.bfloat16), pattern[TIME_ROW : TIME_ROW + 1]


def weigh(near_vec, near_time, far_pattern, weights, live):
    columns = far_pattern.shape[1]
    far_vec = jnp.concatenate([far_pattern] * PARTS, axis=0)
    far_time = far_pattern.astype(jnp.float32)[TIME_ROW : TIME_ROW + 1]
    for k in range(live):
        rows = pl.ds(k * BLOCK, BLOCK)
        own = jnp.concatenate([near_time[:, k * BLOCK : (k + 1) * BLOCK]] * (columns // BLOCK), axis=1)
        lag = jnp.abs(own - far_time) * (-DECAY)
        square = jnp.maximum(jnp.dot(near_vec[rows, :], far_vec, preferred_element_type=jnp.float32), TINY)
        weights[rows, :] = jnp.exp2(lag - square * lax.rsqrt(square)).astype(jnp.bfloat16)


def self_kernel(block, out, near_rows, near_vec, weights):
    near_vec[...], when = prepare_near(block, near_rows)
    weigh(near_vec, when, block[0, BLOCK:ROWS, :], weights, SLOTS)
    gain = jnp.dot(block[0, 0:BLOCK, :], weights[...], preferred_element_type=jnp.float32)
    for j in range(SLOTS):
        out[0, j] = gain[:, j * BLOCK : (j + 1) * BLOCK]


def self_gain(block):
    return pl.pallas_call(
        self_kernel,
        out_shape=jax.ShapeDtypeStruct((1, SLOTS, BLOCK, BLOCK), jnp.float32),
        in_specs=[pl.BlockSpec(memory_space=pltpu.VMEM)],
        out_specs=pl.BlockSpec(memory_space=pltpu.VMEM),
        scratch_shapes=[
            pltpu.VMEM((DEPTH, WIDE), jnp.float32),
            pltpu.VMEM((WIDE, DEPTH), jnp.bfloat16),
            pltpu.VMEM((WIDE, WIDE), jnp.bfloat16),
        ],
        compiler_params=pltpu.CompilerParams(vmem_limit_bytes=12 * 2**20),
        cost_estimate=pl.CostEstimate(flops=2 * 10**9, bytes_accessed=10**6, transcendentals=2**19),
        name="self_gain",
    )(block)


def live_of(pattern):
    count = pattern[:, 0:BLOCK].astype(jnp.float32)[LIVE_ROW : LIVE_ROW + 1]
    return jnp.max(count).astype(jnp.int32)


def columns_at(start, width):
    return pl.ds(pl.multiple_of(start, BLOCK), width)


def tiles_kernel(count, *refs):
    blocks, far, outs = refs[:count], refs[count], refs[count + 1 : 2 * count + 1]
    near_rows, near_vec, near_time, cats, far_pattern, gain, tiles, weights = refs[2 * count + 1 :]
    n_far = far.shape[0]
    near_live = []
    for s in range(count):
        vec, when = prepare_near(blocks[s], near_rows)
        near_vec[s] = vec
        near_time[s] = jnp.broadcast_to(when, near_time.shape[1:])
        cats[s] = blocks[s][0, 0:BLOCK, :]
        near_live.append(live_of(blocks[s][0, BLOCK:ROWS, :]))
    starts, filled = [], jnp.int32(0)
    for r in range(n_far):
        pattern = far[r, BLOCK:ROWS, :]
        far_pattern[:, columns_at(filled * BLOCK, WIDE)] = pattern
        starts.append(filled * BLOCK)
        filled = filled + live_of(pattern)
    far_pattern[:, columns_at(filled * BLOCK, WIDE)] = jnp.zeros((PATTERN, WIDE), jnp.bfloat16)
    turns = (filled * BLOCK + 2 * CHUNK - 1) // (2 * CHUNK)
    gain[:, columns_at(turns * 2 * CHUNK, WIDE)] = jnp.zeros((BLOCK, WIDE), jnp.bfloat16)

    def one_near(s, carry):
        live = near_live[0]
        for other in range(1, count):
            live = jnp.where(s == other, near_live[other], live)

        def weigh_chunk(start, slot, used):
            weigh(
                near_vec.at[s], near_time[s, 0:1, :], far_pattern[:, columns_at(start, CHUNK)], weights.at[slot], used
            )

        def gain_chunk(start, slot, used):
            depth = used * BLOCK
            part = jnp.dot(cats[s, :, 0:depth], weights[slot, 0:depth, :], preferred_element_type=jnp.float32)
            gain[:, columns_at(start, CHUNK)] = part.astype(jnp.bfloat16)

        for used in range(1, SLOTS + 1):

            @pl.when(live == used)
            def _(used=used):
                def turn(i, carry):
                    start = i * 2 * CHUNK
                    weigh_chunk(start, 0, used)
                    gain_chunk(jnp.maximum(start - CHUNK, 0), 1, used)
                    weigh_chunk(start + CHUNK, 1, used)
                    gain_chunk(start, 0, used)
                    return carry

                lax.fori_loop(0, turns, turn, 0)
                gain_chunk(turns * 2 * CHUNK - CHUNK, 1, used)

        for r in range(n_far):
            tiles[s * n_far + r] = lax.dot_general(
                gain[:, columns_at(starts[r], WIDE)],
                far[r, 0:BLOCK, :],
                (((1,), (1,)), ((), ())),
                preferred_element_type=jnp.float32,
            ).astype(tiles.dtype)
        return carry

    lax.fori_loop(0, count, one_near, 0)
    for u in range(count * n_far):
        s, r = u // n_far, u % n_far
        outs[s][:, r * BLOCK : (r + 1) * BLOCK] = tiles[u]


def make_tiles(blocks, far, dtype):
    count, n_far = len(blocks), far.shape[0]
    vmem = pl.BlockSpec(memory_space=pltpu.VMEM)
    shape = jax.ShapeDtypeStruct((BLOCK, n_far * BLOCK), dtype)
    return pl.pallas_call(
        functools.partial(tiles_kernel, count),
        out_shape=(shape,) * count,
        in_specs=[vmem] * (count + 1),
        out_specs=(vmem,) * count,
        scratch_shapes=[
            pltpu.VMEM((DEPTH, WIDE), jnp.float32),
            pltpu.VMEM((count, WIDE, DEPTH), jnp.bfloat16),
            pltpu.VMEM((count, 8, WIDE), jnp.float32),
            pltpu.VMEM((count, BLOCK, WIDE), jnp.bfloat16),
            pltpu.VMEM((PATTERN, (n_far + 1) * WIDE), jnp.bfloat16),
            pltpu.VMEM((BLOCK, (n_far + 1) * WIDE), jnp.bfloat16),
            pltpu.VMEM((count * n_far, BLOCK, BLOCK), dtype),
            pltpu.VMEM((2, WIDE, CHUNK), jnp.bfloat16),
        ],
        compiler_params=pltpu.CompilerParams(vmem_limit_bytes=16 * 2**20),
        cost_estimate=pl.CostEstimate(
            flops=count * 10**9, bytes_accessed=count * 2 * 10**6, transcendentals=count * 2**22
        ),
        name="make_tiles",
    )(*blocks, far)


def pair_start(x, odd):
    return jnp.where(odd, lax.rem((x + 3) // PAIR * PAIR + 1, SIDE), x // PAIR * PAIR)


def spread(source, out, base, start, sems):
    copies = []
    for y in range(SIDE):
        for i in range(PAIR):
            column = base + (y * SIDE + lax.rem(start + i, SIDE)) * BLOCK
            u = y * PAIR + i
            copies.append(
                pltpu.make_async_copy(
                    source.at[:, u * BLOCK : (u + 1) * BLOCK], out.at[:, columns_at(column, BLOCK)], sems.at[u]
                )
            )
    return copies


def place_most_kernel(own, before, before_partner, out, wide, wide_partner, sems):
    x = lax.rem(lax.axis_index("obs"), SIDE)
    odd = lax.rem(lax.axis_index("tm"), 2) == 1
    width = own.shape[1]
    earlier = pair_start(x, jnp.logical_not(odd))
    copies = spread(own, out, 2 * width, pair_start(x, odd), sems.at[0])
    for copy in copies:
        copy.start()
    wide[...] = before[...].astype(jnp.float32)
    more = spread(wide, out, 0, earlier, sems.at[1])
    for copy in more:
        copy.start()
    wide_partner[...] = before_partner[...].astype(jnp.float32)
    last = spread(wide_partner, out, 0, earlier + PAIR, sems.at[2])
    for copy in last:
        copy.start()
    for copy in copies + more + last:
        copy.wait()


def place_most(own, before, before_partner):
    vmem = pl.BlockSpec(memory_space=pltpu.VMEM)
    return pl.pallas_call(
        place_most_kernel,
        out_shape=jax.ShapeDtypeStruct((BLOCK, 4 * own.shape[1]), jnp.float32),
        in_specs=[vmem] * 3,
        out_specs=pl.BlockSpec(memory_space=pltpu.HBM),
        scratch_shapes=[
            pltpu.VMEM(own.shape, jnp.float32),
            pltpu.VMEM(own.shape, jnp.float32),
            pltpu.SemaphoreType.DMA((3, SIDE * PAIR)),
        ],
        compiler_params=pltpu.CompilerParams(vmem_limit_bytes=12 * 2**20),
        cost_estimate=pl.CostEstimate(flops=10**9, bytes_accessed=4 * 10**6, transcendentals=0),
        name="place_most",
    )(own, before, before_partner)


def place_rest_kernel(partner, filled, out, wide, sems):
    del filled
    x = lax.rem(lax.axis_index("obs"), SIDE)
    odd = lax.rem(lax.axis_index("tm"), 2) == 1
    wide[...] = partner[...].astype(jnp.float32)
    copies = spread(wide, out, 2 * wide.shape[1], pair_start(x, odd) + PAIR, sems)
    for copy in copies:
        copy.start()
    for copy in copies:
        copy.wait()


def place_rest(partner, filled):
    hbm = pl.BlockSpec(memory_space=pltpu.HBM)
    return pl.pallas_call(
        place_rest_kernel,
        out_shape=jax.ShapeDtypeStruct(filled.shape, filled.dtype),
        in_specs=[pl.BlockSpec(memory_space=pltpu.VMEM), hbm],
        out_specs=hbm,
        input_output_aliases={1: 0},
        scratch_shapes=[pltpu.VMEM(partner.shape, jnp.float32), pltpu.SemaphoreType.DMA((SIDE * PAIR,))],
        compiler_params=pltpu.CompilerParams(vmem_limit_bytes=12 * 2**20),
        name="place_rest",
    )(partner, filled)


def on_device(footprints, block_times, block_cells, live_counts, cell_lat, cell_lon):
    group = lax.axis_size("obs")
    spans = lax.axis_size("tm")
    axes = ("tm", "obs")
    sides = ((0, 1), (2, 3)), ((1, 2), (3, 0))
    near_by = [
        [t * group + y * SIDE + x for y in range(group // SIDE) for x in pair]
        for t in range(spans)
        for pair in sides[t % 2]
    ]

    def across(t, o):
        x = o % SIDE
        return o - x + (x ^ 1 if t % 2 else SIDE - 1 - x)

    def steps(by, crossing):
        pairs = []
        for t in range(spans):
            if 0 <= t + by < spans:
                for o in range(group):
                    other = across(min(t, t + by), o) if crossing else o
                    pairs.append((t * group + o, (t + by) * group + other))
        return pairs

    lat = cell_lat.reshape(-1, 1, BLOCK)
    lon = cell_lon.reshape(-1, 1, BLOCK)
    block, payload = make_block(
        footprints, block_times, block_cells, live_counts, lat, lon, group // (SIDE // PAIR)
    )
    far = lax.all_to_all(payload, axes, 0, 0, tiled=True, axis_index_groups=near_by)
    partner_block = lax.ppermute(block, axes, steps(0, True))
    next_block = lax.ppermute(block, axes, steps(-1, False))
    next_partner_block = lax.ppermute(block, axes, steps(-1, True))
    footprint_cov = self_gain(block)
    far, footprint_cov = lax.optimization_barrier((far, footprint_cov))
    (next_partner_tiles,) = make_tiles((next_partner_block,), far, jnp.bfloat16)
    before_partner = lax.ppermute(next_partner_tiles, axes, steps(1, True))
    (partner_tiles,) = make_tiles((partner_block,), far, jnp.bfloat16)
    partner = lax.ppermute(partner_tiles, axes, steps(0, True))
    (next_tiles,) = make_tiles((next_block,), far, jnp.bfloat16)
    before = lax.ppermute(next_tiles, axes, steps(1, False))
    (own,) = make_tiles((block,), far, jnp.float32)
    cross_cov = place_rest(partner, place_most(own, before, before_partner))
    return (cross_cov, footprint_cov)


def solution(mesh):
    placed = (
        P(("tm", "obs"), None, None, None),
        P(("tm", "obs"), None),
        P(("tm", "obs"), None),
        P(("tm", "obs")),
        P(),
        P(),
    )
    return jax.shard_map(
        on_device,
        mesh=mesh,
        in_specs=placed,
        out_specs=(P(("tm", "obs"), None), P(("tm", "obs"), None, None, None)),
        check_vma=False,
    )
```

time: 65 us -> 55.5 us (0.85)
  the two profiles are of different devices: /device:TPU:96 before, /device:TPU:134 now
where the time goes in v3:
time: 55.5 us; the launch traced here: 55.2 us
  starting transfers between devices  24.5 us (44%)
  Pallas kernels  22.1 us (40%)
  waiting for transfers between devices  7.22 us (13%)
  between operations  1.4 us (3%)
    pallas_call x4, Pallas kernels, make_tiles(): pl.pallas_call(functools.partial(tiles_kernel, count), out_shape=(shape,)...  15.5 us
    all_to_all x1, starting transfers between devices, on_device(): lax.all_to_all(payload, axes, 0, 0, tiled=True, axis_index_groups=near_by)  6.07 us
    ppermute x1, starting transfers between devices, on_device(): before_partner = lax.ppermute(next_partner_tiles, axes, steps(1, True))  5.82 us
    ppermute x1, starting transfers between devices, on_device(): partner_block = lax.ppermute(block, axes, steps(0, True))  4.95 us
    all_to_all x1, waiting for transfers between devices, on_device(): lax.all_to_all(payload, axes, 0, 0, tiled=True, axis_index_groups=near_by)  4.82 us
    pallas_call x1, Pallas kernels, make_block(): pl.pallas_call(functools.partial(block_kernel, count), out_shape=(jax.Sha...  2.83 us
    ppermute x1, waiting for transfers between devices, on_device(): partner = lax.ppermute(partner_tiles, axes, steps(0, True))  2.39 us
    ppermute x1, starting transfers between devices, on_device(): partner = lax.ppermute(partner_tiles, axes, steps(0, True))  1.92 us
  transfers between devices with their start and end apart: 7, of which 2 were waited for; matrix products, arithmetic and copies ran while one was open for 0% of the time, Pallas kernels for 33%

profile of v3, /device:TPU:134, one launch (start us, length us, event | category | flops | bytes accessed | tf_op | source)
XLA Modules:
  0.0 55.2 jit_solution(11207442442866255827)
XLA Ops:
  1.3 2.8 %make_block.1 = (bf16[1,144,512]{2,1,0:T(8,128)(2,1)}, bf16[8,144,512]{2,1,0:T(8,128)(2,1)}) custom-call(bf16[1,4,128,128]{3,2,1,0:T(8,128)(2,1)} %prints.1, s32[1,4]{1,0:T(1,128)} %times.1, s32[1,4]{1,0:T(1,128)} %cells.1, s32[1]{0:T(128)S(6)} %copy.10.live, s32[512,1,128]{2,1,0:T(1,128)} %bitcast.2, s32[512,1,128]{2,1,0:T(1,128)} %bitcast.3), custom_call_target="tpu_custom_call" | custom-call | tf_op jit(solution)/shard_map/make_block/pallas_call | solution.py:87
  4.1 0.0 copy-start
  4.1 6.1 %all-to-all-start = ((bf16[8,144,512]{2,1,0:T(8,128)(2,1)}), bf16[8,144,512]{2,1,0:T(8,128)(2,1)S(1)}, u32[]{:S(2)}, u32[]{:S(2)}) async-start(bf16[8,144,512]{2,1,0:T(8,128)(2,1)} %get-tuple-element.7), calls=%async_computation | async-start | bytes 2359296 | tf_op jit(solution)/shard_map/all_to_all | solution.py:377
  10.2 0.0 copy-done
  10.2 1.9 %collective-permute-start.4 = (bf16[1,144,512]{2,1,0:T(8,128)(2,1)S(1)}, bf16[1,144,512]{2,1,0:T(8,128)(2,1)S(1)}, u32[]{:S(2)}, u32[]{:S(2)}) collective-permute-start(bf16[1,144,512]{2,1,0:T(8,128)(2,1)S(1)} %copy-done), channel_id=1, source_target_pairs={{16,3},{17,2},{18,1},{19,0},{20,7},{21,6},{22,5},{23,4},{24,11},{2... | collective-permute-start | bytes 442376 | tf_op jit(solution)/shard_map/ppermute | solution.py:380
  12.1 1.9 %collective-permute-start.2 = (bf16[1,144,512]{2,1,0:T(8,128)(2,1)S(1)}, bf16[1,144,512]{2,1,0:T(8,128)(2,1)S(1)}, u32[]{:S(2)}, u32[]{:S(2)}) collective-permute-start(bf16[1,144,512]{2,1,0:T(8,128)(2,1)S(1)} %copy-done), channel_id=1, source_target_pairs={{16,0},{17,1},{18,2},{19,3},{20,4},{21,5},{22,6},{23,7},{24,8},{25... | collective-permute-start | bytes 442376 | tf_op jit(solution)/shard_map/ppermute | solution.py:379
  14.0 4.9 %collective-permute-start = (bf16[1,144,512]{2,1,0:T(8,128)(2,1)S(1)}, bf16[1,144,512]{2,1,0:T(8,128)(2,1)S(1)}, u32[]{:S(2)}, u32[]{:S(2)}) collective-permute-start(bf16[1,144,512]{2,1,0:T(8,128)(2,1)S(1)} %copy-done), channel_id=1, source_target_pairs={{0,3},{1,2},{2,1},{3,0},{4,7},{5,6},{6,5},{7,4},{8,11},{9,10},{10,... | collective-permute-start | bytes 442376 | tf_op jit(solution)/shard_map/ppermute | solution.py:378
  19.0 1.4 %self_gain.1 = f32[1,4,128,128]{3,2,1,0:T(8,128)} custom-call(bf16[1,144,512]{2,1,0:T(8,128)(2,1)S(1)} %copy-done), custom_call_target="tpu_custom_call" | custom-call | flops 2000000000 | bytes 1000000 | tf_op jit(solution)/shard_map/self_gain/pallas_call | solution.py:148
  20.4 4.8 %all-to-all-done.refs_1_ = bf16[8,144,512]{2,1,0:T(8,128)(2,1)S(1)} async-done(((bf16[8,144,512]{2,1,0:T(8,128)(2,1)}), bf16[8,144,512]{2,1,0:T(8,128)(2,1)S(1)}, u32[]{:S(2)}, u32[]{:S(2)}) %all-to-all-start) | async-done | bytes 1179680 | tf_op jit(solution)/shard_map/all_to_all | solution.py:377
  25.2 0.0 collective-permute-done.2.refs_0_
  25.2 4.0 %make_tiles.6 = bf16[128,1024]{1,0:T(8,128)(2,1)S(1)} custom-call(bf16[1,144,512]{2,1,0:T(8,128)(2,1)S(1)} %collective-permute-done.2.refs_0_, bf16[8,144,512]{2,1,0:T(8,128)(2,1)S(1)} %all-to-all-done.refs_1_), custom_call_target="tpu_custom_call" | custom-call | flops 1000000000 | bytes 2000000 | tf_op jit(solution)/shard_map/make_tiles/pallas_call | solution.py:243
  29.2 1.9 %collective-permute-start.3 = (bf16[128,1024]{1,0:T(8,128)(2,1)S(1)}, bf16[128,1024]{1,0:T(8,128)(2,1)S(1)}, u32[]{:S(2)}, u32[]{:S(2)}) collective-permute-start(bf16[128,1024]{1,0:T(8,128)(2,1)S(1)} %make_tiles.6), channel_id=1, source_target_pairs={{0,16},{1,17},{2,18},{3,19},{4,20},{5,21},{6,22},{7,23},{8,24},{9,... | collective-permute-start | bytes 786440 | tf_op jit(solution)/shard_map/ppermute | solution.py:388
  31.2 0.0 collective-permute-done.4.refs_0_
  31.2 4.0 %make_tiles.7 = bf16[128,1024]{1,0:T(8,128)(2,1)S(1)} custom-call(bf16[1,144,512]{2,1,0:T(8,128)(2,1)S(1)} %collective-permute-done.4.refs_0_, bf16[8,144,512]{2,1,0:T(8,128)(2,1)S(1)} %all-to-all-done.refs_1_), custom_call_target="tpu_custom_call" | custom-call | flops 1000000000 | bytes 2000000 | tf_op jit(solution)/shard_map/make_tiles/pallas_call | solution.py:243
  35.2 5.8 %collective-permute-start.5 = (bf16[128,1024]{1,0:T(8,128)(2,1)S(1)}, bf16[128,1024]{1,0:T(8,128)(2,1)S(1)}, u32[]{:S(2)}, u32[]{:S(2)}) collective-permute-start(bf16[128,1024]{1,0:T(8,128)(2,1)S(1)} %make_tiles.7), channel_id=1, source_target_pairs={{0,19},{1,18},{2,17},{3,16},{4,23},{5,22},{6,21},{7,20},{8,27},{9,... | collective-permute-start | bytes 786440 | tf_op jit(solution)/shard_map/ppermute | solution.py:384
  41.0 0.0 collective-permute-done.refs_0_
  41.0 3.8 %make_tiles.4 = bf16[128,1024]{1,0:T(8,128)(2,1)S(1)} custom-call(bf16[1,144,512]{2,1,0:T(8,128)(2,1)S(1)} %collective-permute-done.refs_0_, bf16[8,144,512]{2,1,0:T(8,128)(2,1)S(1)} %all-to-all-done.refs_1_), custom_call_target="tpu_custom_call" | custom-call | flops 1000000000 | bytes 2000000 | tf_op jit(solution)/shard_map/make_tiles/pallas_call | solution.py:243
  44.8 1.9 %collective-permute-start.1 = (bf16[128,1024]{1,0:T(8,128)(2,1)S(1)}, bf16[128,1024]{1,0:T(8,128)(2,1)S(1)}, u32[]{:S(2)}, u32[]{:S(2)}) collective-permute-start(bf16[128,1024]{1,0:T(8,128)(2,1)S(1)} %make_tiles.4), channel_id=1, source_target_pairs={{0,3},{1,2},{2,1},{3,0},{4,7},{5,6},{6,5},{7,4},{8,11},{9,10},{10,... | collective-permute-start | bytes 786440 | tf_op jit(solution)/shard_map/ppermute | solution.py:386
  46.8 3.7 %make_tiles.5.own = f32[128,1024]{1,0:T(8,128)S(1)} custom-call(bf16[1,144,512]{2,1,0:T(8,128)(2,1)S(1)} %copy-done, bf16[8,144,512]{2,1,0:T(8,128)(2,1)S(1)} %all-to-all-done.refs_1_), custom_call_target="tpu_custom_call" | custom-call | flops 1000000000 | bytes 2000000 | tf_op jit(solution)/shard_map/make_tiles/pallas_call | solution.py:243
  50.5 0.0 collective-permute-done.3.before
  50.5 0.0 collective-permute-done.5.before_partner
  50.5 1.4 %place_most.1.filled = f32[128,4096]{1,0:T(8,128)} custom-call(f32[128,1024]{1,0:T(8,128)S(1)} %make_tiles.5.own, bf16[128,1024]{1,0:T(8,128)(2,1)S(1)} %collective-permute-done.3.before, bf16[128,1024]{1,0:T(8,128)(2,1)S(1)} %collective-permute-done.5.before_partner), custom_call_target="tpu_custom_call" | custom-call | flops 1000000000 | bytes 4000000 | tf_op jit(solution)/shard_map/place_most/pallas_call | solution.py:306
  51.9 2.4 %collective-permute-done.1.partner = bf16[128,1024]{1,0:T(8,128)(2,1)S(1)} collective-permute-done((bf16[128,1024]{1,0:T(8,128)(2,1)S(1)}, bf16[128,1024]{1,0:T(8,128)(2,1)S(1)}, u32[]{:S(2)}, u32[]{:S(2)}) %collective-permute-start.1) | collective-permute-done | bytes 262176 | tf_op jit(solution)/shard_map/ppermute | solution.py:386
  54.3 0.9 %place_rest.1 = f32[128,4096]{1,0:T(8,128)} custom-call(bf16[128,1024]{1,0:T(8,128)(2,1)S(1)} %collective-permute-done.1.partner, f32[128,4096]{1,0:T(8,128)} %place_most.1.filled), custom_call_target="tpu_custom_call", output_to_operand_aliasing={{}: (1, {})} | custom-call | tf_op jit(solution)/shard_map/place_rest/pallas_call | solution.py:336
Async XLA Ops:
  4.1 6.1 %copy-start = (bf16[1,144,512]{2,1,0:T(8,128)(2,1)S(1)}, bf16[1,144,512]{2,1,0:T(8,128)(2,1)}, u32[]{:S(2)}) copy-start(bf16[1,144,512]{2,1,0:T(8,128)(2,1)} %get-tuple-element.6.block.refs_0_) | copy-start | bytes 442372
  4.1 21.1 %all-to-all-start = ((bf16[8,144,512]{2,1,0:T(8,128)(2,1)}), bf16[8,144,512]{2,1,0:T(8,128)(2,1)S(1)}, u32[]{:S(2)}, u32[]{:S(2)}) async-start(bf16[8,144,512]{2,1,0:T(8,128)(2,1)} %get-tuple-element.7), calls=%async_computation | async-start | bytes 2359296 | tf_op jit(solution)/shard_map/all_to_all | solution.py:377
  10.2 21.0 %collective-permute-start.4 = (bf16[1,144,512]{2,1,0:T(8,128)(2,1)S(1)}, bf16[1,144,512]{2,1,0:T(8,128)(2,1)S(1)}, u32[]{:S(2)}, u32[]{:S(2)}) collective-permute-start(bf16[1,144,512]{2,1,0:T(8,128)(2,1)S(1)} %copy-done), channel_id=1, source_target_pairs={{16,3},{17,2},{18,1},{19,0},{20,7},{21,6},{22,5},{23,4},{24,11},{2... | collective-permute-start | bytes 442376 | tf_op jit(solution)/shard_map/ppermute | solution.py:380
  12.1 13.1 %collective-permute-start.2 = (bf16[1,144,512]{2,1,0:T(8,128)(2,1)S(1)}, bf16[1,144,512]{2,1,0:T(8,128)(2,1)S(1)}, u32[]{:S(2)}, u32[]{:S(2)}) collective-permute-start(bf16[1,144,512]{2,1,0:T(8,128)(2,1)S(1)} %copy-done), channel_id=1, source_target_pairs={{16,0},{17,1},{18,2},{19,3},{20,4},{21,5},{22,6},{23,7},{24,8},{25... | collective-permute-start | bytes 442376 | tf_op jit(solution)/shard_map/ppermute | solution.py:379
  14.0 27.0 %collective-permute-start = (bf16[1,144,512]{2,1,0:T(8,128)(2,1)S(1)}, bf16[1,144,512]{2,1,0:T(8,128)(2,1)S(1)}, u32[]{:S(2)}, u32[]{:S(2)}) collective-permute-start(bf16[1,144,512]{2,1,0:T(8,128)(2,1)S(1)} %copy-done), channel_id=1, source_target_pairs={{0,3},{1,2},{2,1},{3,0},{4,7},{5,6},{6,5},{7,4},{8,11},{9,10},{10,... | collective-permute-start | bytes 442376 | tf_op jit(solution)/shard_map/ppermute | solution.py:378
  29.2 21.3 %collective-permute-start.3 = (bf16[128,1024]{1,0:T(8,128)(2,1)S(1)}, bf16[128,1024]{1,0:T(8,128)(2,1)S(1)}, u32[]{:S(2)}, u32[]{:S(2)}) collective-permute-start(bf16[128,1024]{1,0:T(8,128)(2,1)S(1)} %make_tiles.6), channel_id=1, source_target_pairs={{0,16},{1,17},{2,18},{3,19},{4,20},{5,21},{6,22},{7,23},{8,24},{9,... | collective-permute-start | bytes 786440 | tf_op jit(solution)/shard_map/ppermute | solution.py:388
  35.2 15.3 %collective-permute-start.5 = (bf16[128,1024]{1,0:T(8,128)(2,1)S(1)}, bf16[128,1024]{1,0:T(8,128)(2,1)S(1)}, u32[]{:S(2)}, u32[]{:S(2)}) collective-permute-start(bf16[128,1024]{1,0:T(8,128)(2,1)S(1)} %make_tiles.7), channel_id=1, source_target_pairs={{0,19},{1,18},{2,17},{3,16},{4,23},{5,22},{6,21},{7,20},{8,27},{9,... | collective-permute-start | bytes 786440 | tf_op jit(solution)/shard_map/ppermute | solution.py:384
  44.8 9.5 %collective-permute-start.1 = (bf16[128,1024]{1,0:T(8,128)(2,1)S(1)}, bf16[128,1024]{1,0:T(8,128)(2,1)S(1)}, u32[]{:S(2)}, u32[]{:S(2)}) collective-permute-start(bf16[128,1024]{1,0:T(8,128)(2,1)S(1)} %make_tiles.4), channel_id=1, source_target_pairs={{0,3},{1,2},{2,1},{3,0},{4,7},{5,6},{6,5},{7,4},{8,11},{9,10},{10,... | collective-permute-start | bytes 786440 | tf_op jit(solution)/shard_map/ppermute | solution.py:386

commit v4 on v3

--- a/solution.py
+++ b/solution.py
@@ -18,7 +18,7 @@
 ONE_ROW = 9
 TIME_ROW = 10
 LIVE_ROW = 11
-CHUNK = 2 * BLOCK
+CHUNK = WIDE
 TSTEP = 8
 CORR = 0.6
 SCALE = (math.log2(math.e) / CORR) ** 2
@@ -39,69 +39,83 @@
     return high, mid, rounded(x - high - mid)
 
 
-def block_kernel(count, prints, times, cells, live, lat_ref, lon_ref, block, payload, own, when, where, alive, lat_row, lon_row, pattern, sems, row_sems):
+def block_kernel(
+    prints, times, cells, live, lat_ref, lon_ref, block, payload, own, when, where, alive, lat, lon, cat, rows, pattern, loads_sem, sends_sem
+):
     loads = [
-        pltpu.make_async_copy(source, target, sems.at[i])
-        for i, (source, target) in enumerate(((cells, where), (times, when), (live, alive), (prints, own)))
+        pltpu.make_async_copy(source, target, loads_sem.at[i])
+        for i, (source, target) in enumerate(
+            ((prints, own), (live, alive), (cells, where), (times, when), (lat_ref, lat), (lon_ref, lon))
+        )
     ]
     for load in loads:
         load.start()
+    targets = [payload.at[i] for i in range(payload.shape[0])] + [block.at[0]]
+
+    def send(source, start, size, sem):
+        copies = [
+            pltpu.make_async_copy(source, target.at[pl.ds(start, size), :], sends_sem.at[sem, i])
+            for i, target in enumerate(targets)
+        ]
+        for copy in copies:
+            copy.start()
+        return copies
+
+    base = lax.axis_index("tm") * TSTEP
     loads[0].wait()
-    copies = []
-    for j in range(SLOTS):
-        for source, target, sem in ((lat_ref, lat_row, 0), (lon_ref, lon_row, 1)):
-            copy = pltpu.make_async_copy(source.at[where[0, j]], target.at[j], row_sems.at[sem, j])
-            copy.start()
-            copies.append(copy)
-    for load in loads[1:]:
-        load.wait()
+    loads[1].wait()
     for j in range(SLOTS):
         kept = jnp.where(j < alive[0], own[0, j], jnp.zeros((BLOCK, BLOCK), jnp.bfloat16))
-        block[0, 0:BLOCK, j * BLOCK : (j + 1) * BLOCK] = kept
-    base = lax.axis_index("tm") * TSTEP
+        cat[0:BLOCK, j * BLOCK : (j + 1) * BLOCK] = kept
+    sends = send(cat.at[pl.ds(0, BLOCK), :], 0, BLOCK, 0)
+    for load in loads[2:]:
+        load.wait()
     pattern[...] = jnp.zeros_like(pattern)
     pattern[pl.ds(ONE_ROW, 1), :] = jnp.ones((1, WIDE), jnp.float32)
     pattern[pl.ds(LIVE_ROW, 1), :] = jnp.full((1, WIDE), alive[0].astype(jnp.float32))
     for j in range(SLOTS):
         moment = (base + when[0, j]).astype(jnp.float32)
         pattern[pl.ds(TIME_ROW, 1), j * BLOCK : (j + 1) * BLOCK] = jnp.full((1, BLOCK), moment)
-    for copy in copies:
-        copy.wait()
-    lat = jnp.concatenate([lat_row[j] for j in range(SLOTS)], axis=1).astype(jnp.float32)
-    lon = jnp.concatenate([lon_row[j] for j in range(SLOTS)], axis=1).astype(jnp.float32)
-    latitude = (lat - 89.5) * RADIANS
-    longitude = (lon + 0.5) * RADIANS
-    across = jnp.cos(latitude)
-    units = (across * jnp.cos(longitude), across * jnp.sin(longitude), jnp.sin(latitude))
+        rows[pl.ds(j, 1), :] = lat[pl.ds(where[0, j], 1), :]
+        rows[pl.ds(SLOTS + j, 1), :] = lon[pl.ds(where[0, j], 1), :]
+    degrees = rows[...].astype(jnp.float32)
+    is_lat = lax.broadcasted_iota(jnp.int32, degrees.shape, 0) < SLOTS
+    angles = (degrees + jnp.where(is_lat, -89.5, 0.5)) * RADIANS
+    cosines, sines = jnp.cos(angles), jnp.sin(angles)
+    across = cosines[0:SLOTS]
+    units = (across * cosines[SLOTS:], across * sines[SLOTS:], sines[0:SLOTS])
     for c, unit in enumerate(units):
         for part, value in enumerate(split3(unit)):
-            pattern[pl.ds(PARTS * c + part, 1), :] = value
-    block[0, BLOCK:ROWS, :] = pattern[...].astype(jnp.bfloat16)
-    for i in range(count):
-        payload[i] = block[0]
+            for j in range(SLOTS):
+                pattern[pl.ds(PARTS * c + part, 1), j * BLOCK : (j + 1) * BLOCK] = value[j : j + 1]
+    cat[BLOCK:ROWS, :] = pattern[...].astype(jnp.bfloat16)
+    sends += send(cat.at[pl.ds(BLOCK, PATTERN), :], BLOCK, PATTERN, 1)
+    for copy in sends:
+        copy.wait()
 
 
 def make_block(footprints, times, cells, live, lat, lon, count):
-    vmem = pl.BlockSpec(memory_space=pltpu.VMEM)
     hbm = pl.BlockSpec(memory_space=pltpu.HBM)
     return pl.pallas_call(
-        functools.partial(block_kernel, count),
+        block_kernel,
         out_shape=(
             jax.ShapeDtypeStruct((1, ROWS, WIDE), jnp.bfloat16),
             jax.ShapeDtypeStruct((count, ROWS, WIDE), jnp.bfloat16),
         ),
         in_specs=[hbm] * 6,
-        out_specs=(vmem, vmem),
+        out_specs=(hbm, hbm),
         scratch_shapes=[
             pltpu.VMEM((1, SLOTS, BLOCK, BLOCK), jnp.bfloat16),
             pltpu.SMEM((1, SLOTS), jnp.int32),
             pltpu.SMEM((1, SLOTS), jnp.int32),
             pltpu.SMEM((1,), jnp.int32),
-            pltpu.VMEM((SLOTS, 1, BLOCK), jnp.int32),
-            pltpu.VMEM((SLOTS, 1, BLOCK), jnp.int32),
+            pltpu.VMEM(lat.shape, jnp.int32),
+            pltpu.VMEM(lon.shape, jnp.int32),
+            pltpu.VMEM((ROWS, WIDE), jnp.bfloat16),
+            pltpu.VMEM((2 * SLOTS, BLOCK), jnp.int32),
             pltpu.VMEM((PATTERN, WIDE), jnp.float32),
-            pltpu.SemaphoreType.DMA((4,)),
-            pltpu.SemaphoreType.DMA((2, SLOTS)),
+            pltpu.SemaphoreType.DMA((6,)),
+            pltpu.SemaphoreType.DMA((2, count + 1)),
         ],
         compiler_params=pltpu.CompilerParams(vmem_limit_bytes=60 * 2**20),
         name="make_block",
@@ -170,9 +184,23 @@
     return pl.ds(pl.multiple_of(start, BLOCK), width)
 
 
-def tiles_kernel(count, *refs):
-    blocks, far, outs = refs[:count], refs[count], refs[count + 1 : 2 * count + 1]
-    near_rows, near_vec, near_time, cats, far_pattern, gain, tiles, weights = refs[2 * count + 1 :]
+def tiles_kernel(count, placing, *refs):
+    blocks, far = refs[:count], refs[count]
+    if placing:
+        before, before_partner, out = refs[count + 1 : count + 4]
+        *scratch, wide, wide_partner, own, sems = refs[count + 4 :]
+        outs = (own,)
+        x, odd, earlier = where_placed()
+        wide[...] = before[...].astype(jnp.float32)
+        wide_partner[...] = before_partner[...].astype(jnp.float32)
+        copies = spread(wide, out, 0, earlier, sems.at[0])
+        copies += spread(wide_partner, out, 0, earlier + PAIR, sems.at[1])
+        for copy in copies:
+            copy.start()
+    else:
+        outs = refs[count + 1 : 2 * count + 1]
+        scratch = refs[2 * count + 1 :]
+    near_rows, near_vec, near_time, cats, far_pattern, gain, tiles, weights = scratch
     n_far = far.shape[0]
     near_live = []
     for s in range(count):
@@ -234,33 +262,47 @@
     for u in range(count * n_far):
         s, r = u // n_far, u % n_far
         outs[s][:, r * BLOCK : (r + 1) * BLOCK] = tiles[u]
-
-
-def make_tiles(blocks, far, dtype):
+    if placing:
+        last = spread(own, out, 2 * own.shape[1], pair_start(x, odd), sems.at[2])
+        for copy in last:
+            copy.start()
+        for copy in copies + last:
+            copy.wait()
+
+
+def make_tiles(blocks, far, dtype, arrived=()):
     count, n_far = len(blocks), far.shape[0]
     vmem = pl.BlockSpec(memory_space=pltpu.VMEM)
-    shape = jax.ShapeDtypeStruct((BLOCK, n_far * BLOCK), dtype)
+    width = n_far * BLOCK
+    scratch = [
+        pltpu.VMEM((DEPTH, WIDE), jnp.float32),
+        pltpu.VMEM((count, WIDE, DEPTH), jnp.bfloat16),
+        pltpu.VMEM((count, 8, WIDE), jnp.float32),
+        pltpu.VMEM((count, BLOCK, WIDE), jnp.bfloat16),
+        pltpu.VMEM((PATTERN, (n_far + 2) * WIDE), jnp.bfloat16),
+        pltpu.VMEM((BLOCK, (n_far + 2) * WIDE), jnp.bfloat16),
+        pltpu.VMEM((count * n_far, BLOCK, BLOCK), dtype),
+        pltpu.VMEM((2, WIDE, CHUNK), jnp.bfloat16),
+    ]
+    if arrived:
+        out_shape = (jax.ShapeDtypeStruct((BLOCK, 4 * width), jnp.float32),)
+        scratch += [pltpu.VMEM((BLOCK, width), jnp.float32)] * 3 + [pltpu.SemaphoreType.DMA((3, SIDE * PAIR))]
+        out_specs = (pl.BlockSpec(memory_space=pltpu.HBM),)
+    else:
+        out_shape = (jax.ShapeDtypeStruct((BLOCK, width), dtype),) * count
+        out_specs = (vmem,) * count
     return pl.pallas_call(
-        functools.partial(tiles_kernel, count),
-        out_shape=(shape,) * count,
-        in_specs=[vmem] * (count + 1),
-        out_specs=(vmem,) * count,
-        scratch_shapes=[
-            pltpu.VMEM((DEPTH, WIDE), jnp.float32),
-            pltpu.VMEM((count, WIDE, DEPTH), jnp.bfloat16),
-            pltpu.VMEM((count, 8, WIDE), jnp.float32),
-            pltpu.VMEM((count, BLOCK, WIDE), jnp.bfloat16),
-            pltpu.VMEM((PATTERN, (n_far + 1) * WIDE), jnp.bfloat16),
-            pltpu.VMEM((BLOCK, (n_far + 1) * WIDE), jnp.bfloat16),
-            pltpu.VMEM((count * n_far, BLOCK, BLOCK), dtype),
-            pltpu.VMEM((2, WIDE, CHUNK), jnp.bfloat16),
-        ],
+        functools.partial(tiles_kernel, count, bool(arrived)),
+        out_shape=out_shape,
+        in_specs=[vmem] * (count + 1 + len(arrived)),
+        out_specs=out_specs,
+        scratch_shapes=scratch,
         compiler_params=pltpu.CompilerParams(vmem_limit_bytes=16 * 2**20),
         cost_estimate=pl.CostEstimate(
             flops=count * 10**9, bytes_accessed=count * 2 * 10**6, transcendentals=count * 2**22
         ),
         name="make_tiles",
-    )(*blocks, far)
+    )(*blocks, far, *arrived)
 
 
 def pair_start(x, odd):
@@ -281,48 +323,15 @@
     return copies
 
 
-def place_most_kernel(own, before, before_partner, out, wide, wide_partner, sems):
+def where_placed():
     x = lax.rem(lax.axis_index("obs"), SIDE)
     odd = lax.rem(lax.axis_index("tm"), 2) == 1
-    width = own.shape[1]
-    earlier = pair_start(x, jnp.logical_not(odd))
-    copies = spread(own, out, 2 * width, pair_start(x, odd), sems.at[0])
-    for copy in copies:
-        copy.start()
-    wide[...] = before[...].astype(jnp.float32)
-    more = spread(wide, out, 0, earlier, sems.at[1])
-    for copy in more:
-        copy.start()
-    wide_partner[...] = before_partner[...].astype(jnp.float32)
-    last = spread(wide_partner, out, 0, earlier + PAIR, sems.at[2])
-    for copy in last:
-        copy.start()
-    for copy in copies + more + last:
-        copy.wait()
-
-
-def place_most(own, before, before_partner):
-    vmem = pl.BlockSpec(memory_space=pltpu.VMEM)
-    return pl.pallas_call(
-        place_most_kernel,
-        out_shape=jax.ShapeDtypeStruct((BLOCK, 4 * own.shape[1]), jnp.float32),
-        in_specs=[vmem] * 3,
-        out_specs=pl.BlockSpec(memory_space=pltpu.HBM),
-        scratch_shapes=[
-            pltpu.VMEM(own.shape, jnp.float32),
-            pltpu.VMEM(own.shape, jnp.float32),
-            pltpu.SemaphoreType.DMA((3, SIDE * PAIR)),
-        ],
-        compiler_params=pltpu.CompilerParams(vmem_limit_bytes=12 * 2**20),
-        cost_estimate=pl.CostEstimate(flops=10**9, bytes_accessed=4 * 10**6, transcendentals=0),
-        name="place_most",
-    )(own, before, before_partner)
+    return x, odd, pair_start(x, jnp.logical_not(odd))
 
 
 def place_rest_kernel(partner, filled, out, wide, sems):
     del filled
-    x = lax.rem(lax.axis_index("obs"), SIDE)
-    odd = lax.rem(lax.axis_index("tm"), 2) == 1
+    x, odd, _ = where_placed()
     wide[...] = partner[...].astype(jnp.float32)
     copies = spread(wide, out, 2 * wide.shape[1], pair_start(x, odd) + PAIR, sems)
     for copy in copies:
@@ -369,8 +378,8 @@
                     pairs.append((t * group + o, (t + by) * group + other))
         return pairs
 
-    lat = cell_lat.reshape(-1, 1, BLOCK)
-    lon = cell_lon.reshape(-1, 1, BLOCK)
+    lat = cell_lat.reshape(-1, BLOCK)
+    lon = cell_lon.reshape(-1, BLOCK)
     block, payload = make_block(
         footprints, block_times, block_cells, live_counts, lat, lon, group // (SIDE // PAIR)
     )
@@ -386,8 +395,8 @@
     partner = lax.ppermute(partner_tiles, axes, steps(0, True))
     (next_tiles,) = make_tiles((next_block,), far, jnp.bfloat16)
     before = lax.ppermute(next_tiles, axes, steps(1, False))
-    (own,) = make_tiles((block,), far, jnp.float32)
-    cross_cov = place_rest(partner, place_most(own, before, before_partner))
+    (filled,) = make_tiles((block,), far, jnp.float32, (before, before_partner))
+    cross_cov = place_rest(partner, filled)
     return (cross_cov, footprint_cov)
 
 

time: 55.5 us -> 52.9 us (0.953)
  the two profiles are of different devices: /device:TPU:134 before, /device:TPU:230 now
where the time goes in v4:
time: 52.9 us; the launch traced here: 52.5 us
  starting transfers between devices  27.3 us (52%)
  Pallas kernels  15.6 us (29%)
  waiting for transfers between devices  8.23 us (16%)
  between operations  1.39 us (3%)
    pallas_call x4, Pallas kernels, make_tiles(): pl.pallas_call(functools.partial(tiles_kernel, count, bool(arrived)), out...  11.1 us
    ppermute x1, starting transfers between devices, on_device(): before_partner = lax.ppermute(next_partner_tiles, axes, steps(1, True))  8.16 us
    all_to_all x1, starting transfers between devices, on_device(): lax.all_to_all(payload, axes, 0, 0, tiled=True, axis_index_groups=near_by)  6.07 us
    ppermute x1, starting transfers between devices, on_device(): partner_block = lax.ppermute(block, axes, steps(0, True))  4.95 us
    all_to_all x1, waiting for transfers between devices, on_device(): lax.all_to_all(payload, axes, 0, 0, tiled=True, axis_index_groups=near_by)  4.82 us
    ppermute x1, waiting for transfers between devices, on_device(): partner = lax.ppermute(partner_tiles, axes, steps(0, True))  3.4 us
    ppermute x1, starting transfers between devices, on_device(): partner = lax.ppermute(partner_tiles, axes, steps(0, True))  2.33 us
    pallas_call x1, Pallas kernels, make_block(): pl.pallas_call(block_kernel, out_shape=(jax.ShapeDtypeStruct((1, ROWS, WI...  2.19 us
  transfers between devices with their start and end apart: 7, of which 2 were waited for; matrix products, arithmetic and copies ran while one was open for 0% of the time, Pallas kernels for 24%

profile of v4, /device:TPU:230, one launch (start us, length us, event | category | flops | bytes accessed | tf_op | source)
XLA Modules:
  0.0 52.5 jit_solution(10508389230102312662)
XLA Ops:
  1.3 2.2 %make_block.1 = (bf16[1,144,512]{2,1,0:T(8,128)(2,1)}, bf16[8,144,512]{2,1,0:T(8,128)(2,1)}) custom-call(bf16[1,4,128,128]{3,2,1,0:T(8,128)(2,1)} %prints.1, s32[1,4]{1,0:T(1,128)} %times.1, s32[1,4]{1,0:T(1,128)} %cells.1, s32[1]{0:T(128)S(6)} %copy.10.live, s32[512,128]{1,0:T(8,128)} %bitcast.2, s32[512,128]{1,0:T(8,128)} %bitcast.3), custom_call_target="tpu_custom_call" | custom-call | tf_op jit(solution)/shard_map/make_block/pallas_call | solution.py:99
  3.5 0.0 copy-start
  3.5 6.1 %all-to-all-start = ((bf16[8,144,512]{2,1,0:T(8,128)(2,1)}), bf16[8,144,512]{2,1,0:T(8,128)(2,1)S(1)}, u32[]{:S(2)}, u32[]{:S(2)}) async-start(bf16[8,144,512]{2,1,0:T(8,128)(2,1)} %get-tuple-element.7), calls=%async_computation | async-start | bytes 2359296 | tf_op jit(solution)/shard_map/all_to_all | solution.py:386
  9.6 0.0 copy-done
  9.6 1.9 %collective-permute-start.4 = (bf16[1,144,512]{2,1,0:T(8,128)(2,1)S(1)}, bf16[1,144,512]{2,1,0:T(8,128)(2,1)S(1)}, u32[]{:S(2)}, u32[]{:S(2)}) collective-permute-start(bf16[1,144,512]{2,1,0:T(8,128)(2,1)S(1)} %copy-done), channel_id=1, source_target_pairs={{16,3},{17,2},{18,1},{19,0},{20,7},{21,6},{22,5},{23,4},{24,11},{2... | collective-permute-start | bytes 442376 | tf_op jit(solution)/shard_map/ppermute | solution.py:389
  11.5 1.9 %collective-permute-start.2 = (bf16[1,144,512]{2,1,0:T(8,128)(2,1)S(1)}, bf16[1,144,512]{2,1,0:T(8,128)(2,1)S(1)}, u32[]{:S(2)}, u32[]{:S(2)}) collective-permute-start(bf16[1,144,512]{2,1,0:T(8,128)(2,1)S(1)} %copy-done), channel_id=1, source_target_pairs={{16,0},{17,1},{18,2},{19,3},{20,4},{21,5},{22,6},{23,7},{24,8},{25... | collective-permute-start | bytes 442376 | tf_op jit(solution)/shard_map/ppermute | solution.py:388
  13.4 4.9 %collective-permute-start = (bf16[1,144,512]{2,1,0:T(8,128)(2,1)S(1)}, bf16[1,144,512]{2,1,0:T(8,128)(2,1)S(1)}, u32[]{:S(2)}, u32[]{:S(2)}) collective-permute-start(bf16[1,144,512]{2,1,0:T(8,128)(2,1)S(1)} %copy-done), channel_id=1, source_target_pairs={{0,3},{1,2},{2,1},{3,0},{4,7},{5,6},{6,5},{7,4},{8,11},{9,10},{10,... | collective-permute-start | bytes 442376 | tf_op jit(solution)/shard_map/ppermute | solution.py:387
  18.4 1.4 %self_gain.1 = f32[1,4,128,128]{3,2,1,0:T(8,128)} custom-call(bf16[1,144,512]{2,1,0:T(8,128)(2,1)S(1)} %copy-done), custom_call_target="tpu_custom_call" | custom-call | flops 2000000000 | bytes 1000000 | tf_op jit(solution)/shard_map/self_gain/pallas_call | solution.py:162
  19.8 4.8 %all-to-all-done.refs_1_ = bf16[8,144,512]{2,1,0:T(8,128)(2,1)S(1)} async-done(((bf16[8,144,512]{2,1,0:T(8,128)(2,1)}), bf16[8,144,512]{2,1,0:T(8,128)(2,1)S(1)}, u32[]{:S(2)}, u32[]{:S(2)}) %all-to-all-start) | async-done | bytes 1179680 | tf_op jit(solution)/shard_map/all_to_all | solution.py:386
  24.6 0.0 collective-permute-done.2.refs_0_
  24.6 2.0 %make_tiles.5 = bf16[128,1024]{1,0:T(8,128)(2,1)S(1)} custom-call(bf16[1,144,512]{2,1,0:T(8,128)(2,1)S(1)} %collective-permute-done.2.refs_0_, bf16[8,144,512]{2,1,0:T(8,128)(2,1)S(1)} %all-to-all-done.refs_1_), custom_call_target="tpu_custom_call" | custom-call | flops 1000000000 | bytes 2000000 | tf_op jit(solution)/shard_map/make_tiles/pallas_call | solution.py:294
  26.6 1.9 %collective-permute-start.3 = (bf16[128,1024]{1,0:T(8,128)(2,1)S(1)}, bf16[128,1024]{1,0:T(8,128)(2,1)S(1)}, u32[]{:S(2)}, u32[]{:S(2)}) collective-permute-start(bf16[128,1024]{1,0:T(8,128)(2,1)S(1)} %make_tiles.5), channel_id=1, source_target_pairs={{0,16},{1,17},{2,18},{3,19},{4,20},{5,21},{6,22},{7,23},{8,24},{9,... | collective-permute-start | bytes 786440 | tf_op jit(solution)/shard_map/ppermute | solution.py:397
  28.5 0.0 collective-permute-done.4.refs_0_
  28.5 2.7 %make_tiles.6 = bf16[128,1024]{1,0:T(8,128)(2,1)S(1)} custom-call(bf16[1,144,512]{2,1,0:T(8,128)(2,1)S(1)} %collective-permute-done.4.refs_0_, bf16[8,144,512]{2,1,0:T(8,128)(2,1)S(1)} %all-to-all-done.refs_1_), custom_call_target="tpu_custom_call" | custom-call | flops 1000000000 | bytes 2000000 | tf_op jit(solution)/shard_map/make_tiles/pallas_call | solution.py:294
  31.3 8.2 %collective-permute-start.5 = (bf16[128,1024]{1,0:T(8,128)(2,1)S(1)}, bf16[128,1024]{1,0:T(8,128)(2,1)S(1)}, u32[]{:S(2)}, u32[]{:S(2)}) collective-permute-start(bf16[128,1024]{1,0:T(8,128)(2,1)S(1)} %make_tiles.6), channel_id=1, source_target_pairs={{0,19},{1,18},{2,17},{3,16},{4,23},{5,22},{6,21},{7,20},{8,27},{9,... | collective-permute-start | bytes 786440 | tf_op jit(solution)/shard_map/ppermute | solution.py:393
  39.4 0.0 collective-permute-done.refs_0_
  39.4 2.7 %make_tiles.4 = bf16[128,1024]{1,0:T(8,128)(2,1)S(1)} custom-call(bf16[1,144,512]{2,1,0:T(8,128)(2,1)S(1)} %collective-permute-done.refs_0_, bf16[8,144,512]{2,1,0:T(8,128)(2,1)S(1)} %all-to-all-done.refs_1_), custom_call_target="tpu_custom_call" | custom-call | flops 1000000000 | bytes 2000000 | tf_op jit(solution)/shard_map/make_tiles/pallas_call | solution.py:294
  42.1 2.3 %collective-permute-start.1 = (bf16[128,1024]{1,0:T(8,128)(2,1)S(1)}, bf16[128,1024]{1,0:T(8,128)(2,1)S(1)}, u32[]{:S(2)}, u32[]{:S(2)}) collective-permute-start(bf16[128,1024]{1,0:T(8,128)(2,1)S(1)} %make_tiles.4), channel_id=1, source_target_pairs={{0,3},{1,2},{2,1},{3,0},{4,7},{5,6},{6,5},{7,4},{8,11},{9,10},{10,... | collective-permute-start | bytes 786440 | tf_op jit(solution)/shard_map/ppermute | solution.py:395
  44.5 0.0 collective-permute-done.3.refs_2_
  44.5 0.0 collective-permute-done.5.refs_3_
  44.5 3.7 %make_tiles.7.filled = f32[128,4096]{1,0:T(8,128)} custom-call(bf16[1,144,512]{2,1,0:T(8,128)(2,1)S(1)} %copy-done, bf16[8,144,512]{2,1,0:T(8,128)(2,1)S(1)} %all-to-all-done.refs_1_, bf16[128,1024]{1,0:T(8,128)(2,1)S(1)} %collective-permute-done.3.refs_2_, bf16[128,1024]{1,0:T(8,128)(2,1)S(1)} %collective-permute-done.5.refs_3_), custom_call_target="tpu_custom_call" | custom-call | flops 1000000000 | bytes 2000000 | tf_op jit(solution)/shard_map/make_tiles/pallas_call | solution.py:294
  48.2 3.4 %collective-permute-done.1.partner = bf16[128,1024]{1,0:T(8,128)(2,1)S(1)} collective-permute-done((bf16[128,1024]{1,0:T(8,128)(2,1)S(1)}, bf16[128,1024]{1,0:T(8,128)(2,1)S(1)}, u32[]{:S(2)}, u32[]{:S(2)}) %collective-permute-start.1) | collective-permute-done | bytes 262176 | tf_op jit(solution)/shard_map/ppermute | solution.py:395
  51.6 0.9 %place_rest.1 = f32[128,4096]{1,0:T(8,128)} custom-call(bf16[128,1024]{1,0:T(8,128)(2,1)S(1)} %collective-permute-done.1.partner, f32[128,4096]{1,0:T(8,128)} %make_tiles.7.filled), custom_call_target="tpu_custom_call", output_to_operand_aliasing={{}: (1, {})} | custom-call | tf_op jit(solution)/shard_map/place_rest/pallas_call | solution.py:345
Async XLA Ops:
  3.5 6.1 %copy-start = (bf16[1,144,512]{2,1,0:T(8,128)(2,1)S(1)}, bf16[1,144,512]{2,1,0:T(8,128)(2,1)}, u32[]{:S(2)}) copy-start(bf16[1,144,512]{2,1,0:T(8,128)(2,1)} %get-tuple-element.6.block.refs_0_) | copy-start | bytes 442372
  3.5 21.1 %all-to-all-start = ((bf16[8,144,512]{2,1,0:T(8,128)(2,1)}), bf16[8,144,512]{2,1,0:T(8,128)(2,1)S(1)}, u32[]{:S(2)}, u32[]{:S(2)}) async-start(bf16[8,144,512]{2,1,0:T(8,128)(2,1)} %get-tuple-element.7), calls=%async_computation | async-start | bytes 2359296 | tf_op jit(solution)/shard_map/all_to_all | solution.py:386
  9.6 19.0 %collective-permute-start.4 = (bf16[1,144,512]{2,1,0:T(8,128)(2,1)S(1)}, bf16[1,144,512]{2,1,0:T(8,128)(2,1)S(1)}, u32[]{:S(2)}, u32[]{:S(2)}) collective-permute-start(bf16[1,144,512]{2,1,0:T(8,128)(2,1)S(1)} %copy-done), channel_id=1, source_target_pairs={{16,3},{17,2},{18,1},{19,0},{20,7},{21,6},{22,5},{23,4},{24,11},{2... | collective-permute-start | bytes 442376 | tf_op jit(solution)/shard_map/ppermute | solution.py:389
  11.5 13.1 %collective-permute-start.2 = (bf16[1,144,512]{2,1,0:T(8,128)(2,1)S(1)}, bf16[1,144,512]{2,1,0:T(8,128)(2,1)S(1)}, u32[]{:S(2)}, u32[]{:S(2)}) collective-permute-start(bf16[1,144,512]{2,1,0:T(8,128)(2,1)S(1)} %copy-done), channel_id=1, source_target_pairs={{16,0},{17,1},{18,2},{19,3},{20,4},{21,5},{22,6},{23,7},{24,8},{25... | collective-permute-start | bytes 442376 | tf_op jit(solution)/shard_map/ppermute | solution.py:388
  13.4 26.0 %collective-permute-start = (bf16[1,144,512]{2,1,0:T(8,128)(2,1)S(1)}, bf16[1,144,512]{2,1,0:T(8,128)(2,1)S(1)}, u32[]{:S(2)}, u32[]{:S(2)}) collective-permute-start(bf16[1,144,512]{2,1,0:T(8,128)(2,1)S(1)} %copy-done), channel_id=1, source_target_pairs={{0,3},{1,2},{2,1},{3,0},{4,7},{5,6},{6,5},{7,4},{8,11},{9,10},{10,... | collective-permute-start | bytes 442376 | tf_op jit(solution)/shard_map/ppermute | solution.py:387
  26.6 17.9 %collective-permute-start.3 = (bf16[128,1024]{1,0:T(8,128)(2,1)S(1)}, bf16[128,1024]{1,0:T(8,128)(2,1)S(1)}, u32[]{:S(2)}, u32[]{:S(2)}) collective-permute-start(bf16[128,1024]{1,0:T(8,128)(2,1)S(1)} %make_tiles.5), channel_id=1, source_target_pairs={{0,16},{1,17},{2,18},{3,19},{4,20},{5,21},{6,22},{7,23},{8,24},{9,... | collective-permute-start | bytes 786440 | tf_op jit(solution)/shard_map/ppermute | solution.py:397
  31.3 13.3 %collective-permute-start.5 = (bf16[128,1024]{1,0:T(8,128)(2,1)S(1)}, bf16[128,1024]{1,0:T(8,128)(2,1)S(1)}, u32[]{:S(2)}, u32[]{:S(2)}) collective-permute-start(bf16[128,1024]{1,0:T(8,128)(2,1)S(1)} %make_tiles.6), channel_id=1, source_target_pairs={{0,19},{1,18},{2,17},{3,16},{4,23},{5,22},{6,21},{7,20},{8,27},{9,... | collective-permute-start | bytes 786440 | tf_op jit(solution)/shard_map/ppermute | solution.py:393
  42.1 9.5 %collective-permute-start.1 = (bf16[128,1024]{1,0:T(8,128)(2,1)S(1)}, bf16[128,1024]{1,0:T(8,128)(2,1)S(1)}, u32[]{:S(2)}, u32[]{:S(2)}) collective-permute-start(bf16[128,1024]{1,0:T(8,128)(2,1)S(1)} %make_tiles.4), channel_id=1, source_target_pairs={{0,3},{1,2},{2,1},{3,0},{4,7},{5,6},{6,5},{7,4},{8,11},{9,10},{10,... | collective-permute-start | bytes 786440 | tf_op jit(solution)/shard_map/ppermute | solution.py:395

commit v5 on v4

--- a/solution.py
+++ b/solution.py
@@ -150,29 +150,54 @@
         weights[rows, :] = jnp.exp2(lag - square * lax.rsqrt(square)).astype(jnp.bfloat16)
 
 
-def self_kernel(block, out, near_rows, near_vec, weights):
-    near_vec[...], when = prepare_near(block, near_rows)
-    weigh(near_vec, when, block[0, BLOCK:ROWS, :], weights, SLOTS)
-    gain = jnp.dot(block[0, 0:BLOCK, :], weights[...], preferred_element_type=jnp.float32)
-    for j in range(SLOTS):
-        out[0, j] = gain[:, j * BLOCK : (j + 1) * BLOCK]
-
-
-def self_gain(block):
+def local_kernel(*refs):
+    *blocks, cov, local, near_rows, near_vec, weights = refs
+    last = len(blocks) - 1
+    own = blocks[last]
+    far_pattern = own[0, BLOCK:ROWS, :]
+
+    def weigh_near(s):
+        near_vec[s], when = prepare_near(blocks[s], near_rows)
+        weigh(near_vec.at[s], when, far_pattern, weights.at[s % 2], SLOTS)
+
+    def finish(s):
+        gain = jnp.dot(blocks[s][0, 0:BLOCK, :], weights[s % 2], preferred_element_type=jnp.float32)
+        if s == last:
+            for j in range(SLOTS):
+                cov[0, j] = gain[:, j * BLOCK : (j + 1) * BLOCK]
+        local[s] = lax.dot_general(
+            gain.astype(jnp.bfloat16),
+            own[0, 0:BLOCK, :],
+            (((1,), (1,)), ((), ())),
+            preferred_element_type=jnp.float32,
+        )
+
+    for s in range(last + 1):
+        weigh_near(s)
+        if s:
+            finish(s - 1)
+    finish(last)
+
+
+def make_local(*blocks):
+    vmem = pl.BlockSpec(memory_space=pltpu.VMEM)
     return pl.pallas_call(
-        self_kernel,
-        out_shape=jax.ShapeDtypeStruct((1, SLOTS, BLOCK, BLOCK), jnp.float32),
-        in_specs=[pl.BlockSpec(memory_space=pltpu.VMEM)],
-        out_specs=pl.BlockSpec(memory_space=pltpu.VMEM),
+        local_kernel,
+        out_shape=(
+            jax.ShapeDtypeStruct((1, SLOTS, BLOCK, BLOCK), jnp.float32),
+            jax.ShapeDtypeStruct((len(blocks), BLOCK, BLOCK), jnp.float32),
+        ),
+        in_specs=[vmem] * len(blocks),
+        out_specs=(vmem, vmem),
         scratch_shapes=[
             pltpu.VMEM((DEPTH, WIDE), jnp.float32),
-            pltpu.VMEM((WIDE, DEPTH), jnp.bfloat16),
-            pltpu.VMEM((WIDE, WIDE), jnp.bfloat16),
+            pltpu.VMEM((len(blocks), WIDE, DEPTH), jnp.bfloat16),
+            pltpu.VMEM((2, WIDE, WIDE), jnp.bfloat16),
         ],
         compiler_params=pltpu.CompilerParams(vmem_limit_bytes=12 * 2**20),
-        cost_estimate=pl.CostEstimate(flops=2 * 10**9, bytes_accessed=10**6, transcendentals=2**19),
-        name="self_gain",
-    )(block)
+        cost_estimate=pl.CostEstimate(flops=4 * 10**9, bytes_accessed=10**6, transcendentals=2**21),
+        name="make_local",
+    )(*blocks)
 
 
 def live_of(pattern):
@@ -184,13 +209,15 @@
     return pl.ds(pl.multiple_of(start, BLOCK), width)
 
 
-def tiles_kernel(count, placing, *refs):
-    blocks, far = refs[:count], refs[count]
+def tiles_kernel(count, base, placing, *refs):
+    blocks, (far, local), refs = refs[:count], refs[count : count + 2], refs[count + 2 :]
+    x, odd, earlier = where_placed()
+    row = lax.axis_index("obs") // SIDE
+    mine = row * PAIR + lax.rem(x - pair_start(x, odd) + SIDE, SIDE)
+    known = base >= 0
     if placing:
-        before, before_partner, out = refs[count + 1 : count + 4]
-        *scratch, wide, wide_partner, own, sems = refs[count + 4 :]
+        before, before_partner, out, *scratch, wide, wide_partner, own, sems = refs
         outs = (own,)
-        x, odd, earlier = where_placed()
         wide[...] = before[...].astype(jnp.float32)
         wide_partner[...] = before_partner[...].astype(jnp.float32)
         copies = spread(wide, out, 0, earlier, sems.at[0])
@@ -198,8 +225,7 @@
         for copy in copies:
             copy.start()
     else:
-        outs = refs[count + 1 : 2 * count + 1]
-        scratch = refs[2 * count + 1 :]
+        outs, scratch = refs[:count], refs[count:]
     near_rows, near_vec, near_time, cats, far_pattern, gain, tiles, weights = scratch
     n_far = far.shape[0]
     near_live = []
@@ -214,10 +240,11 @@
         pattern = far[r, BLOCK:ROWS, :]
         far_pattern[:, columns_at(filled * BLOCK, WIDE)] = pattern
         starts.append(filled * BLOCK)
-        filled = filled + live_of(pattern)
+        filled = filled + (jnp.where(r == mine, 0, live_of(pattern)) if known else live_of(pattern))
     far_pattern[:, columns_at(filled * BLOCK, WIDE)] = jnp.zeros((PATTERN, WIDE), jnp.bfloat16)
-    turns = (filled * BLOCK + 2 * CHUNK - 1) // (2 * CHUNK)
-    gain[:, columns_at(turns * 2 * CHUNK, WIDE)] = jnp.zeros((BLOCK, WIDE), jnp.bfloat16)
+    chunks = (filled * BLOCK + CHUNK - 1) // CHUNK
+    turns = chunks // 2
+    gain[:, columns_at(chunks * CHUNK, WIDE)] = jnp.zeros((BLOCK, WIDE), jnp.bfloat16)
 
     def one_near(s, carry):
         live = near_live[0]
@@ -247,30 +274,50 @@
                     return carry
 
                 lax.fori_loop(0, turns, turn, 0)
-                gain_chunk(turns * 2 * CHUNK - CHUNK, 1, used)
+                rest = turns * 2 * CHUNK
+
+                @pl.when(chunks == 2 * turns)
+                def _():
+                    gain_chunk(rest - CHUNK, 1, used)
+
+                @pl.when(chunks != 2 * turns)
+                def _():
+                    weigh_chunk(rest, 0, used)
+                    gain_chunk(jnp.maximum(rest - CHUNK, 0), 1, used)
+                    gain_chunk(rest, 0, used)
 
         for r in range(n_far):
-            tiles[s * n_far + r] = lax.dot_general(
+            tile = lax.dot_general(
                 gain[:, columns_at(starts[r], WIDE)],
                 far[r, 0:BLOCK, :],
                 (((1,), (1,)), ((), ())),
                 preferred_element_type=jnp.float32,
-            ).astype(tiles.dtype)
+            )
+            if known:
+                tile = jnp.where(r == mine, local[base + s], tile)
+            if count == 1:
+                outs[0][:, r * BLOCK : (r + 1) * BLOCK] = tile.astype(outs[0].dtype)
+                if placing:
+                    last[r].start()
+            else:
+                tiles[s * n_far + r] = tile.astype(tiles.dtype)
         return carry
 
-    lax.fori_loop(0, count, one_near, 0)
-    for u in range(count * n_far):
-        s, r = u // n_far, u % n_far
-        outs[s][:, r * BLOCK : (r + 1) * BLOCK] = tiles[u]
     if placing:
         last = spread(own, out, 2 * own.shape[1], pair_start(x, odd), sems.at[2])
-        for copy in last:
-            copy.start()
+    if count == 1:
+        one_near(0, 0)
+    else:
+        lax.fori_loop(0, count, one_near, 0)
+        for u in range(count * n_far):
+            s, r = u // n_far, u % n_far
+            outs[s][:, r * BLOCK : (r + 1) * BLOCK] = tiles[u]
+    if placing:
         for copy in copies + last:
             copy.wait()
 
 
-def make_tiles(blocks, far, dtype, arrived=()):
+def make_tiles(blocks, base, far, local, dtype, arrived=()):
     count, n_far = len(blocks), far.shape[0]
     vmem = pl.BlockSpec(memory_space=pltpu.VMEM)
     width = n_far * BLOCK
@@ -292,9 +339,9 @@
         out_shape = (jax.ShapeDtypeStruct((BLOCK, width), dtype),) * count
         out_specs = (vmem,) * count
     return pl.pallas_call(
-        functools.partial(tiles_kernel, count, bool(arrived)),
+        functools.partial(tiles_kernel, count, base, bool(arrived)),
         out_shape=out_shape,
-        in_specs=[vmem] * (count + 1 + len(arrived)),
+        in_specs=[vmem] * (count + 2 + len(arrived)),
         out_specs=out_specs,
         scratch_shapes=scratch,
         compiler_params=pltpu.CompilerParams(vmem_limit_bytes=16 * 2**20),
@@ -302,7 +349,7 @@
             flops=count * 10**9, bytes_accessed=count * 2 * 10**6, transcendentals=count * 2**22
         ),
         name="make_tiles",
-    )(*blocks, far, *arrived)
+    )(*blocks, far, local, *arrived)
 
 
 def pair_start(x, odd):
@@ -387,15 +434,15 @@
     partner_block = lax.ppermute(block, axes, steps(0, True))
     next_block = lax.ppermute(block, axes, steps(-1, False))
     next_partner_block = lax.ppermute(block, axes, steps(-1, True))
-    footprint_cov = self_gain(block)
-    far, footprint_cov = lax.optimization_barrier((far, footprint_cov))
-    (next_partner_tiles,) = make_tiles((next_partner_block,), far, jnp.bfloat16)
+    footprint_cov, local = make_local(partner_block, block)
+    far, local = lax.optimization_barrier((far, local))
+    (next_partner_tiles,) = make_tiles((next_partner_block,), -1, far, local, jnp.bfloat16)
+    (next_tiles,) = make_tiles((next_block,), -1, far, local, jnp.bfloat16)
     before_partner = lax.ppermute(next_partner_tiles, axes, steps(1, True))
-    (partner_tiles,) = make_tiles((partner_block,), far, jnp.bfloat16)
+    before = lax.ppermute(next_tiles, axes, steps(1, False))
+    (partner_tiles,) = make_tiles((partner_block,), 0, far, local, jnp.bfloat16)
     partner = lax.ppermute(partner_tiles, axes, steps(0, True))
-    (next_tiles,) = make_tiles((next_block,), far, jnp.bfloat16)
-    before = lax.ppermute(next_tiles, axes, steps(1, False))
-    (filled,) = make_tiles((block,), far, jnp.float32, (before, before_partner))
+    (filled,) = make_tiles((block,), 1, far, local, jnp.float32, (before, before_partner))
     cross_cov = place_rest(partner, filled)
     return (cross_cov, footprint_cov)
 

time: 52.9 us -> 52 us (0.983)
  the two profiles are of different devices: /device:TPU:230 before, /device:TPU:238 now
where the time goes in v5:
time: 52 us; the launch traced here: 51.7 us
  starting transfers between devices  27.3 us (52%)
  Pallas kernels  15.1 us (29%)
  waiting for transfers between devices  7.77 us (15%)
  between operations  1.56 us (3%)
    pallas_call x4, Pallas kernels, make_tiles(): pl.pallas_call(functools.partial(tiles_kernel, count, base, bool(arrived)...  10.2 us
    ppermute x1, starting transfers between devices, on_device(): before_partner = lax.ppermute(next_partner_tiles, axes, steps(1, True))  8.18 us
    all_to_all x1, starting transfers between devices, on_device(): lax.all_to_all(payload, axes, 0, 0, tiled=True, axis_index_groups=near_by)  5.96 us
    ppermute x1, starting transfers between devices, on_device(): next_block = lax.ppermute(block, axes, steps(-1, False))  4.46 us
    ppermute x1, waiting for transfers between devices, on_device(): partner = lax.ppermute(partner_tiles, axes, steps(0, True))  4.2 us
    all_to_all x1, waiting for transfers between devices, on_device(): lax.all_to_all(payload, axes, 0, 0, tiled=True, axis_index_groups=near_by)  2.46 us
    ppermute x1, starting transfers between devices, on_device(): before = lax.ppermute(next_tiles, axes, steps(1, False))  2.41 us
    ppermute x1, starting transfers between devices, on_device(): partner_block = lax.ppermute(block, axes, steps(0, True))  2.4 us
  transfers between devices with their start and end apart: 7, of which 3 were waited for; matrix products, arithmetic and copies ran while one was open for 0% of the time, Pallas kernels for 23%

profile of v5, /device:TPU:238, one launch (start us, length us, event | category | flops | bytes accessed | tf_op | source)
XLA Modules:
  0.0 51.7 jit_solution(14333681442159998536)
XLA Ops:
  1.3 2.2 %make_block.1 = (bf16[1,144,512]{2,1,0:T(8,128)(2,1)}, bf16[8,144,512]{2,1,0:T(8,128)(2,1)}) custom-call(bf16[1,4,128,128]{3,2,1,0:T(8,128)(2,1)} %prints.1, s32[1,4]{1,0:T(1,128)} %times.1, s32[1,4]{1,0:T(1,128)} %cells.1, s32[1]{0:T(128)S(6)} %copy.10.live, s32[512,128]{1,0:T(8,128)} %bitcast.2, s32[512,128]{1,0:T(8,128)} %bitcast.3), custom_call_target="tpu_custom_call" | custom-call | tf_op jit(solution)/shard_map/make_block/pallas_call | solution.py:99
  3.5 0.0 copy-start
  3.5 6.0 %all-to-all-start = ((bf16[8,144,512]{2,1,0:T(8,128)(2,1)}), bf16[8,144,512]{2,1,0:T(8,128)(2,1)S(1)}, u32[]{:S(2)}, u32[]{:S(2)}) async-start(bf16[8,144,512]{2,1,0:T(8,128)(2,1)} %get-tuple-element.9), calls=%async_computation | async-start | bytes 2359296 | tf_op jit(solution)/shard_map/all_to_all | solution.py:433
  9.4 0.0 copy-done
  9.4 2.4 %collective-permute-start = (bf16[1,144,512]{2,1,0:T(8,128)(2,1)S(1)}, bf16[1,144,512]{2,1,0:T(8,128)(2,1)S(1)}, u32[]{:S(2)}, u32[]{:S(2)}) collective-permute-start(bf16[1,144,512]{2,1,0:T(8,128)(2,1)S(1)} %copy-done), channel_id=1, source_target_pairs={{0,3},{1,2},{2,1},{3,0},{4,7},{5,6},{6,5},{7,4},{8,11},{9,10},{10,... | collective-permute-start | bytes 442376 | tf_op jit(solution)/shard_map/ppermute | solution.py:434
  11.9 1.9 %collective-permute-start.4 = (bf16[1,144,512]{2,1,0:T(8,128)(2,1)S(1)}, bf16[1,144,512]{2,1,0:T(8,128)(2,1)S(1)}, u32[]{:S(2)}, u32[]{:S(2)}) collective-permute-start(bf16[1,144,512]{2,1,0:T(8,128)(2,1)S(1)} %copy-done), channel_id=1, source_target_pairs={{16,3},{17,2},{18,1},{19,0},{20,7},{21,6},{22,5},{23,4},{24,11},{2... | collective-permute-start | bytes 442376 | tf_op jit(solution)/shard_map/ppermute | solution.py:436
  13.8 4.5 %collective-permute-start.2 = (bf16[1,144,512]{2,1,0:T(8,128)(2,1)S(1)}, bf16[1,144,512]{2,1,0:T(8,128)(2,1)S(1)}, u32[]{:S(2)}, u32[]{:S(2)}) collective-permute-start(bf16[1,144,512]{2,1,0:T(8,128)(2,1)S(1)} %copy-done), channel_id=1, source_target_pairs={{16,0},{17,1},{18,2},{19,3},{20,4},{21,5},{22,6},{23,7},{24,8},{25... | collective-permute-start | bytes 442376 | tf_op jit(solution)/shard_map/ppermute | solution.py:435
  18.2 1.1 %collective-permute-done.refs_0_ = bf16[1,144,512]{2,1,0:T(8,128)(2,1)S(1)} collective-permute-done((bf16[1,144,512]{2,1,0:T(8,128)(2,1)S(1)}, bf16[1,144,512]{2,1,0:T(8,128)(2,1)S(1)}, u32[]{:S(2)}, u32[]{:S(2)}) %collective-permute-start) | collective-permute-done | bytes 147488 | tf_op jit(solution)/shard_map/ppermute | solution.py:434
  19.4 1.8 %make_local.1 = (f32[1,4,128,128]{3,2,1,0:T(8,128)}, f32[2,128,128]{2,1,0:T(8,128)S(1)}) custom-call(bf16[1,144,512]{2,1,0:T(8,128)(2,1)S(1)} %collective-permute-done.refs_0_, bf16[1,144,512]{2,1,0:T(8,128)(2,1)S(1)} %copy-done), custom_call_target="tpu_custom_call" | custom-call | flops 4000000000 | bytes 1000000 | tf_op jit(solution)/shard_map/make_local/pallas_call | solution.py:184
  21.1 2.5 %all-to-all-done.refs_1_ = bf16[8,144,512]{2,1,0:T(8,128)(2,1)S(1)} async-done(((bf16[8,144,512]{2,1,0:T(8,128)(2,1)}), bf16[8,144,512]{2,1,0:T(8,128)(2,1)S(1)}, u32[]{:S(2)}, u32[]{:S(2)}) %all-to-all-start) | async-done | bytes 1179680 | tf_op jit(solution)/shard_map/all_to_all | solution.py:433
  23.6 0.0 collective-permute-done.2.refs_0_
  23.6 2.0 %make_tiles.5 = bf16[128,1024]{1,0:T(8,128)(2,1)S(1)} custom-call(bf16[1,144,512]{2,1,0:T(8,128)(2,1)S(1)} %collective-permute-done.2.refs_0_, bf16[8,144,512]{2,1,0:T(8,128)(2,1)S(1)} %all-to-all-done.refs_1_, f32[2,128,128]{2,1,0:T(8,128)S(1)} %get-tuple-element.12.refs_2_), custom_call_target="tpu_custom_call" | custom-call | flops 1000000000 | bytes 2000000 | tf_op jit(solution)/shard_map/make_tiles/pallas_call | solution.py:341
  25.6 2.4 %collective-permute-start.3 = (bf16[128,1024]{1,0:T(8,128)(2,1)S(1)}, bf16[128,1024]{1,0:T(8,128)(2,1)S(1)}, u32[]{:S(2)}, u32[]{:S(2)}) collective-permute-start(bf16[128,1024]{1,0:T(8,128)(2,1)S(1)} %make_tiles.5), channel_id=1, source_target_pairs={{0,16},{1,17},{2,18},{3,19},{4,20},{5,21},{6,22},{7,23},{8,24},{9,... | collective-permute-start | bytes 786440 | tf_op jit(solution)/shard_map/ppermute | solution.py:442
  28.0 0.0 collective-permute-done.4.refs_0_
  28.0 2.0 %make_tiles.6 = bf16[128,1024]{1,0:T(8,128)(2,1)S(1)} custom-call(bf16[1,144,512]{2,1,0:T(8,128)(2,1)S(1)} %collective-permute-done.4.refs_0_, bf16[8,144,512]{2,1,0:T(8,128)(2,1)S(1)} %all-to-all-done.refs_1_, f32[2,128,128]{2,1,0:T(8,128)S(1)} %get-tuple-element.12.refs_2_), custom_call_target="tpu_custom_call" | custom-call | flops 1000000000 | bytes 2000000 | tf_op jit(solution)/shard_map/make_tiles/pallas_call | solution.py:341
  30.0 8.2 %collective-permute-start.5 = (bf16[128,1024]{1,0:T(8,128)(2,1)S(1)}, bf16[128,1024]{1,0:T(8,128)(2,1)S(1)}, u32[]{:S(2)}, u32[]{:S(2)}) collective-permute-start(bf16[128,1024]{1,0:T(8,128)(2,1)S(1)} %make_tiles.6), channel_id=1, source_target_pairs={{0,19},{1,18},{2,17},{3,16},{4,23},{5,22},{6,21},{7,20},{8,27},{9,... | collective-permute-start | bytes 786440 | tf_op jit(solution)/shard_map/ppermute | solution.py:441
  38.2 3.0 %make_tiles.4 = bf16[128,1024]{1,0:T(8,128)(2,1)S(1)} custom-call(bf16[1,144,512]{2,1,0:T(8,128)(2,1)S(1)} %collective-permute-done.refs_0_, bf16[8,144,512]{2,1,0:T(8,128)(2,1)S(1)} %all-to-all-done.refs_1_, f32[2,128,128]{2,1,0:T(8,128)S(1)} %get-tuple-element.12.refs_2_), custom_call_target="tpu_custom_call" | custom-call | flops 1000000000 | bytes 2000000 | tf_op jit(solution)/shard_map/make_tiles/pallas_call | solution.py:341
  41.1 1.9 %collective-permute-start.1 = (bf16[128,1024]{1,0:T(8,128)(2,1)S(1)}, bf16[128,1024]{1,0:T(8,128)(2,1)S(1)}, u32[]{:S(2)}, u32[]{:S(2)}) collective-permute-start(bf16[128,1024]{1,0:T(8,128)(2,1)S(1)} %make_tiles.4), channel_id=1, source_target_pairs={{0,3},{1,2},{2,1},{3,0},{4,7},{5,6},{6,5},{7,4},{8,11},{9,10},{10,... | collective-permute-start | bytes 786440 | tf_op jit(solution)/shard_map/ppermute | solution.py:444
  43.1 0.0 collective-permute-done.3.refs_3_
  43.1 0.0 collective-permute-done.5.refs_4_
  43.1 3.3 %make_tiles.7.filled = f32[128,4096]{1,0:T(8,128)} custom-call(bf16[1,144,512]{2,1,0:T(8,128)(2,1)S(1)} %copy-done, bf16[8,144,512]{2,1,0:T(8,128)(2,1)S(1)} %all-to-all-done.refs_1_, f32[2,128,128]{2,1,0:T(8,128)S(1)} %get-tuple-element.12.refs_2_, bf16[128,1024]{1,0:T(8,128)(2,1)S(1)} %collective-permute-done.3.refs_3_, ...), custom_call_target="tpu_custom_call" | custom-call | flops 1000000000 | bytes 2000000 | tf_op jit(solution)/shard_map/make_tiles/pallas_call | solution.py:341
  46.4 4.2 %collective-permute-done.1.partner = bf16[128,1024]{1,0:T(8,128)(2,1)S(1)} collective-permute-done((bf16[128,1024]{1,0:T(8,128)(2,1)S(1)}, bf16[128,1024]{1,0:T(8,128)(2,1)S(1)}, u32[]{:S(2)}, u32[]{:S(2)}) %collective-permute-start.1) | collective-permute-done | bytes 262176 | tf_op jit(solution)/shard_map/ppermute | solution.py:444
  50.6 0.9 %place_rest.1 = f32[128,4096]{1,0:T(8,128)} custom-call(bf16[128,1024]{1,0:T(8,128)(2,1)S(1)} %collective-permute-done.1.partner, f32[128,4096]{1,0:T(8,128)} %make_tiles.7.filled), custom_call_target="tpu_custom_call", output_to_operand_aliasing={{}: (1, {})} | custom-call | tf_op jit(solution)/shard_map/place_rest/pallas_call | solution.py:392
Async XLA Ops:
  3.5 6.0 %copy-start = (bf16[1,144,512]{2,1,0:T(8,128)(2,1)S(1)}, bf16[1,144,512]{2,1,0:T(8,128)(2,1)}, u32[]{:S(2)}) copy-start(bf16[1,144,512]{2,1,0:T(8,128)(2,1)} %get-tuple-element.8.refs_1_.refs_0_) | copy-start | bytes 442372
  3.5 20.1 %all-to-all-start = ((bf16[8,144,512]{2,1,0:T(8,128)(2,1)}), bf16[8,144,512]{2,1,0:T(8,128)(2,1)S(1)}, u32[]{:S(2)}, u32[]{:S(2)}) async-start(bf16[8,144,512]{2,1,0:T(8,128)(2,1)} %get-tuple-element.9), calls=%async_computation | async-start | bytes 2359296 | tf_op jit(solution)/shard_map/all_to_all | solution.py:433
  9.4 9.9 %collective-permute-start = (bf16[1,144,512]{2,1,0:T(8,128)(2,1)S(1)}, bf16[1,144,512]{2,1,0:T(8,128)(2,1)S(1)}, u32[]{:S(2)}, u32[]{:S(2)}) collective-permute-start(bf16[1,144,512]{2,1,0:T(8,128)(2,1)S(1)} %copy-done), channel_id=1, source_target_pairs={{0,3},{1,2},{2,1},{3,0},{4,7},{5,6},{6,5},{7,4},{8,11},{9,10},{10,... | collective-permute-start | bytes 442376 | tf_op jit(solution)/shard_map/ppermute | solution.py:434
  11.9 16.1 %collective-permute-start.4 = (bf16[1,144,512]{2,1,0:T(8,128)(2,1)S(1)}, bf16[1,144,512]{2,1,0:T(8,128)(2,1)S(1)}, u32[]{:S(2)}, u32[]{:S(2)}) collective-permute-start(bf16[1,144,512]{2,1,0:T(8,128)(2,1)S(1)} %copy-done), channel_id=1, source_target_pairs={{16,3},{17,2},{18,1},{19,0},{20,7},{21,6},{22,5},{23,4},{24,11},{2... | collective-permute-start | bytes 442376 | tf_op jit(solution)/shard_map/ppermute | solution.py:436
  13.8 9.8 %collective-permute-start.2 = (bf16[1,144,512]{2,1,0:T(8,128)(2,1)S(1)}, bf16[1,144,512]{2,1,0:T(8,128)(2,1)S(1)}, u32[]{:S(2)}, u32[]{:S(2)}) collective-permute-start(bf16[1,144,512]{2,1,0:T(8,128)(2,1)S(1)} %copy-done), channel_id=1, source_target_pairs={{16,0},{17,1},{18,2},{19,3},{20,4},{21,5},{22,6},{23,7},{24,8},{25... | collective-permute-start | bytes 442376 | tf_op jit(solution)/shard_map/ppermute | solution.py:435
  25.6 17.5 %collective-permute-start.3 = (bf16[128,1024]{1,0:T(8,128)(2,1)S(1)}, bf16[128,1024]{1,0:T(8,128)(2,1)S(1)}, u32[]{:S(2)}, u32[]{:S(2)}) collective-permute-start(bf16[128,1024]{1,0:T(8,128)(2,1)S(1)} %make_tiles.5), channel_id=1, source_target_pairs={{0,16},{1,17},{2,18},{3,19},{4,20},{5,21},{6,22},{7,23},{8,24},{9,... | collective-permute-start | bytes 786440 | tf_op jit(solution)/shard_map/ppermute | solution.py:442
  30.0 13.1 %collective-permute-start.5 = (bf16[128,1024]{1,0:T(8,128)(2,1)S(1)}, bf16[128,1024]{1,0:T(8,128)(2,1)S(1)}, u32[]{:S(2)}, u32[]{:S(2)}) collective-permute-start(bf16[128,1024]{1,0:T(8,128)(2,1)S(1)} %make_tiles.6), channel_id=1, source_target_pairs={{0,19},{1,18},{2,17},{3,16},{4,23},{5,22},{6,21},{7,20},{8,27},{9,... | collective-permute-start | bytes 786440 | tf_op jit(solution)/shard_map/ppermute | solution.py:441
  41.1 9.5 %collective-permute-start.1 = (bf16[128,1024]{1,0:T(8,128)(2,1)S(1)}, bf16[128,1024]{1,0:T(8,128)(2,1)S(1)}, u32[]{:S(2)}, u32[]{:S(2)}) collective-permute-start(bf16[128,1024]{1,0:T(8,128)(2,1)S(1)} %make_tiles.4), channel_id=1, source_target_pairs={{0,3},{1,2},{2,1},{3,0},{4,7},{5,6},{6,5},{7,4},{8,11},{9,10},{10,... | collective-permute-start | bytes 786440 | tf_op jit(solution)/shard_map/ppermute | solution.py:444

commit v6 on v5

--- a/solution.py
+++ b/solution.py
@@ -216,12 +216,12 @@
     mine = row * PAIR + lax.rem(x - pair_start(x, odd) + SIDE, SIDE)
     known = base >= 0
     if placing:
-        before, before_partner, out, *scratch, wide, wide_partner, own, sems = refs
+        before_partner, partner, out, *scratch, wide, wide_partner, own, sems = refs
         outs = (own,)
-        wide[...] = before[...].astype(jnp.float32)
-        wide_partner[...] = before_partner[...].astype(jnp.float32)
-        copies = spread(wide, out, 0, earlier, sems.at[0])
-        copies += spread(wide_partner, out, 0, earlier + PAIR, sems.at[1])
+        wide[...] = before_partner[...].astype(jnp.float32)
+        wide_partner[...] = partner[...].astype(jnp.float32)
+        copies = spread(wide, out, 0, earlier + PAIR, sems.at[0])
+        copies += spread(wide_partner, out, 2 * own.shape[1], pair_start(x, odd) + PAIR, sems.at[1])
         for copy in copies:
             copy.start()
     else:
@@ -376,18 +376,17 @@
     return x, odd, pair_start(x, jnp.logical_not(odd))
 
 
-def place_rest_kernel(partner, filled, out, wide, sems):
+def place_rest_kernel(before, filled, out, wide, sems):
     del filled
-    x, odd, _ = where_placed()
-    wide[...] = partner[...].astype(jnp.float32)
-    copies = spread(wide, out, 2 * wide.shape[1], pair_start(x, odd) + PAIR, sems)
+    wide[...] = before[...].astype(jnp.float32)
+    copies = spread(wide, out, 0, where_placed()[2], sems)
     for copy in copies:
         copy.start()
     for copy in copies:
         copy.wait()
 
 
-def place_rest(partner, filled):
+def place_rest(before, filled):
     hbm = pl.BlockSpec(memory_space=pltpu.HBM)
     return pl.pallas_call(
         place_rest_kernel,
@@ -395,10 +394,10 @@
         in_specs=[pl.BlockSpec(memory_space=pltpu.VMEM), hbm],
         out_specs=hbm,
         input_output_aliases={1: 0},
-        scratch_shapes=[pltpu.VMEM(partner.shape, jnp.float32), pltpu.SemaphoreType.DMA((SIDE * PAIR,))],
+        scratch_shapes=[pltpu.VMEM(before.shape, jnp.float32), pltpu.SemaphoreType.DMA((SIDE * PAIR,))],
         compiler_params=pltpu.CompilerParams(vmem_limit_bytes=12 * 2**20),
         name="place_rest",
-    )(partner, filled)
+    )(before, filled)
 
 
 def on_device(footprints, block_times, block_cells, live_counts, cell_lat, cell_lon):
@@ -437,13 +436,14 @@
     footprint_cov, local = make_local(partner_block, block)
     far, local = lax.optimization_barrier((far, local))
     (next_partner_tiles,) = make_tiles((next_partner_block,), -1, far, local, jnp.bfloat16)
-    (next_tiles,) = make_tiles((next_block,), -1, far, local, jnp.bfloat16)
     before_partner = lax.ppermute(next_partner_tiles, axes, steps(1, True))
-    before = lax.ppermute(next_tiles, axes, steps(1, False))
     (partner_tiles,) = make_tiles((partner_block,), 0, far, local, jnp.bfloat16)
     partner = lax.ppermute(partner_tiles, axes, steps(0, True))
-    (filled,) = make_tiles((block,), 1, far, local, jnp.float32, (before, before_partner))
-    cross_cov = place_rest(partner, filled)
+    far, partner_tiles = lax.optimization_barrier((far, partner_tiles))
+    (next_tiles,) = make_tiles((next_block,), -1, far, local, jnp.bfloat16)
+    before = lax.ppermute(next_tiles, axes, steps(1, False))
+    (filled,) = make_tiles((block,), 1, far, local, jnp.float32, (before_partner, partner))
+    cross_cov = place_rest(before, filled)
     return (cross_cov, footprint_cov)
 
 

time: 52 us -> 50 us (0.962)
  the two profiles are of different devices: /device:TPU:238 before, /device:TPU:224 now
where the time goes in v6:
time: 50 us; the launch traced here: 49.7 us
  starting transfers between devices  24.2 us (48%)
  Pallas kernels  17 us (34%)
  waiting for transfers between devices  6.95 us (14%)
  between operations  1.58 us (3%)
    pallas_call x4, Pallas kernels, make_tiles(): pl.pallas_call(functools.partial(tiles_kernel, count, base, bool(arrived)...  12.1 us
    all_to_all x1, waiting for transfers between devices, on_device(): lax.all_to_all(payload, axes, 0, 0, tiled=True, axis_index_groups=near_by)  6.05 us
    all_to_all x1, starting transfers between devices, on_device(): lax.all_to_all(payload, axes, 0, 0, tiled=True, axis_index_groups=near_by)  5.54 us
    ppermute x1, starting transfers between devices, on_device(): before = lax.ppermute(next_tiles, axes, steps(1, False))  5.28 us
    ppermute x1, starting transfers between devices, on_device(): partner_block = lax.ppermute(block, axes, steps(0, True))  5.18 us
    ppermute x1, starting transfers between devices, on_device(): partner = lax.ppermute(partner_tiles, axes, steps(0, True))  2.46 us
    pallas_call x1, Pallas kernels, make_block(): pl.pallas_call(block_kernel, out_shape=(jax.ShapeDtypeStruct((1, ROWS, WI...  2.19 us
    ppermute x1, starting transfers between devices, on_device(): next_partner_block = lax.ppermute(block, axes, steps(-1, True))  1.92 us
  transfers between devices with their start and end apart: 7, of which 2 were waited for; matrix products, arithmetic and copies ran while one was open for 0% of the time, Pallas kernels for 28%

profile of v6, /device:TPU:224, one launch (start us, length us, event | category | flops | bytes accessed | tf_op | source)
XLA Modules:
  0.0 49.7 jit_solution(3928306918692610021)
XLA Ops:
  1.3 2.2 %make_block.1 = (bf16[1,144,512]{2,1,0:T(8,128)(2,1)}, bf16[8,144,512]{2,1,0:T(8,128)(2,1)}) custom-call(bf16[1,4,128,128]{3,2,1,0:T(8,128)(2,1)} %prints.1, s32[1,4]{1,0:T(1,128)} %times.1, s32[1,4]{1,0:T(1,128)} %cells.1, s32[1]{0:T(128)S(6)} %copy.10.live, s32[512,128]{1,0:T(8,128)} %bitcast.2, s32[512,128]{1,0:T(8,128)} %bitcast.3), custom_call_target="tpu_custom_call" | custom-call | tf_op jit(solution)/shard_map/make_block/pallas_call | solution.py:99
  3.5 0.0 copy-start
  3.5 5.5 %all-to-all-start = ((bf16[8,144,512]{2,1,0:T(8,128)(2,1)}), bf16[8,144,512]{2,1,0:T(8,128)(2,1)S(1)}, u32[]{:S(2)}, u32[]{:S(2)}) async-start(bf16[8,144,512]{2,1,0:T(8,128)(2,1)} %get-tuple-element.10), calls=%async_computation | async-start | bytes 2359296 | tf_op jit(solution)/shard_map/all_to_all | solution.py:432
  9.0 0.0 copy-done
  9.0 5.2 %collective-permute-start.1 = (bf16[1,144,512]{2,1,0:T(8,128)(2,1)S(1)}, bf16[1,144,512]{2,1,0:T(8,128)(2,1)S(1)}, u32[]{:S(2)}, u32[]{:S(2)}) collective-permute-start(bf16[1,144,512]{2,1,0:T(8,128)(2,1)S(1)} %copy-done), channel_id=1, source_target_pairs={{0,3},{1,2},{2,1},{3,0},{4,7},{5,6},{6,5},{7,4},{8,11},{9,10},{10,... | collective-permute-start | bytes 442376 | tf_op jit(solution)/shard_map/ppermute | solution.py:433
  14.2 1.9 %collective-permute-start.3 = (bf16[1,144,512]{2,1,0:T(8,128)(2,1)S(1)}, bf16[1,144,512]{2,1,0:T(8,128)(2,1)S(1)}, u32[]{:S(2)}, u32[]{:S(2)}) collective-permute-start(bf16[1,144,512]{2,1,0:T(8,128)(2,1)S(1)} %copy-done), channel_id=1, source_target_pairs={{16,3},{17,2},{18,1},{19,0},{20,7},{21,6},{22,5},{23,4},{24,11},{2... | collective-permute-start | bytes 442376 | tf_op jit(solution)/shard_map/ppermute | solution.py:435
  16.2 1.9 %collective-permute-start = (bf16[1,144,512]{2,1,0:T(8,128)(2,1)S(1)}, bf16[1,144,512]{2,1,0:T(8,128)(2,1)S(1)}, u32[]{:S(2)}, u32[]{:S(2)}) collective-permute-start(bf16[1,144,512]{2,1,0:T(8,128)(2,1)S(1)} %copy-done), channel_id=1, source_target_pairs={{16,0},{17,1},{18,2},{19,3},{20,4},{21,5},{22,6},{23,7},{24,8},{25... | collective-permute-start | bytes 442376 | tf_op jit(solution)/shard_map/ppermute | solution.py:434
  18.1 0.9 %collective-permute-done.1.refs_0_ = bf16[1,144,512]{2,1,0:T(8,128)(2,1)S(1)} collective-permute-done((bf16[1,144,512]{2,1,0:T(8,128)(2,1)S(1)}, bf16[1,144,512]{2,1,0:T(8,128)(2,1)S(1)}, u32[]{:S(2)}, u32[]{:S(2)}) %collective-permute-start.1) | collective-permute-done | bytes 147488 | tf_op jit(solution)/shard_map/ppermute | solution.py:433
  19.0 1.8 %make_local.1 = (f32[1,4,128,128]{3,2,1,0:T(8,128)}, f32[2,128,128]{2,1,0:T(8,128)S(1)}) custom-call(bf16[1,144,512]{2,1,0:T(8,128)(2,1)S(1)} %collective-permute-done.1.refs_0_, bf16[1,144,512]{2,1,0:T(8,128)(2,1)S(1)} %copy-done), custom_call_target="tpu_custom_call" | custom-call | flops 4000000000 | bytes 1000000 | tf_op jit(solution)/shard_map/make_local/pallas_call | solution.py:184
  20.7 6.0 %all-to-all-done.refs_1_ = bf16[8,144,512]{2,1,0:T(8,128)(2,1)S(1)} async-done(((bf16[8,144,512]{2,1,0:T(8,128)(2,1)}), bf16[8,144,512]{2,1,0:T(8,128)(2,1)S(1)}, u32[]{:S(2)}, u32[]{:S(2)}) %all-to-all-start) | async-done | bytes 1179680 | tf_op jit(solution)/shard_map/all_to_all | solution.py:432
  26.8 2.8 %make_tiles.4 = bf16[128,1024]{1,0:T(8,128)(2,1)S(1)} custom-call(bf16[1,144,512]{2,1,0:T(8,128)(2,1)S(1)} %collective-permute-done.1.refs_0_, bf16[8,144,512]{2,1,0:T(8,128)(2,1)S(1)} %all-to-all-done.refs_1_, f32[2,128,128]{2,1,0:T(8,128)S(1)} %get-tuple-element.13.refs_2_), custom_call_target="tpu_custom_call" | custom-call | flops 1000000000 | bytes 2000000 | tf_op jit(solution)/shard_map/make_tiles/pallas_call | solution.py:341
  29.6 2.5 %collective-permute-start.5 = (bf16[128,1024]{1,0:T(8,128)(2,1)S(1)}, bf16[128,1024]{1,0:T(8,128)(2,1)S(1)}, u32[]{:S(2)}, u32[]{:S(2)}) collective-permute-start(bf16[128,1024]{1,0:T(8,128)(2,1)S(1)} %make_tiles.4), channel_id=1, source_target_pairs={{0,3},{1,2},{2,1},{3,0},{4,7},{5,6},{6,5},{7,4},{8,11},{9,10},{10,... | collective-permute-start | bytes 786440 | tf_op jit(solution)/shard_map/ppermute | solution.py:441
  32.1 0.0 collective-permute-done.3.refs_0_
  32.1 3.2 %make_tiles.6 = bf16[128,1024]{1,0:T(8,128)(2,1)S(1)} custom-call(bf16[1,144,512]{2,1,0:T(8,128)(2,1)S(1)} %collective-permute-done.3.refs_0_, bf16[8,144,512]{2,1,0:T(8,128)(2,1)S(1)} %all-to-all-done.refs_1_, f32[2,128,128]{2,1,0:T(8,128)S(1)} %get-tuple-element.13.refs_2_), custom_call_target="tpu_custom_call" | custom-call | flops 1000000000 | bytes 2000000 | tf_op jit(solution)/shard_map/make_tiles/pallas_call | solution.py:341
  35.2 1.9 %collective-permute-start.4 = (bf16[128,1024]{1,0:T(8,128)(2,1)S(1)}, bf16[128,1024]{1,0:T(8,128)(2,1)S(1)}, u32[]{:S(2)}, u32[]{:S(2)}) collective-permute-start(bf16[128,1024]{1,0:T(8,128)(2,1)S(1)} %make_tiles.6), channel_id=1, source_target_pairs={{0,19},{1,18},{2,17},{3,16},{4,23},{5,22},{6,21},{7,20},{8,27},{9,... | collective-permute-start | bytes 786440 | tf_op jit(solution)/shard_map/ppermute | solution.py:439
  37.2 0.0 collective-permute-done.refs_0_
  37.2 2.4 %make_tiles.5 = bf16[128,1024]{1,0:T(8,128)(2,1)S(1)} custom-call(bf16[1,144,512]{2,1,0:T(8,128)(2,1)S(1)} %collective-permute-done.refs_0_, bf16[8,144,512]{2,1,0:T(8,128)(2,1)S(1)} %all-to-all-done.refs_1_, f32[2,128,128]{2,1,0:T(8,128)S(1)} %get-tuple-element.13.refs_2_), custom_call_target="tpu_custom_call" | custom-call | flops 1000000000 | bytes 2000000 | tf_op jit(solution)/shard_map/make_tiles/pallas_call | solution.py:341
  39.6 5.3 %collective-permute-start.2 = (bf16[128,1024]{1,0:T(8,128)(2,1)S(1)}, bf16[128,1024]{1,0:T(8,128)(2,1)S(1)}, u32[]{:S(2)}, u32[]{:S(2)}) collective-permute-start(bf16[128,1024]{1,0:T(8,128)(2,1)S(1)} %make_tiles.5), channel_id=1, source_target_pairs={{0,16},{1,17},{2,18},{3,19},{4,20},{5,21},{6,22},{7,23},{8,24},{9,... | collective-permute-start | bytes 786440 | tf_op jit(solution)/shard_map/ppermute | solution.py:444
  44.9 0.0 collective-permute-done.4.refs_3_
  44.9 0.0 collective-permute-done.5.refs_4_
  44.9 3.7 %make_tiles.7.filled = f32[128,4096]{1,0:T(8,128)} custom-call(bf16[1,144,512]{2,1,0:T(8,128)(2,1)S(1)} %copy-done, bf16[8,144,512]{2,1,0:T(8,128)(2,1)S(1)} %all-to-all-done.refs_1_, f32[2,128,128]{2,1,0:T(8,128)S(1)} %get-tuple-element.13.refs_2_, bf16[128,1024]{1,0:T(8,128)(2,1)S(1)} %collective-permute-done.4.refs_3_, ...), custom_call_target="tpu_custom_call" | custom-call | flops 1000000000 | bytes 2000000 | tf_op jit(solution)/shard_map/make_tiles/pallas_call | solution.py:341
  48.7 0.0 collective-permute-done.2.before
  48.7 0.9 %place_rest.1 = f32[128,4096]{1,0:T(8,128)} custom-call(bf16[128,1024]{1,0:T(8,128)(2,1)S(1)} %collective-permute-done.2.before, f32[128,4096]{1,0:T(8,128)} %make_tiles.7.filled), custom_call_target="tpu_custom_call", output_to_operand_aliasing={{}: (1, {})} | custom-call | tf_op jit(solution)/shard_map/place_rest/pallas_call | solution.py:391
Async XLA Ops:
  3.5 5.6 %copy-start = (bf16[1,144,512]{2,1,0:T(8,128)(2,1)S(1)}, bf16[1,144,512]{2,1,0:T(8,128)(2,1)}, u32[]{:S(2)}) copy-start(bf16[1,144,512]{2,1,0:T(8,128)(2,1)} %get-tuple-element.9.refs_1_.refs_0_) | copy-start | bytes 442372
  3.5 23.3 %all-to-all-start = ((bf16[8,144,512]{2,1,0:T(8,128)(2,1)}), bf16[8,144,512]{2,1,0:T(8,128)(2,1)S(1)}, u32[]{:S(2)}, u32[]{:S(2)}) async-start(bf16[8,144,512]{2,1,0:T(8,128)(2,1)} %get-tuple-element.10), calls=%async_computation | async-start | bytes 2359296 | tf_op jit(solution)/shard_map/all_to_all | solution.py:432
  9.0 9.9 %collective-permute-start.1 = (bf16[1,144,512]{2,1,0:T(8,128)(2,1)S(1)}, bf16[1,144,512]{2,1,0:T(8,128)(2,1)S(1)}, u32[]{:S(2)}, u32[]{:S(2)}) collective-permute-start(bf16[1,144,512]{2,1,0:T(8,128)(2,1)S(1)} %copy-done), channel_id=1, source_target_pairs={{0,3},{1,2},{2,1},{3,0},{4,7},{5,6},{6,5},{7,4},{8,11},{9,10},{10,... | collective-permute-start | bytes 442376 | tf_op jit(solution)/shard_map/ppermute | solution.py:433
  14.2 17.8 %collective-permute-start.3 = (bf16[1,144,512]{2,1,0:T(8,128)(2,1)S(1)}, bf16[1,144,512]{2,1,0:T(8,128)(2,1)S(1)}, u32[]{:S(2)}, u32[]{:S(2)}) collective-permute-start(bf16[1,144,512]{2,1,0:T(8,128)(2,1)S(1)} %copy-done), channel_id=1, source_target_pairs={{16,3},{17,2},{18,1},{19,0},{20,7},{21,6},{22,5},{23,4},{24,11},{2... | collective-permute-start | bytes 442376 | tf_op jit(solution)/shard_map/ppermute | solution.py:435
  16.2 21.0 %collective-permute-start = (bf16[1,144,512]{2,1,0:T(8,128)(2,1)S(1)}, bf16[1,144,512]{2,1,0:T(8,128)(2,1)S(1)}, u32[]{:S(2)}, u32[]{:S(2)}) collective-permute-start(bf16[1,144,512]{2,1,0:T(8,128)(2,1)S(1)} %copy-done), channel_id=1, source_target_pairs={{16,0},{17,1},{18,2},{19,3},{20,4},{21,5},{22,6},{23,7},{24,8},{25... | collective-permute-start | bytes 442376 | tf_op jit(solution)/shard_map/ppermute | solution.py:434
  29.6 15.3 %collective-permute-start.5 = (bf16[128,1024]{1,0:T(8,128)(2,1)S(1)}, bf16[128,1024]{1,0:T(8,128)(2,1)S(1)}, u32[]{:S(2)}, u32[]{:S(2)}) collective-permute-start(bf16[128,1024]{1,0:T(8,128)(2,1)S(1)} %make_tiles.4), channel_id=1, source_target_pairs={{0,3},{1,2},{2,1},{3,0},{4,7},{5,6},{6,5},{7,4},{8,11},{9,10},{10,... | collective-permute-start | bytes 786440 | tf_op jit(solution)/shard_map/ppermute | solution.py:441
  35.2 9.7 %collective-permute-start.4 = (bf16[128,1024]{1,0:T(8,128)(2,1)S(1)}, bf16[128,1024]{1,0:T(8,128)(2,1)S(1)}, u32[]{:S(2)}, u32[]{:S(2)}) collective-permute-start(bf16[128,1024]{1,0:T(8,128)(2,1)S(1)} %make_tiles.6), channel_id=1, source_target_pairs={{0,19},{1,18},{2,17},{3,16},{4,23},{5,22},{6,21},{7,20},{8,27},{9,... | collective-permute-start | bytes 786440 | tf_op jit(solution)/shard_map/ppermute | solution.py:439
  39.6 9.0 %collective-permute-start.2 = (bf16[128,1024]{1,0:T(8,128)(2,1)S(1)}, bf16[128,1024]{1,0:T(8,128)(2,1)S(1)}, u32[]{:S(2)}, u32[]{:S(2)}) collective-permute-start(bf16[128,1024]{1,0:T(8,128)(2,1)S(1)} %make_tiles.5), channel_id=1, source_target_pairs={{0,16},{1,17},{2,18},{3,19},{4,20},{5,21},{6,22},{7,23},{8,24},{9,... | collective-permute-start | bytes 786440 | tf_op jit(solution)/shard_map/ppermute | solution.py:444
